TPU v7x, 256 devices: a whole 4x4x8 slice. The times are simulated.
256 devices in a mesh: row: 8 (over z), col: 4 (over x_hi, core), dep: 8 (over x_lo, y).
Axes of the slice: x: 4 (x_hi: 2, x_lo: 2; x = x_hi * 2 + x_lo), y: 4, z: 8, core: 2. Of those that a mesh axis runs over, the one named last changes fastest.
Arguments:
- tokens: bfloat16 [1024, 12288], P(('row', 'col'), 'dep'), may hold values from -16 to 16
- w_up: bfloat16 [12288, 49152], P('dep', ('row', 'col')), may hold values from -0.14433757 to 0.14433757
- bias_up: float32 [49152], P(('row', 'col')), may hold values from -3 to 3
- w_down: bfloat16 [49152, 12288], P(('row', 'col'), 'dep'), may hold values from -0.02734375 to 0.02734375
- bias_down: float32 [12288], P('dep'), may hold values from -3 to 3
- amax_history: float32 [1024], replicated, may hold values from 0.5 to 3
Outputs:
- layer_output: bfloat16 [1024, 12288], P(('row', 'col'), 'dep')
- history_next: float32 [1024], replicated
All inputs are finite; a program needn't handle non-finite values.
Results may differ from a plain program's by a relative error of at most 0.0039.
Values may be sent and summed in bfloat16 or wider, within the bound.
No kernel may reach another device: no remote copies, remote signals or barrier semaphores. Data moves between devices by JAX's collectives and lax.ppermute only.
A program may use at most 64 MiB of HBM per device.

v0:
```python
import jax
import jax.numpy as jnp
from jax import lax
from jax.sharding import PartitionSpec as P

format_limit = 448.0


def activate(pre_sums, bias_up):
    return jax.nn.gelu(pre_sums + bias_up[None, :], approximate=True)


def quantize(activated, scale_factor):
    return jnp.clip(activated * scale_factor, -format_limit, format_limit).astype(jnp.bfloat16)


def local(tokens, w_up, bias_up, w_down, bias_down, amax_history):
    scale_factor = format_limit / jnp.max(amax_history)
    partial_value = jnp.dot(
        lax.all_gather(tokens, ("row", "col"), axis=0, tiled=True),
        w_up,
        preferred_element_type=jnp.float32,
    )
    summed = lax.psum(partial_value, "dep")
    activated = activate(summed, bias_up)
    new_peak = lax.pmax(jnp.max(jnp.abs(activated)), ("row", "col"))
    full_rows = quantize(activated, scale_factor)
    mixed_sum = lax.psum_scatter(
        jnp.dot(full_rows, w_down, preferred_element_type=jnp.float32),
        ("row", "col"),
        scatter_dimension=0,
        tiled=True,
    )
    layer_output = (mixed_sum / scale_factor + bias_down[None, :]).astype(jnp.bfloat16)
    history_next = jnp.concatenate([new_peak.reshape(1), amax_history[:-1]])
    return (layer_output, history_next)


def solution(mesh):
    in_specs = (
        P(("row", "col"), "dep"),
        P("dep", ("row", "col")),
        P(("row", "col")),
        P(("row", "col"), "dep"),
        P("dep"),
        P(),
    )
    out_specs = (P(("row", "col"), "dep"), P())
    return jax.shard_map(local, mesh=mesh, in_specs=in_specs, out_specs=out_specs, check_vma=False)
```

profile of v0, /device:TPU:32, one launch (start us, length us, event | category | flops | bytes accessed | tf_op | source)
XLA Modules:
  0.0 407.8 jit_solution(12023327524641202119)
XLA Ops:
  7.2 0.0 all-gather.2.cloned.1.call-start
  7.2 0.7 all-gather.2.cloned.1.call-update
  7.9 0.0 all-reduce.2.cloned.1.call-start
  7.9 88.3 %all-gather.2.cloned.1.call-done = bf16[1024,1536]{1,0:T(8,128)(2,1)} async-done(((bf16[32,1536]{1,0:T(8,128)(2,1)}), bf16[1024,1536]{1,0:T(8,128)(2,1)}) %all-gather.2.cloned.1.call-update) | async-done | bytes 3145744 | tf_op jit(solution)/shard_map/all_gather | solution.py:20
  96.2 9.7 %fusion.18 = f32[1024,1536]{1,0:T(8,128)} fusion(bf16[1024,1536]{1,0:T(8,128)(2,1)} %all-gather.2.cloned.1.call-done, bf16[1536,1536]{1,0:T(8,128)(2,1)} %param.7), kind=kOutput, calls=%fused_computation.22 | convolution fusion | flops 4831838208 | bytes 14155776 | tf_op jit(solution)/shard_map/dot_general | solution.py:19
  105.9 0.0 copy-start
  105.9 0.0 copy-start.1
  105.9 0.0 all-reduce.2.cloned.1.call-update
  105.9 0.0 reduce-scatter.2.cloned.1.call-start
  106.0 0.6 copy-done
  106.6 0.6 reduce_max.18
  107.9 145.4 %all-reduce.2.cloned.1.call-done = f32[1024,1536]{1,0:T(8,128)} async-done(((f32[1024,1536]{1,0:T(8,128)}), f32[1024,1536]{1,0:T(8,128)}) %all-reduce.2.cloned.1.call-update) | async-done | bytes 6291472 | tf_op jit(solution)/shard_map/psum | solution.py:24
  253.3 0.0 copy-done.1
  253.3 11.1 %fusion.7 = f32[1024,1536]{1,0:T(8,128)} fusion(bf16[1536,1536]{1,0:T(8,128)(2,1)} %param.9, f32[]{:T(128)S(6)} %div.9, f32[1024,1536]{1,0:T(8,128)} %all-reduce.2.cloned.1.call-done, f32[1536]{0:T(1024)S(1)} %copy-done.1), kind=kOutput, calls=%fused_computation.10 | convolution fusion | flops 4850712576 | bytes 17307652 | tf_op jit(solution)/shard_map/dot_general | solution.py:29
  264.4 0.0 copy-start.2
  264.5 0.0 reduce-scatter.2.cloned.1.call-update
  264.5 4.7 %abs_reduce_fusion = f32[]{:T(128)} fusion(f32[1024,1536]{1,0:T(8,128)} %all-reduce.2.cloned.1.call-done, f32[1536]{0:T(1024)S(1)} %copy-done.1), kind=kLoop, calls=%fused_computation.8 | loop fusion | flops 17301504 | bytes 6297604 | tf_op jit(solution)/shard_map/reduce_max | solution.py:26
  269.1 62.5 %pmax.7 = f32[1]{0:T(128)} all-reduce(f32[1]{0:T(128)} %bitcast), channel_id=1, replica_groups=mesh['row'=8,'col'=4,'dep'=8] {'row','col'}, use_global_device_ids=true, to_apply=%region_4.5 | all-reduce | flops 1 | bytes 8 | tf_op jit(solution)/shard_map/pmax | solution.py:26
  331.6 1.3 pad_maximum_fusion
  332.9 66.8 %reduce-scatter.2.cloned.1.call-done = f32[32,1536]{1,0:T(8,128)} async-done(((f32[1024,1536]{1,0:T(8,128)}), f32[32,1536]{1,0:T(8,128)}) %reduce-scatter.2.cloned.1.call-update) | async-done | bytes 196624 | tf_op jit(solution)/shard_map/reduce_scatter | solution.py:28
  399.7 0.0 copy-done.2
  399.7 1.6 add_convert_fusion
Async XLA Ops:
  7.2 89.1 %all-gather.2.cloned.1.call-start = ((), (), s32[]{:S(2)}) async-start(), calls=%async_computation.1 | async-start | bytes 3244032 | tf_op jit(solution)/shard_map/all_gather | solution.py:20
  7.9 245.4 %all-reduce.2.cloned.1.call-start = ((), (), s32[]{:S(2)}) async-start(), calls=%async_computation.2 | async-start | bytes 12582912 | tf_op jit(solution)/shard_map/psum | solution.py:24
  105.9 0.7 copy-start
  105.9 147.4 %copy-start.1 = (f32[1536]{0:T(1024)S(1)}, f32[1536]{0:T(1024)}, u32[]{:S(2)}) copy-start(f32[1536]{0:T(1024)} %param.8) | copy-start | bytes 18436
  105.9 293.8 %reduce-scatter.2.cloned.1.call-start = ((), (), s32[]{:S(2)}) async-start(), calls=%async_computation.3 | async-start | bytes 6488064 | tf_op jit(solution)/shard_map/reduce_scatter | solution.py:28
  264.4 135.3 %copy-start.2 = (f32[1536]{0:T(1024)S(1)}, f32[1536]{0:T(1024)}, u32[]{:S(2)}) copy-start(f32[1536]{0:T(1024)} %param.10) | copy-start | bytes 18436
Sparse Core Ops, SparseCore 0:
  10.8 85.4 all-gather.1
  106.0 147.2 all-reduce.1
  264.6 135.0 reduce-scatter.1
where the time goes:
time: 409 us; the launch traced here: 408 us
  waiting for transfers between devices  301 us (74%)
  blocking collectives  62.5 us (15%)
  matrix products  20.8 us (5%)
  between operations  14.4 us (4%)
  other arithmetic  8.16 us (2%)
    psum x1, waiting for transfers between devices, local(): summed = lax.psum(partial_value, 'dep')  145 us
    all_gather x1, waiting for transfers between devices, local(): lax.all_gather(tokens, ('row', 'col'), axis=0, tiled=True)  88.3 us
    reduce_scatter x1, waiting for transfers between devices, local(): lax.psum_scatter(jnp.dot(full_rows, w_down, preferred_element_type=jnp.fl...  66.8 us
    pmax x1, blocking collectives, local(): new_peak = lax.pmax(jnp.max(jnp.abs(activated)), ('row', 'col'))  62.5 us
    dot_general x1, matrix products, local(): jnp.dot(full_rows, w_down, preferred_element_type=jnp.float32)  11.1 us
    dot_general x1, matrix products, local(): jnp.dot(lax.all_gather(tokens, ('row', 'col'), axis=0, tiled=True), w_up,...  9.66 us
  transfers between devices with their start and end apart: 3, of which 3 were waited for; matrix products, arithmetic and copies ran while one was open for 2% of the time, Pallas kernels for 0%

commit v1 on v0

v1 whole, which is shorter than its diff:
```python
import jax
import jax.numpy as jnp
from jax import lax
from jax.sharding import PartitionSpec as P

format_limit = 448.0
f32, f16, bf16 = jnp.float32, jnp.float16, jnp.bfloat16

up_gain = 16.0
down_gain = 64.0

core_swap = [(0, 1), (1, 0), (2, 3), (3, 2)]
x_hi_swap = [(0, 2), (2, 0), (1, 3), (3, 1)]
x_lo_swap = [(i, (i + 4) % 8) for i in range(8)]
y_up = [(4 * l + i, 4 * l + (i + 1) % 4) for l in range(2) for i in range(4)]
y_down = [(4 * l + (i + 1) % 4, 4 * l + i) for l in range(2) for i in range(4)]


def dot(a, b):
    return jnp.dot(a, b, preferred_element_type=f32)


def gather_tokens(tokens):
    pair = jnp.concatenate([tokens, lax.ppermute(tokens, "col", x_hi_swap)])
    mine = lax.all_gather(pair, "row", axis=0, tiled=True)
    return mine, lax.ppermute(mine, "col", core_swap)


def gather_hidden(q):
    n = q.shape[0]
    p = lax.ppermute(q, "dep", x_lo_swap)
    a_q = lax.ppermute(q, "dep", y_up)
    b_q = lax.ppermute(q, "dep", y_down)
    a_p = lax.ppermute(p, "dep", y_up)
    b_p = lax.ppermute(p, "dep", y_down)
    h = n // 2
    c = lax.ppermute(jnp.concatenate([a_q[:h], a_p[:h]]), "dep", y_up)
    d = lax.ppermute(jnp.concatenate([b_q[h:], b_p[h:]]), "dep", y_down)
    rel = jnp.stack(
        [
            jnp.stack([q, a_q, jnp.concatenate([c[:h], d[:h]]), b_q]),
            jnp.stack([p, a_p, jnp.concatenate([c[h:], d[h:]]), b_p]),
        ]
    )
    me = lax.axis_index("dep")
    lo, y = me // 4, me % 4
    parts = []
    for l in range(2):
        for k in range(4):
            parts.append(rel[(l + lo) % 2, (y - k) % 4])
    return jnp.concatenate(parts)


def local(tokens, w_up, bias_up, w_down, bias_down, amax_history):
    scale_factor = format_limit / jnp.max(amax_history)
    mine, other = gather_tokens(tokens)
    up = jnp.concatenate([dot(mine, w_up), dot(other, w_up)])
    sent = (up * up_gain).astype(f16)
    got = lax.all_to_all(sent.reshape(8, 128, 1536), "dep", 0, 0, tiled=True)
    summed = jnp.sum(got.astype(f32), axis=0) * (1.0 / up_gain)
    activated = jax.nn.gelu(summed + bias_up[None, :], approximate=True)
    peaks = lax.all_gather(jnp.max(jnp.abs(activated)).reshape(1), ("row", "col", "dep"), axis=0, tiled=True)
    new_peak = jnp.max(peaks)
    quantized = jnp.clip(activated * scale_factor, -format_limit, format_limit).astype(bf16)
    full_rows = gather_hidden(quantized)
    factor = down_gain / scale_factor
    away = (dot(full_rows[512:], w_down) * factor).astype(f16)
    came = lax.ppermute(away, "col", core_swap)
    near = dot(full_rows[:512], w_down) * factor + came.astype(f32)
    near = near.reshape(8, 2, 32, 1536)
    came = lax.ppermute(near[:, 1].astype(f16), "col", x_hi_swap)
    near = near[:, 0] + came.astype(f32)
    got = lax.all_to_all(near.astype(f16), "row", 0, 0, tiled=True)
    mixed = jnp.sum(got.astype(f32), axis=0) * (1.0 / down_gain)
    layer_output = (mixed + bias_down[None, :]).astype(bf16)
    history_next = jnp.concatenate([new_peak.reshape(1), amax_history[:-1]])
    return (layer_output, history_next)


def solution(mesh):
    in_specs = (
        P(("row", "col"), "dep"),
        P("dep", ("row", "col")),
        P(("row", "col")),
        P(("row", "col"), "dep"),
        P("dep"),
        P(),
    )
    out_specs = (P(("row", "col"), "dep"), P())
    return jax.shard_map(local, mesh=mesh, in_specs=in_specs, out_specs=out_specs, check_vma=False)
```

time: 409 us -> 285 us (0.70)
  waiting for transfers between devices: 301 us -> 134 us
  starting transfers between devices: 0.12 us -> 25.4 us
  blocking collectives: 62.5 us -> 77 us
  matrix products: 20.8 us -> 14.6 us
  other arithmetic: 8.16 us -> 13.1 us
    psum x1 -> x0, waiting for transfers between devices: 145 us -> none  [local(): summed = lax.psum(partial_value, 'dep')]
    unnamed x0 -> x1, blocking collectives: none -> 77 us
    reduce_scatter x1 -> x0, waiting for transfers between devices: 66.8 us -> none  [local(): lax.psum_scatter(jnp.dot(full_rows, w_down, preferred_element_type=jnp.fl...]
    pmax x1 -> x0, blocking collectives: 62.5 us -> none  [local(): new_peak = lax.pmax(jnp.max(jnp.abs(activated)), ('row', 'col'))]
    ppermute x0 -> x11, waiting for transfers between devices: none -> 55.3 us  [the longest x1 18.4 us: local(): came = lax.ppermute(near[:, 1].astype(f16), 'col', x_hi_swap)]
    all_gather x1, waiting for transfers between devices: 88.3 us -> 42.4 us  [gather_tokens(): mine = lax.all_gather(pair, 'row', axis=0, tiled=True)]
    all_to_all x0 -> x2, waiting for transfers between devices: none -> 36.6 us  [the longest x1 36.6 us: local(): got = lax.all_to_all(sent.reshape(8, 128, 1536), 'dep', 0, 0, tiled=True)]
    ppermute x0 -> x11, starting transfers between devices: none -> 14.9 us  [the longest x1 3.11 us: gather_tokens(): pair = jnp.concatenate([tokens, lax.ppermute(tokens, 'col', x_hi_swap)])]
  transfers between devices with their start and end apart: 3 -> 14, of which waited for: 3 -> 10; matrix products, arithmetic and copies ran while one was open for 2% -> 4% of each run, Pallas kernels for 0% -> 0%
where the time goes in v1:
time: 285 us; the launch traced here: 283 us
  waiting for transfers between devices  134 us (47%)
  blocking collectives  77 us (27%)
  starting transfers between devices  25.4 us (9%)
  between operations  15.6 us (5%)
  matrix products  14.6 us (5%)
  other arithmetic  13.1 us (5%)
    unnamed x1, blocking collectives  77 us
    all_gather x1, waiting for transfers between devices, gather_tokens(): mine = lax.all_gather(pair, 'row', axis=0, tiled=True)  42.4 us
    all_to_all x1, waiting for transfers between devices, local(): got = lax.all_to_all(sent.reshape(8, 128, 1536), 'dep', 0, 0, tiled=True)  36.6 us
    ppermute x1, waiting for transfers between devices, local(): came = lax.ppermute(near[:, 1].astype(f16), 'col', x_hi_swap)  18.4 us
    dot_general x4, matrix products, dot(): return jnp.dot(a, b, preferred_element_type=f32)  14.6 us
    ppermute x1, waiting for transfers between devices, gather_hidden(): c = lax.ppermute(jnp.concatenate([a_q[:h], a_p[:h]]), 'dep', y_up)  9.46 us
    ppermute x1, waiting for transfers between devices, gather_hidden(): p = lax.ppermute(q, 'dep', x_lo_swap)  7.86 us
    ppermute x1, waiting for transfers between devices, gather_hidden(): b_p = lax.ppermute(p, 'dep', y_down)  6.24 us
  transfers between devices with their start and end apart: 14, of which 10 were waited for; matrix products, arithmetic and copies ran while one was open for 4% of the time, Pallas kernels for 0%

profile of v1, /device:TPU:32, one launch (start us, length us, event | category | flops | bytes accessed | tf_op | source)
XLA Modules:
  0.0 282.9 jit_solution(6294411519780334666)
XLA Ops:
  7.2 3.1 %collective-permute-start = (bf16[32,1536]{1,0:T(8,128)(2,1)}, bf16[32,1536]{1,0:T(8,128)(2,1)S(1)}, u32[]{:S(2)}, u32[]{:S(2)}) collective-permute-start(bf16[32,1536]{1,0:T(8,128)(2,1)} %param.6), channel_id=1, source_target_pairs={{0,16},{16,0},{8,24},{24,8},{1,17},{17,1},{9,25},{25,9},{2,18},{18... | collective-permute-start | bytes 294920 | tf_op jit(solution)/shard_map/ppermute | solution.py:24
  10.3 3.3 %collective-permute-done = bf16[32,1536]{1,0:T(8,128)(2,1)S(1)} collective-permute-done((bf16[32,1536]{1,0:T(8,128)(2,1)}, bf16[32,1536]{1,0:T(8,128)(2,1)S(1)}, u32[]{:S(2)}, u32[]{:S(2)}) %collective-permute-start) | collective-permute-done | bytes 98336 | tf_op jit(solution)/shard_map/ppermute | solution.py:24
  13.6 1.6 pad_maximum_fusion.2
  15.2 42.4 %all-gather.2.cloned.1.call-done = bf16[512,1536]{1,0:T(8,128)(2,1)} async-done(((bf16[64,1536]{1,0:T(8,128)(2,1)}), bf16[512,1536]{1,0:T(8,128)(2,1)}) %all-gather.2.cloned.1.call-update) | async-done | bytes 1572880 | tf_op jit(solution)/shard_map/all_gather | solution.py:25
  57.7 4.9 %fusion.58 = f32[512,1536]{1,0:T(8,128)S(1)} fusion(bf16[512,1536]{1,0:T(8,128)(2,1)} %all-gather.2.cloned.1.call-done, bf16[1536,1536]{1,0:T(8,128)(2,1)} %param.7), kind=kOutput, calls=%fused_computation.94 | convolution fusion | flops 2415919104 | bytes 9437184 | tf_op jit(solution)/shard_map/dot_general | solution.py:20
  62.6 4.5 %fusion.59 = f32[512,1536]{1,0:T(8,128)S(1)} fusion(bf16[512,1536]{1,0:T(8,128)(2,1)S(1)} %collective-permute-done.1, bf16[1536,1536]{1,0:T(8,128)(2,1)} %param.7), kind=kOutput, calls=%fused_computation.95 | convolution fusion | flops 2415919104 | bytes 9437184 | tf_op jit(solution)/shard_map/dot_general | solution.py:20
  67.1 2.4 fusion
  69.5 5.3 %all-to-all-start = ((f16[8,128,1536]{2,1,0:T(8,128)(2,1)}), f16[8,128,1536]{2,1,0:T(8,128)(2,1)S(1)}, u32[]{:S(2)}, u32[]{:S(2)}) async-start(f16[8,128,1536]{2,1,0:T(8,128)(2,1)} %bitcast.54), calls=%async_computation | async-start | bytes 6291456 | tf_op jit(solution)/shard_map/all_to_all | solution.py:59
  76.2 36.6 %all-to-all-done = f16[8,128,1536]{2,1,0:T(8,128)(2,1)S(1)} async-done(((f16[8,128,1536]{2,1,0:T(8,128)(2,1)}), f16[8,128,1536]{2,1,0:T(8,128)(2,1)S(1)}, u32[]{:S(2)}, u32[]{:S(2)}) %all-to-all-start) | async-done | bytes 3145760 | tf_op jit(solution)/shard_map/all_to_all | solution.py:59
  115.1 1.5 collective-permute-start.3
  118.0 7.9 %collective-permute-done.3 = bf16[128,1536]{1,0:T(8,128)(2,1)S(1)} collective-permute-done((bf16[128,1536]{1,0:T(8,128)(2,1)S(1)}, bf16[128,1536]{1,0:T(8,128)(2,1)S(1)}, u32[]{:S(2)}, u32[]{:S(2)}) %collective-permute-start.3) | collective-permute-done | bytes 393248 | tf_op jit(solution)/shard_map/ppermute | solution.py:31
  125.9 1.6 collective-permute-start.7
  129.5 6.2 %collective-permute-done.7 = bf16[128,1536]{1,0:T(8,128)(2,1)S(1)} collective-permute-done((bf16[128,1536]{1,0:T(8,128)(2,1)S(1)}, bf16[128,1536]{1,0:T(8,128)(2,1)S(1)}, u32[]{:S(2)}, u32[]{:S(2)}) %collective-permute-start.7) | collective-permute-done | bytes 393248 | tf_op jit(solution)/shard_map/ppermute | solution.py:35
  135.8 2.7 collective-permute-start.8
  138.6 1.5 fusion.29
  141.5 5.6 %collective-permute-done.4 = bf16[128,1536]{1,0:T(8,128)(2,1)S(1)} collective-permute-done((bf16[128,1536]{1,0:T(8,128)(2,1)S(1)}, bf16[128,1536]{1,0:T(8,128)(2,1)S(1)}, u32[]{:S(2)}, u32[]{:S(2)}) %collective-permute-start.4) | collective-permute-done | bytes 393248 | tf_op jit(solution)/shard_map/ppermute | solution.py:34
  147.4 9.5 %collective-permute-done.5 = bf16[128,1536]{1,0:T(8,128)(2,1)S(1)} collective-permute-done((bf16[128,1536]{1,0:T(8,128)(2,1)S(1)}, bf16[128,1536]{1,0:T(8,128)(2,1)S(1)}, u32[]{:S(2)}, u32[]{:S(2)}) %collective-permute-start.5) | collective-permute-done | bytes 393248 | tf_op jit(solution)/shard_map/ppermute | solution.py:37
  159.3 2.6 fusion.1
  162.3 3.1 %collective-permute-done.9 = f16[512,1536]{1,0:T(8,128)(2,1)S(1)} collective-permute-done((f16[512,1536]{1,0:T(8,128)(2,1)S(1)}, f16[512,1536]{1,0:T(8,128)(2,1)S(1)}, u32[]{:S(2)}, u32[]{:S(2)}) %collective-permute-start.9) | collective-permute-done | bytes 1572896 | tf_op jit(solution)/shard_map/ppermute | solution.py:68
  165.4 2.6 convert_add_fusion
  168.1 2.8 collective-permute-start.10
  170.9 18.4 %collective-permute-done.10 = f16[8,32,1536]{2,1,0:T(8,128)(2,1)S(1)} collective-permute-done((f16[8,32,1536]{2,1,0:T(8,128)(2,1)S(1)}, f16[8,32,1536]{2,1,0:T(8,128)(2,1)S(1)}, u32[]{:S(2)}, u32[]{:S(2)}) %collective-permute-start.10) | collective-permute-done | bytes 786464 | tf_op jit(solution)/shard_map/ppermute | solution.py:71
  190.5 5.1 %all-to-all-start.1 = ((f16[8,32,1536]{2,1,0:T(8,128)(2,1)}), f16[8,32,1536]{2,1,0:T(8,128)(2,1)S(1)}, u32[]{:S(2)}, u32[]{:S(2)}) async-start(f16[8,32,1536]{2,1,0:T(8,128)(2,1)} %fusion.3), calls=%async_computation.1 | async-start | bytes 1572864 | tf_op jit(solution)/shard_map/all_to_all | solution.py:73
  196.4 77.0 %all-reduce = f32[256]{0:T(256)S(1)} all-reduce(f32[256]{0:T(256)S(1)} %dynamic-update-slice), channel_id=1, replica_groups=mesh['row'=8,'col'=4,'dep'=8] {'row','col','dep'}, use_global_device_ids=true, to_apply=%add | all-reduce | flops 256 | bytes 2048
  (50 shorter events, 15.1 us)
Async XLA Ops:
  7.2 50.5 %all-gather.2.cloned.1.call-start = ((), (), s32[]{:S(2)}) async-start(), calls=%async_computation.2 | async-start | bytes 1769472 | tf_op jit(solution)/shard_map/all_gather | solution.py:25
  7.2 6.4 %collective-permute-start = (bf16[32,1536]{1,0:T(8,128)(2,1)}, bf16[32,1536]{1,0:T(8,128)(2,1)S(1)}, u32[]{:S(2)}, u32[]{:S(2)}) collective-permute-start(bf16[32,1536]{1,0:T(8,128)(2,1)} %param.6), channel_id=1, source_target_pairs={{0,16},{16,0},{8,24},{24,8},{1,17},{17,1},{9,25},{25,9},{2,18},{18... | collective-permute-start | bytes 294920 | tf_op jit(solution)/shard_map/ppermute | solution.py:24
  57.7 4.9 %collective-permute-start.1 = (bf16[512,1536]{1,0:T(8,128)(2,1)}, bf16[512,1536]{1,0:T(8,128)(2,1)S(1)}, u32[]{:S(2)}, u32[]{:S(2)}) collective-permute-start(bf16[512,1536]{1,0:T(8,128)(2,1)} %all-gather.2.cloned.1.call-done), channel_id=1, source_target_pairs={{0,8},{8,0},{16,24},{24,16},{1,9},{9,1},{17,25},{25,17},{2,10},{10... | collective-permute-start | bytes 4718600 | tf_op jit(solution)/shard_map/ppermute | solution.py:26
  69.5 5.3 %copy-start.2 = (f32[1024]{0:T(1024)S(1)}, f32[1024]{0:T(1024)}, u32[]{:S(2)}) copy-start(f32[1024]{0:T(1024)} %param.11) | copy-start | bytes 12292
  69.5 43.3 %all-to-all-start = ((f16[8,128,1536]{2,1,0:T(8,128)(2,1)}), f16[8,128,1536]{2,1,0:T(8,128)(2,1)S(1)}, u32[]{:S(2)}, u32[]{:S(2)}) async-start(f16[8,128,1536]{2,1,0:T(8,128)(2,1)} %bitcast.54), calls=%async_computation | async-start | bytes 6291456 | tf_op jit(solution)/shard_map/all_to_all | solution.py:59
  74.9 39.3 %copy-start.1 = (f32[1536]{0:T(1024)S(1)}, f32[1536]{0:T(1024)}, u32[]{:S(2)}) copy-start(f32[1536]{0:T(1024)} %param.8) | copy-start | bytes 18436
  113.2 0.9 copy-start
  115.1 10.8 %collective-permute-start.3 = (bf16[128,1536]{1,0:T(8,128)(2,1)S(1)}, bf16[128,1536]{1,0:T(8,128)(2,1)S(1)}, u32[]{:S(2)}, u32[]{:S(2)}) collective-permute-start(bf16[128,1536]{1,0:T(8,128)(2,1)S(1)} %get-tuple-element.11), channel_id=1, source_target_pairs={{0,4},{1,5},{2,6},{3,7},{4,0},{5,1},{6,2},{7,3},{8,12},{9,13},{10,... | collective-permute-start | bytes 1179656 | tf_op jit(solution)/shard_map/ppermute | solution.py:31
  116.6 12.9 %collective-permute-start.6 = (bf16[128,1536]{1,0:T(8,128)(2,1)S(1)}, bf16[128,1536]{1,0:T(8,128)(2,1)S(1)}, u32[]{:S(2)}, u32[]{:S(2)}) collective-permute-start(bf16[128,1536]{1,0:T(8,128)(2,1)S(1)} %get-tuple-element.11), channel_id=1, source_target_pairs={{1,0},{2,1},{3,2},{0,3},{5,4},{6,5},{7,6},{4,7},{9,8},{10,9},{11,1... | collective-permute-start | bytes 1179656 | tf_op jit(solution)/shard_map/ppermute | solution.py:33
  125.9 9.9 %collective-permute-start.7 = (bf16[128,1536]{1,0:T(8,128)(2,1)S(1)}, bf16[128,1536]{1,0:T(8,128)(2,1)S(1)}, u32[]{:S(2)}, u32[]{:S(2)}) collective-permute-start(bf16[128,1536]{1,0:T(8,128)(2,1)S(1)} %collective-permute-done.3), channel_id=1, source_target_pairs={{1,0},{2,1},{3,2},{0,3},{5,4},{6,5},{7,6},{4,7},{9,8},{10,9},{11,1... | collective-permute-start | bytes 1179656 | tf_op jit(solution)/shard_map/ppermute | solution.py:35
  128.1 13.3 %collective-permute-start.2 = (bf16[128,1536]{1,0:T(8,128)(2,1)S(1)}, bf16[128,1536]{1,0:T(8,128)(2,1)S(1)}, u32[]{:S(2)}, u32[]{:S(2)}) collective-permute-start(bf16[128,1536]{1,0:T(8,128)(2,1)S(1)} %get-tuple-element.11), channel_id=1, source_target_pairs={{0,1},{1,2},{2,3},{3,0},{4,5},{5,6},{6,7},{7,4},{8,9},{9,10},{10,1... | collective-permute-start | bytes 1179656 | tf_op jit(solution)/shard_map/ppermute | solution.py:32
  128.7 18.4 %collective-permute-start.4 = (bf16[128,1536]{1,0:T(8,128)(2,1)S(1)}, bf16[128,1536]{1,0:T(8,128)(2,1)S(1)}, u32[]{:S(2)}, u32[]{:S(2)}) collective-permute-start(bf16[128,1536]{1,0:T(8,128)(2,1)S(1)} %collective-permute-done.3), channel_id=1, source_target_pairs={{0,1},{1,2},{2,3},{3,0},{4,5},{5,6},{6,7},{7,4},{8,9},{9,10},{10,1... | collective-permute-start | bytes 1179656 | tf_op jit(solution)/shard_map/ppermute | solution.py:34
  135.8 11.5 %collective-permute-start.8 = (bf16[128,1536]{1,0:T(8,128)(2,1)S(1)}, bf16[128,1536]{1,0:T(8,128)(2,1)S(1)}, u32[]{:S(2)}, u32[]{:S(2)}) collective-permute-start(bf16[128,1536]{1,0:T(8,128)(2,1)S(1)} %pad_maximum_fusion.1), channel_id=1, source_target_pairs={{1,0},{2,1},{3,2},{0,3},{5,4},{6,5},{7,6},{4,7},{9,8},{10,9},{11,1... | collective-permute-start | bytes 1179656 | tf_op jit(solution)/shard_map/ppermute | solution.py:38
  147.1 9.8 %collective-permute-start.5 = (bf16[128,1536]{1,0:T(8,128)(2,1)S(1)}, bf16[128,1536]{1,0:T(8,128)(2,1)S(1)}, u32[]{:S(2)}, u32[]{:S(2)}) collective-permute-start(bf16[128,1536]{1,0:T(8,128)(2,1)S(1)} %pad_maximum_fusion), channel_id=1, source_target_pairs={{0,1},{1,2},{2,3},{3,0},{4,5},{5,6},{6,7},{7,4},{8,9},{9,10},{10,1... | collective-permute-start | bytes 1179656 | tf_op jit(solution)/shard_map/ppermute | solution.py:37
  157.0 2.2 slice-start
  157.2 2.1 slice-start.1
  161.9 3.5 %collective-permute-start.9 = (f16[512,1536]{1,0:T(8,128)(2,1)S(1)}, f16[512,1536]{1,0:T(8,128)(2,1)S(1)}, u32[]{:S(2)}, u32[]{:S(2)}) collective-permute-start(f16[512,1536]{1,0:T(8,128)(2,1)S(1)} %fusion.1), channel_id=1, source_target_pairs={{0,8},{8,0},{16,24},{24,16},{1,9},{9,1},{17,25},{25,17},{2,10},{10... | collective-permute-start | bytes 4718600 | tf_op jit(solution)/shard_map/ppermute | solution.py:68
  168.1 107.3 %copy-start.3 = (f32[1536]{0:T(1024)S(1)}, f32[1536]{0:T(1024)}, u32[]{:S(2)}) copy-start(f32[1536]{0:T(1024)} %param.10) | copy-start | bytes 18436
  168.1 21.2 %collective-permute-start.10 = (f16[8,32,1536]{2,1,0:T(8,128)(2,1)S(1)}, f16[8,32,1536]{2,1,0:T(8,128)(2,1)S(1)}, u32[]{:S(2)}, u32[]{:S(2)}) collective-permute-start(f16[8,32,1536]{2,1,0:T(8,128)(2,1)S(1)} %fusion.37), channel_id=1, source_target_pairs={{0,16},{16,0},{8,24},{24,8},{1,17},{17,1},{9,25},{25,9},{2,18},{18... | collective-permute-start | bytes 2359304 | tf_op jit(solution)/shard_map/ppermute | solution.py:71
  190.5 84.8 %all-to-all-start.1 = ((f16[8,32,1536]{2,1,0:T(8,128)(2,1)}), f16[8,32,1536]{2,1,0:T(8,128)(2,1)S(1)}, u32[]{:S(2)}, u32[]{:S(2)}) async-start(f16[8,32,1536]{2,1,0:T(8,128)(2,1)} %fusion.3), calls=%async_computation.1 | async-start | bytes 1572864 | tf_op jit(solution)/shard_map/all_to_all | solution.py:73
Sparse Core Ops, SparseCore 0:
  15.4 42.2 all-gather.1

commit v2 on v0

v2 whole, which is shorter than its diff:
```python
import jax
import jax.numpy as jnp
from jax import lax
from jax.sharding import PartitionSpec as P

format_limit = 448.0
f32, f16, bf16 = jnp.float32, jnp.float16, jnp.bfloat16

up_gain = 16.0
down_gain = 64.0

core_swap = [(0, 1), (1, 0), (2, 3), (3, 2)]
x_hi_swap = [(0, 2), (2, 0), (1, 3), (3, 1)]
x_lo_swap = [(i, (i + 4) % 8) for i in range(8)]


def dot(a, b):
    return jnp.dot(a, b, preferred_element_type=f32)


def from_z(x, k):
    return lax.ppermute(x, "row", [((i + k) % 8, i) for i in range(8)])


def from_y(x, k):
    return lax.ppermute(x, "dep", [(4 * l + (i + k) % 4, 4 * l + i) for l in range(2) for i in range(4)])


def after(x, y):
    return lax.optimization_barrier((x, y))[0]


def gather_tokens(tokens):
    n, width = tokens.shape[0] // 2, tokens.shape[1]
    came = lax.ppermute(tokens, "col", x_hi_swap)
    own = jnp.concatenate([tokens[:n], came[:n], tokens[n:], came[n:]])
    z1, z7, z2, z6 = from_z(own, 1), from_z(own, 7), from_z(own, 2), from_z(own, 6)
    z3, z5 = from_z(z2, 1), from_z(z6, 7)
    z4 = jnp.concatenate([from_z(z2[: 2 * n], 2), from_z(z6[2 * n :], 6)])
    mine = jnp.stack([own, z1, z2, z3, z4, z5, z6, z7])
    both = jnp.stack([mine, lax.ppermute(mine, "col", core_swap)])
    both = both.reshape(2, 4, 2, 2, 2 * n, width)
    return both.transpose(3, 1, 0, 2, 4, 5).reshape(64 * n, width)


def local(tokens, w_up, bias_up, w_down, bias_down, amax_history):
    scale_factor = format_limit / jnp.max(amax_history)
    factor = down_gain / scale_factor
    dep, z = lax.axis_index("dep"), lax.axis_index("row")
    lo, y = dep // 4, dep % 4
    turn = (24 - z - 2 * y) % 8
    n, width = tokens.shape[0] // 2, tokens.shape[1]

    rows = gather_tokens(tokens)
    sent = (dot(rows, w_up) * up_gain).astype(f16).reshape(8, 8 * n, -1)
    got = lax.all_to_all(sent, "dep", 0, 0, tiled=True)
    summed = jnp.sum(got.astype(f32), axis=0) * (1.0 / up_gain)
    activated = jax.nn.gelu(summed + bias_up[None, :], approximate=True)
    peak = jnp.full((256, 128), jnp.max(jnp.abs(activated)))
    peak = lax.all_to_all(peak, ("row", "col", "dep"), 0, 0, tiled=True)
    q = jnp.clip(activated * scale_factor, -format_limit, format_limit).astype(bf16)

    h = 4 * n
    q1, q3 = from_y(q, 1), from_y(q, 3)
    p = lax.ppermute(q, "dep", x_lo_swap)
    q2 = from_y(q1[:h], 1), from_y(q3[h:], 3)
    p1, p3 = from_y(p, 1), from_y(p, 3)
    p2 = from_y(p1[:h], 1), from_y(p3[h:], 3)
    families = [
        [jnp.concatenate([v0[s], v1[s], v2[i], v3[s]]) for i, s in enumerate((slice(0, h), slice(h, 2 * h)))]
        for v0, v1, v2, v3 in ((q, q1, q2, q3), (p, p1, p2, p3))
    ]

    def away(rows):
        return lax.ppermute((dot(rows[1], w_down) * factor).astype(f16), "col", core_swap)

    def near(rows, came):
        total = (dot(rows[0], w_down) * factor + came.astype(f32)).reshape(8, 2, n, -1)
        return total[:, 0], total[:, 1].astype(f16)

    def turned(keep, came):
        total = (keep + came.astype(f32)).astype(f16)
        return lax.dynamic_slice_in_dim(jnp.concatenate([total, total]), turn, 8)

    def over_x_hi(x):
        return lax.ppermute(x, "col", x_hi_swap)

    def over_row(x):
        return lax.all_to_all(x, "row", 0, 0, tiled=True)

    def finish(got):
        mixed = jnp.sum(got.astype(f32), axis=0) * (1.0 / down_gain)
        return (mixed + bias_down[None, :]).astype(bf16)

    q_rows, p_rows = families
    q_came = away(q_rows)
    q_keep, q_send = near(q_rows, q_came)
    p_rows, peak = after((p_rows, peak), q_send)
    q_got = over_row(turned(q_keep, over_x_hi(q_send)))
    p_came = away(p_rows)
    p_keep, p_send = near(p_rows, p_came)
    p_got = over_row(after(turned(p_keep, over_x_hi(p_send)), q_got))
    q_out, p_out = finish(q_got), finish(p_got)
    first = lo == 0
    layer_output = jnp.concatenate([jnp.where(first, q_out, p_out), jnp.where(first, p_out, q_out)])
    history_next = jnp.concatenate([jnp.max(peak).reshape(1), amax_history[:-1]])
    return (layer_output, history_next)


def solution(mesh):
    in_specs = (
        P(("row", "col"), "dep"),
        P("dep", ("row", "col")),
        P(("row", "col")),
        P(("row", "col"), "dep"),
        P("dep"),
        P(),
    )
    out_specs = (P(("row", "col"), "dep"), P())
    return jax.shard_map(local, mesh=mesh, in_specs=in_specs, out_specs=out_specs, check_vma=False)
```

time: 409 us -> 193 us (0.47)
  waiting for transfers between devices: 301 us -> 89.3 us
  starting transfers between devices: 0.12 us -> 65.8 us
  blocking collectives: 62.5 us -> 0 us
  between operations: 14.4 us -> 2.31 us
    psum x1 -> x0, waiting for transfers between devices: 145 us -> none  [local(): summed = lax.psum(partial_value, 'dep')]
    all_gather x1 -> x0, waiting for transfers between devices: 88.3 us -> none  [local(): lax.all_gather(tokens, ('row', 'col'), axis=0, tiled=True)]
    reduce_scatter x1 -> x0, waiting for transfers between devices: 66.8 us -> none  [local(): lax.psum_scatter(jnp.dot(full_rows, w_down, preferred_element_type=jnp.fl...]
    pmax x1 -> x0, blocking collectives: 62.5 us -> none  [local(): new_peak = lax.pmax(jnp.max(jnp.abs(activated)), ('row', 'col'))]
    all_to_all x0 -> x4, waiting for transfers between devices: none -> 54.8 us  [the longest x1 35.6 us: local(): got = lax.all_to_all(sent, 'dep', 0, 0, tiled=True)]
    ppermute x0 -> x23, starting transfers between devices: none -> 38.7 us  [the longest x8 15.4 us: from_z(): return lax.ppermute(x, 'row', [((i + k) % 8, i) for i in range(8)])]
    ppermute x0 -> x23, waiting for transfers between devices: none -> 34.5 us  [the longest x8 13.6 us: from_z(): return lax.ppermute(x, 'row', [((i + k) % 8, i) for i in range(8)])]
    all_to_all x0 -> x4, starting transfers between devices: none -> 27 us  [the longest x2 12.7 us: over_row(): return lax.all_to_all(x, 'row', 0, 0, tiled=True)]
  transfers between devices with their start and end apart: 3 -> 27, of which waited for: 3 -> 14; matrix products, arithmetic and copies ran while one was open for 2% -> 11% of each run, Pallas kernels for 0% -> 0%
where the time goes in v2:
time: 193 us; the launch traced here: 191 us
  waiting for transfers between devices  89.3 us (46%)
  starting transfers between devices  65.8 us (34%)
  matrix products  19.5 us (10%)
  other arithmetic  10.8 us (6%)
  local copies, waits for them, and re-layouts  3.25 us (2%)
  between operations  2.31 us (1%)
    all_to_all x1, waiting for transfers between devices, local(): got = lax.all_to_all(sent, 'dep', 0, 0, tiled=True)  35.6 us
    dot_general x5, matrix products, dot(): return jnp.dot(a, b, preferred_element_type=f32)  19.5 us
    all_to_all x2, waiting for transfers between devices, over_row(): return lax.all_to_all(x, 'row', 0, 0, tiled=True)  19.2 us
    ppermute x8, starting transfers between devices, from_z(): return lax.ppermute(x, 'row', [((i + k) % 8, i) for i in range(8)])  15.4 us
    ppermute x8, waiting for transfers between devices, from_z(): return lax.ppermute(x, 'row', [((i + k) % 8, i) for i in range(8)])  13.6 us
    ppermute x8, starting transfers between devices, from_y(): lax.ppermute(x, 'dep', [(4 * l + (i + k) % 4, 4 * l + i) for l in range(2...  13.3 us
    all_to_all x2, starting transfers between devices, over_row(): return lax.all_to_all(x, 'row', 0, 0, tiled=True)  12.7 us
    ppermute x8, waiting for transfers between devices, from_y(): lax.ppermute(x, 'dep', [(4 * l + (i + k) % 4, 4 * l + i) for l in range(2...  11.5 us
  transfers between devices with their start and end apart: 27, of which 14 were waited for; matrix products, arithmetic and copies ran while one was open for 11% of the time, Pallas kernels for 0%

profile of v2, /device:TPU:32, one launch (start us, length us, event | category | flops | bytes accessed | tf_op | source)
XLA Modules:
  0.0 191.0 jit_solution(8820170501150173346)
XLA Ops:
  0.6 3.1 %collective-permute-start = (bf16[32,1536]{1,0:T(8,128)(2,1)}, bf16[32,1536]{1,0:T(8,128)(2,1)S(1)}, u32[]{:S(2)}, u32[]{:S(2)}) collective-permute-start(bf16[32,1536]{1,0:T(8,128)(2,1)} %param.6), channel_id=1, source_target_pairs={{0,16},{16,0},{8,24},{24,8},{1,17},{17,1},{9,25},{25,9},{2,18},{18... | collective-permute-start | bytes 294920 | tf_op jit(solution)/shard_map/ppermute | solution.py:35
  9.0 4.6 %collective-permute-start.2 = (bf16[64,1536]{1,0:T(8,128)(2,1)S(1)}, bf16[64,1536]{1,0:T(8,128)(2,1)S(1)}, u32[]{:S(2)}, u32[]{:S(2)}) collective-permute-start(bf16[64,1536]{1,0:T(8,128)(2,1)S(1)} %pad_maximum_fusion.2), channel_id=1, source_target_pairs={{64,0},{96,32},{128,64},{160,96},{192,128},{224,160},{0,192},{32,2... | collective-permute-start | bytes 589832 | tf_op jit(solution)/shard_map/ppermute | solution.py:22
  14.6 6.0 %collective-permute-done.2 = bf16[64,1536]{1,0:T(8,128)(2,1)S(1)} collective-permute-done((bf16[64,1536]{1,0:T(8,128)(2,1)S(1)}, bf16[64,1536]{1,0:T(8,128)(2,1)S(1)}, u32[]{:S(2)}, u32[]{:S(2)}) %collective-permute-start.2) | collective-permute-done | bytes 196640 | tf_op jit(solution)/shard_map/ppermute | solution.py:22
  20.7 4.6 %collective-permute-start.4 = (bf16[32,1536]{1,0:T(8,128)(2,1)S(1)}, bf16[32,1536]{1,0:T(8,128)(2,1)S(1)}, u32[]{:S(2)}, u32[]{:S(2)}) collective-permute-start(bf16[32,1536]{1,0:T(8,128)(2,1)S(1)} %slice.100), channel_id=1, source_target_pairs={{64,0},{96,32},{128,64},{160,96},{192,128},{224,160},{0,192},{32,2... | collective-permute-start | bytes 294920 | tf_op jit(solution)/shard_map/ppermute | solution.py:22
  30.1 3.6 %collective-permute-done.3 = bf16[64,1536]{1,0:T(8,128)(2,1)S(1)} collective-permute-done((bf16[64,1536]{1,0:T(8,128)(2,1)S(1)}, bf16[64,1536]{1,0:T(8,128)(2,1)S(1)}, u32[]{:S(2)}, u32[]{:S(2)}) %collective-permute-start.3) | collective-permute-done | bytes 196640 | tf_op jit(solution)/shard_map/ppermute | solution.py:22
  36.4 3.4 %collective-permute-done.9 = bf16[8,64,1536]{2,1,0:T(8,128)(2,1)S(1)} collective-permute-done((bf16[8,64,1536]{2,1,0:T(8,128)(2,1)S(1)}, bf16[8,64,1536]{2,1,0:T(8,128)(2,1)S(1)}, u32[]{:S(2)}, u32[]{:S(2)}) %collective-permute-start.9) | collective-permute-done | bytes 1572896 | tf_op jit(solution)/shard_map/ppermute | solution.py:41
  40.9 6.4 %multiply_convert_fusion = f16[1024,1536]{1,0:T(8,128)(2,1)} fusion(bf16[1024,1536]{1,0:T(8,128)(2,1)S(1)} %bitcast.58, bf16[1536,1536]{1,0:T(8,128)(2,1)S(1)} %bitcast.68), kind=kOutput, calls=%fused_computation.1 | convolution fusion | flops 4834983936 | bytes 11010048 | tf_op jit(solution)/shard_map/dot_general | solution.py:18
  47.3 6.0 %all-to-all-start = ((f16[8,128,1536]{2,1,0:T(8,128)(2,1)}), f16[8,128,1536]{2,1,0:T(8,128)(2,1)S(1)}, u32[]{:S(2)}, u32[]{:S(2)}) async-start(f16[8,128,1536]{2,1,0:T(8,128)(2,1)} %bitcast.57), calls=%async_computation | async-start | bytes 6291456 | tf_op jit(solution)/shard_map/all_to_all | solution.py:56
  55.3 35.6 %all-to-all-done = f16[8,128,1536]{2,1,0:T(8,128)(2,1)S(1)} async-done(((f16[8,128,1536]{2,1,0:T(8,128)(2,1)}), f16[8,128,1536]{2,1,0:T(8,128)(2,1)S(1)}, u32[]{:S(2)}, u32[]{:S(2)}) %all-to-all-start) | async-done | bytes 3145760 | tf_op jit(solution)/shard_map/all_to_all | solution.py:56
  98.4 8.3 %all-to-all-start.2 = ((f32[256,1,128]{2,1,0:T(1,128)}), f32[256,1,128]{2,1,0:T(1,128)S(1)}, u32[]{:S(2)}, u32[]{:S(2)}) async-start(f32[256,1,128]{2,1,0:T(1,128)} %broadcast_in_dim.2), calls=%async_computation.2 | async-start | bytes 262144 | tf_op jit(solution)/shard_map/all_to_all | solution.py:60
  110.5 2.9 %collective-permute-start.17 = (bf16[128,1536]{1,0:T(8,128)(2,1)S(1)}, bf16[128,1536]{1,0:T(8,128)(2,1)S(1)}, u32[]{:S(2)}, u32[]{:S(2)}) collective-permute-start(bf16[128,1536]{1,0:T(8,128)(2,1)S(1)} %collective-permute-done.16), channel_id=1, source_target_pairs={{1,0},{2,1},{3,2},{0,3},{5,4},{6,5},{7,6},{4,7},{9,8},{10,9},{11,1... | collective-permute-start | bytes 1179656 | tf_op jit(solution)/shard_map/ppermute | solution.py:26
  113.5 3.2 %collective-permute-done.13 = bf16[64,1536]{1,0:T(8,128)(2,1)S(1)} collective-permute-done((bf16[64,1536]{1,0:T(8,128)(2,1)S(1)}, bf16[64,1536]{1,0:T(8,128)(2,1)S(1)}, u32[]{:S(2)}, u32[]{:S(2)}) %collective-permute-start.13) | collective-permute-done | bytes 196640 | tf_op jit(solution)/shard_map/ppermute | solution.py:26
  116.7 3.8 %fusion.1 = f16[256,1536]{1,0:T(8,128)(2,1)S(1)} fusion(bf16[1536,1536]{1,0:T(8,128)(2,1)} %param.9, bf16[64,1536]{1,0:T(8,128)(2,1)S(1)} %get-tuple-element.23, bf16[64,1536]{1,0:T(8,128)(2,1)S(1)} %collective-permute-done.13, bf16[64,1536]{1,0:T(8,128)(2,1)S(1)} %get-tuple-element.21, bf16[64,1536]{1,0:T(8,128)(2,1)S(1)} %get-tuple-element.19, f32[]{:T(128)S(6)} %div.18), kind=kOutput, calls=%fused_computation.8 | convolution fusion | flops 1211891712 | bytes 6291460 | tf_op jit(solution)/shard_map/dot_general | solution.py:18
  120.7 4.1 %collective-permute-done.19 = bf16[128,1536]{1,0:T(8,128)(2,1)S(1)} collective-permute-done((bf16[128,1536]{1,0:T(8,128)(2,1)S(1)}, bf16[128,1536]{1,0:T(8,128)(2,1)S(1)}, u32[]{:S(2)}, u32[]{:S(2)}) %collective-permute-start.19) | collective-permute-done | bytes 393248 | tf_op jit(solution)/shard_map/ppermute | solution.py:26
  125.0 3.2 %collective-permute-start.18 = (bf16[64,1536]{1,0:T(8,128)(2,1)S(1)}, bf16[64,1536]{1,0:T(8,128)(2,1)S(1)}, u32[]{:S(2)}, u32[]{:S(2)}) collective-permute-start(bf16[64,1536]{1,0:T(8,128)(2,1)S(1)} %get-tuple-element.15), channel_id=1, source_target_pairs={{1,0},{2,1},{3,2},{0,3},{5,4},{6,5},{7,6},{4,7},{9,8},{10,9},{11,1... | collective-permute-start | bytes 589832 | tf_op jit(solution)/shard_map/ppermute | solution.py:26
  128.2 4.1 %collective-permute-done.20 = bf16[64,1536]{1,0:T(8,128)(2,1)S(1)} collective-permute-done((bf16[64,1536]{1,0:T(8,128)(2,1)S(1)}, bf16[64,1536]{1,0:T(8,128)(2,1)S(1)}, u32[]{:S(2)}, u32[]{:S(2)}) %collective-permute-start.20) | collective-permute-done | bytes 196640 | tf_op jit(solution)/shard_map/ppermute | solution.py:26
  135.6 3.7 %fusion.2 = f16[256,1536]{1,0:T(8,128)(2,1)S(1)} fusion(bf16[256,1536]{1,0:T(8,128)(2,1)S(1)} %pad_maximum_fusion.1, bf16[1536,1536]{1,0:T(8,128)(2,1)} %param.9, f32[]{:T(128)S(6)} %div.18), kind=kOutput, calls=%fused_computation.9 | convolution fusion | flops 1208745984 | bytes 6291460 | tf_op jit(solution)/shard_map/dot_general | solution.py:18
  139.5 2.9 %collective-permute-start.15 = (f16[8,16,1536]{2,1,0:T(8,128)(2,1)}, f16[8,16,1536]{2,1,0:T(8,128)(2,1)S(1)}, u32[]{:S(2)}, u32[]{:S(2)}) collective-permute-start(f16[8,16,1536]{2,1,0:T(8,128)(2,1)} %fusion.30), channel_id=1, source_target_pairs={{0,16},{16,0},{8,24},{24,8},{1,17},{17,1},{9,25},{25,9},{2,18},{18... | collective-permute-start | bytes 1179656 | tf_op jit(solution)/shard_map/ppermute | solution.py:86
  142.4 4.2 %convert_add_fusion = f32[256,1536]{1,0:T(8,128)S(1)} fusion(f16[256,1536]{1,0:T(8,128)(2,1)} %collective-permute-done.21, f32[]{:T(128)S(6)} %div.18, bf16[256,1536]{1,0:T(8,128)(2,1)} %pad_maximum_fusion, bf16[1536,1536]{1,0:T(8,128)(2,1)} %param.9), kind=kOutput, calls=%fused_computation.10 | convolution fusion | flops 1209139200 | bytes 7864324 | tf_op jit(solution)/shard_map/dot_general | solution.py:18
  149.6 3.6 %collective-permute-done.15 = f16[8,16,1536]{2,1,0:T(8,128)(2,1)S(1)} collective-permute-done((f16[8,16,1536]{2,1,0:T(8,128)(2,1)}, f16[8,16,1536]{2,1,0:T(8,128)(2,1)S(1)}, u32[]{:S(2)}, u32[]{:S(2)}) %collective-permute-start.15) | collective-permute-done | bytes 393248 | tf_op jit(solution)/shard_map/ppermute | solution.py:86
  154.3 7.9 %all-to-all-start.1 = ((f16[8,16,1536]{2,1,0:T(8,128)(2,1)}), f16[8,16,1536]{2,1,0:T(8,128)(2,1)S(1)}, u32[]{:S(2)}, u32[]{:S(2)}) async-start(f16[8,16,1536]{2,1,0:T(8,128)(2,1)} %fusion.29), calls=%async_computation.1 | async-start | bytes 786432 | tf_op jit(solution)/shard_map/all_to_all | solution.py:89
  164.3 10.3 %all-to-all-done.1 = f16[8,16,1536]{2,1,0:T(8,128)(2,1)S(1)} async-done(((f16[8,16,1536]{2,1,0:T(8,128)(2,1)}), f16[8,16,1536]{2,1,0:T(8,128)(2,1)S(1)}, u32[]{:S(2)}, u32[]{:S(2)}) %all-to-all-start.1) | async-done | bytes 393248 | tf_op jit(solution)/shard_map/all_to_all | solution.py:89
  174.6 4.8 %all-to-all-start.3 = ((f16[8,16,1536]{2,1,0:T(8,128)(2,1)}), f16[8,16,1536]{2,1,0:T(8,128)(2,1)S(1)}, u32[]{:S(2)}, u32[]{:S(2)}) async-start(f16[8,16,1536]{2,1,0:T(8,128)(2,1)} %fusion.28), calls=%async_computation.3 | async-start | bytes 786432 | tf_op jit(solution)/shard_map/all_to_all | solution.py:89
  181.4 8.9 %all-to-all-done.3 = f16[8,16,1536]{2,1,0:T(8,128)(2,1)S(1)} async-done(((f16[8,16,1536]{2,1,0:T(8,128)(2,1)}), f16[8,16,1536]{2,1,0:T(8,128)(2,1)S(1)}, u32[]{:S(2)}, u32[]{:S(2)}) %all-to-all-start.3) | async-done | bytes 393248 | tf_op jit(solution)/shard_map/all_to_all | solution.py:89
  (90 shorter events, 39.3 us)
Async XLA Ops:
  7.1 22.4 %collective-permute-start.1 = (bf16[64,1536]{1,0:T(8,128)(2,1)S(1)}, bf16[64,1536]{1,0:T(8,128)(2,1)S(1)}, u32[]{:S(2)}, u32[]{:S(2)}) collective-permute-start(bf16[64,1536]{1,0:T(8,128)(2,1)S(1)} %pad_maximum_fusion.2), channel_id=1, source_target_pairs={{32,0},{64,32},{96,64},{128,96},{160,128},{192,160},{224,192},{0,2... | collective-permute-start | bytes 589832 | tf_op jit(solution)/shard_map/ppermute | solution.py:22
  9.0 11.6 %collective-permute-start.2 = (bf16[64,1536]{1,0:T(8,128)(2,1)S(1)}, bf16[64,1536]{1,0:T(8,128)(2,1)S(1)}, u32[]{:S(2)}, u32[]{:S(2)}) collective-permute-start(bf16[64,1536]{1,0:T(8,128)(2,1)S(1)} %pad_maximum_fusion.2), channel_id=1, source_target_pairs={{64,0},{96,32},{128,64},{160,96},{192,128},{224,160},{0,192},{32,2... | collective-permute-start | bytes 589832 | tf_op jit(solution)/shard_map/ppermute | solution.py:22
  13.6 13.2 %collective-permute-start.5 = (bf16[64,1536]{1,0:T(8,128)(2,1)S(1)}, bf16[64,1536]{1,0:T(8,128)(2,1)S(1)}, u32[]{:S(2)}, u32[]{:S(2)}) collective-permute-start(bf16[64,1536]{1,0:T(8,128)(2,1)S(1)} %pad_maximum_fusion.2), channel_id=1, source_target_pairs={{192,0},{224,32},{0,64},{32,96},{64,128},{96,160},{128,192},{160,2... | collective-permute-start | bytes 589832 | tf_op jit(solution)/shard_map/ppermute | solution.py:22
  13.6 22.7 %collective-permute-start.8 = (bf16[64,1536]{1,0:T(8,128)(2,1)S(1)}, bf16[64,1536]{1,0:T(8,128)(2,1)S(1)}, u32[]{:S(2)}, u32[]{:S(2)}) collective-permute-start(bf16[64,1536]{1,0:T(8,128)(2,1)S(1)} %pad_maximum_fusion.2), channel_id=1, source_target_pairs={{224,0},{0,32},{32,64},{64,96},{96,128},{128,160},{160,192},{192,2... | collective-permute-start | bytes 589832 | tf_op jit(solution)/shard_map/ppermute | solution.py:22
  20.7 13.1 %collective-permute-start.4 = (bf16[32,1536]{1,0:T(8,128)(2,1)S(1)}, bf16[32,1536]{1,0:T(8,128)(2,1)S(1)}, u32[]{:S(2)}, u32[]{:S(2)}) collective-permute-start(bf16[32,1536]{1,0:T(8,128)(2,1)S(1)} %slice.100), channel_id=1, source_target_pairs={{64,0},{96,32},{128,64},{160,96},{192,128},{224,160},{0,192},{32,2... | collective-permute-start | bytes 294920 | tf_op jit(solution)/shard_map/ppermute | solution.py:22
  26.8 8.6 %collective-permute-start.6 = (bf16[32,1536]{1,0:T(8,128)(2,1)S(1)}, bf16[32,1536]{1,0:T(8,128)(2,1)S(1)}, u32[]{:S(2)}, u32[]{:S(2)}) collective-permute-start(bf16[32,1536]{1,0:T(8,128)(2,1)S(1)} %slice.101), channel_id=1, source_target_pairs={{192,0},{224,32},{0,64},{32,96},{64,128},{96,160},{128,192},{160,2... | collective-permute-start | bytes 294920 | tf_op jit(solution)/shard_map/ppermute | solution.py:22
  26.9 6.8 %collective-permute-start.3 = (bf16[64,1536]{1,0:T(8,128)(2,1)S(1)}, bf16[64,1536]{1,0:T(8,128)(2,1)S(1)}, u32[]{:S(2)}, u32[]{:S(2)}) collective-permute-start(bf16[64,1536]{1,0:T(8,128)(2,1)S(1)} %collective-permute-done.2), channel_id=1, source_target_pairs={{32,0},{64,32},{96,64},{128,96},{160,128},{192,160},{224,192},{0,2... | collective-permute-start | bytes 589832 | tf_op jit(solution)/shard_map/ppermute | solution.py:22
  29.5 6.7 %collective-permute-start.7 = (bf16[64,1536]{1,0:T(8,128)(2,1)S(1)}, bf16[64,1536]{1,0:T(8,128)(2,1)S(1)}, u32[]{:S(2)}, u32[]{:S(2)}) collective-permute-start(bf16[64,1536]{1,0:T(8,128)(2,1)S(1)} %collective-permute-done.5), channel_id=1, source_target_pairs={{224,0},{0,32},{32,64},{64,96},{96,128},{128,160},{160,192},{192,2... | collective-permute-start | bytes 589832 | tf_op jit(solution)/shard_map/ppermute | solution.py:22
  47.3 43.6 %all-to-all-start = ((f16[8,128,1536]{2,1,0:T(8,128)(2,1)}), f16[8,128,1536]{2,1,0:T(8,128)(2,1)S(1)}, u32[]{:S(2)}, u32[]{:S(2)}) async-start(f16[8,128,1536]{2,1,0:T(8,128)(2,1)} %bitcast.57), calls=%async_computation | async-start | bytes 6291456 | tf_op jit(solution)/shard_map/all_to_all | solution.py:56
  92.3 17.9 %collective-permute-start.16 = (bf16[128,1536]{1,0:T(8,128)(2,1)S(1)}, bf16[128,1536]{1,0:T(8,128)(2,1)S(1)}, u32[]{:S(2)}, u32[]{:S(2)}) collective-permute-start(bf16[128,1536]{1,0:T(8,128)(2,1)S(1)} %get-tuple-element.11), channel_id=1, source_target_pairs={{0,4},{1,5},{2,6},{3,7},{4,0},{5,1},{6,2},{7,3},{8,12},{9,13},{10,... | collective-permute-start | bytes 1179656 | tf_op jit(solution)/shard_map/ppermute | solution.py:65
  93.8 13.0 %collective-permute-start.12 = (bf16[128,1536]{1,0:T(8,128)(2,1)S(1)}, bf16[128,1536]{1,0:T(8,128)(2,1)S(1)}, u32[]{:S(2)}, u32[]{:S(2)}) collective-permute-start(bf16[128,1536]{1,0:T(8,128)(2,1)S(1)} %get-tuple-element.11), channel_id=1, source_target_pairs={{3,0},{0,1},{1,2},{2,3},{7,4},{4,5},{5,6},{6,7},{11,8},{8,9},{9,10... | collective-permute-start | bytes 1179656 | tf_op jit(solution)/shard_map/ppermute | solution.py:26
  94.6 13.8 %collective-permute-start.10 = (bf16[128,1536]{1,0:T(8,128)(2,1)S(1)}, bf16[128,1536]{1,0:T(8,128)(2,1)S(1)}, u32[]{:S(2)}, u32[]{:S(2)}) collective-permute-start(bf16[128,1536]{1,0:T(8,128)(2,1)S(1)} %get-tuple-element.11), channel_id=1, source_target_pairs={{1,0},{2,1},{3,2},{0,3},{5,4},{6,5},{7,6},{4,7},{9,8},{10,9},{11,1... | collective-permute-start | bytes 1179656 | tf_op jit(solution)/shard_map/ppermute | solution.py:26
  98.4 37.2 %all-to-all-start.2 = ((f32[256,1,128]{2,1,0:T(1,128)}), f32[256,1,128]{2,1,0:T(1,128)S(1)}, u32[]{:S(2)}, u32[]{:S(2)}) async-start(f32[256,1,128]{2,1,0:T(1,128)} %broadcast_in_dim.2), calls=%async_computation.2 | async-start | bytes 262144 | tf_op jit(solution)/shard_map/all_to_all | solution.py:60
  106.8 9.9 %collective-permute-start.13 = (bf16[64,1536]{1,0:T(8,128)(2,1)S(1)}, bf16[64,1536]{1,0:T(8,128)(2,1)S(1)}, u32[]{:S(2)}, u32[]{:S(2)}) collective-permute-start(bf16[64,1536]{1,0:T(8,128)(2,1)S(1)} %get-tuple-element.23), channel_id=1, source_target_pairs={{3,0},{0,1},{1,2},{2,3},{7,4},{4,5},{5,6},{6,7},{11,8},{8,9},{9,10... | collective-permute-start | bytes 589832 | tf_op jit(solution)/shard_map/ppermute | solution.py:26
  108.4 24.9 %collective-permute-start.11 = (bf16[64,1536]{1,0:T(8,128)(2,1)S(1)}, bf16[64,1536]{1,0:T(8,128)(2,1)S(1)}, u32[]{:S(2)}, u32[]{:S(2)}) collective-permute-start(bf16[64,1536]{1,0:T(8,128)(2,1)S(1)} %get-tuple-element.20), channel_id=1, source_target_pairs={{1,0},{2,1},{3,2},{0,3},{5,4},{6,5},{7,6},{4,7},{9,8},{10,9},{11,1... | collective-permute-start | bytes 589832 | tf_op jit(solution)/shard_map/ppermute | solution.py:26
  110.2 14.5 %collective-permute-start.19 = (bf16[128,1536]{1,0:T(8,128)(2,1)S(1)}, bf16[128,1536]{1,0:T(8,128)(2,1)S(1)}, u32[]{:S(2)}, u32[]{:S(2)}) collective-permute-start(bf16[128,1536]{1,0:T(8,128)(2,1)S(1)} %collective-permute-done.16), channel_id=1, source_target_pairs={{3,0},{0,1},{1,2},{2,3},{7,4},{4,5},{5,6},{6,7},{11,8},{8,9},{9,10... | collective-permute-start | bytes 1179656 | tf_op jit(solution)/shard_map/ppermute | solution.py:26
  110.5 14.5 %collective-permute-start.17 = (bf16[128,1536]{1,0:T(8,128)(2,1)S(1)}, bf16[128,1536]{1,0:T(8,128)(2,1)S(1)}, u32[]{:S(2)}, u32[]{:S(2)}) collective-permute-start(bf16[128,1536]{1,0:T(8,128)(2,1)S(1)} %collective-permute-done.16), channel_id=1, source_target_pairs={{1,0},{2,1},{3,2},{0,3},{5,4},{6,5},{7,6},{4,7},{9,8},{10,9},{11,1... | collective-permute-start | bytes 1179656 | tf_op jit(solution)/shard_map/ppermute | solution.py:26
  120.6 12.8 %collective-permute-start.14 = (f16[256,1536]{1,0:T(8,128)(2,1)S(1)}, f16[256,1536]{1,0:T(8,128)(2,1)S(1)}, u32[]{:S(2)}, u32[]{:S(2)}) collective-permute-start(f16[256,1536]{1,0:T(8,128)(2,1)S(1)} %fusion.1), channel_id=1, source_target_pairs={{0,8},{8,0},{16,24},{24,16},{1,9},{9,1},{17,25},{25,17},{2,10},{10... | collective-permute-start | bytes 2359304 | tf_op jit(solution)/shard_map/ppermute | solution.py:75
  124.8 7.5 %collective-permute-start.20 = (bf16[64,1536]{1,0:T(8,128)(2,1)S(1)}, bf16[64,1536]{1,0:T(8,128)(2,1)S(1)}, u32[]{:S(2)}, u32[]{:S(2)}) collective-permute-start(bf16[64,1536]{1,0:T(8,128)(2,1)S(1)} %get-tuple-element.16), channel_id=1, source_target_pairs={{3,0},{0,1},{1,2},{2,3},{7,4},{4,5},{5,6},{6,7},{11,8},{8,9},{9,10... | collective-permute-start | bytes 589832 | tf_op jit(solution)/shard_map/ppermute | solution.py:26
  125.0 7.3 %collective-permute-start.18 = (bf16[64,1536]{1,0:T(8,128)(2,1)S(1)}, bf16[64,1536]{1,0:T(8,128)(2,1)S(1)}, u32[]{:S(2)}, u32[]{:S(2)}) collective-permute-start(bf16[64,1536]{1,0:T(8,128)(2,1)S(1)} %get-tuple-element.15), channel_id=1, source_target_pairs={{1,0},{2,1},{3,2},{0,3},{5,4},{6,5},{7,6},{4,7},{9,8},{10,9},{11,1... | collective-permute-start | bytes 589832 | tf_op jit(solution)/shard_map/ppermute | solution.py:26
  139.5 13.7 %collective-permute-start.15 = (f16[8,16,1536]{2,1,0:T(8,128)(2,1)}, f16[8,16,1536]{2,1,0:T(8,128)(2,1)S(1)}, u32[]{:S(2)}, u32[]{:S(2)}) collective-permute-start(f16[8,16,1536]{2,1,0:T(8,128)(2,1)} %fusion.30), channel_id=1, source_target_pairs={{0,16},{16,0},{8,24},{24,8},{1,17},{17,1},{9,25},{25,9},{2,18},{18... | collective-permute-start | bytes 1179656 | tf_op jit(solution)/shard_map/ppermute | solution.py:86
  147.4 14.8 %collective-permute-start.22 = (f16[8,16,1536]{2,1,0:T(8,128)(2,1)}, f16[8,16,1536]{2,1,0:T(8,128)(2,1)}, u32[]{:S(2)}, u32[]{:S(2)}) collective-permute-start(f16[8,16,1536]{2,1,0:T(8,128)(2,1)} %fusion.31), channel_id=1, source_target_pairs={{0,16},{16,0},{8,24},{24,8},{1,17},{17,1},{9,25},{25,9},{2,18},{18... | collective-permute-start | bytes 1179656 | tf_op jit(solution)/shard_map/ppermute | solution.py:86
  154.3 20.3 %all-to-all-start.1 = ((f16[8,16,1536]{2,1,0:T(8,128)(2,1)}), f16[8,16,1536]{2,1,0:T(8,128)(2,1)S(1)}, u32[]{:S(2)}, u32[]{:S(2)}) async-start(f16[8,16,1536]{2,1,0:T(8,128)(2,1)} %fusion.29), calls=%async_computation.1 | async-start | bytes 786432 | tf_op jit(solution)/shard_map/all_to_all | solution.py:89
  174.6 15.7 %all-to-all-start.3 = ((f16[8,16,1536]{2,1,0:T(8,128)(2,1)}), f16[8,16,1536]{2,1,0:T(8,128)(2,1)S(1)}, u32[]{:S(2)}, u32[]{:S(2)}) async-start(f16[8,16,1536]{2,1,0:T(8,128)(2,1)} %fusion.28), calls=%async_computation.3 | async-start | bytes 786432 | tf_op jit(solution)/shard_map/all_to_all | solution.py:89
  (10 other events, 123.8 us)

commit v3 on v2

--- a/solution.py
+++ b/solution.py
@@ -43,6 +43,13 @@
     return both.transpose(3, 1, 0, 2, 4, 5).reshape(64 * n, width)
 
 
+def peak_over(peak, *steps):
+    for axis, step in steps:
+        size = {"row": 8, "col": 4, "dep": 8}[axis]
+        peak = jnp.maximum(peak, lax.ppermute(peak, axis, [(i, i ^ step) for i in range(size)]))
+    return peak
+
+
 def local(tokens, w_up, bias_up, w_down, bias_down, amax_history):
     scale_factor = format_limit / jnp.max(amax_history)
     factor = down_gain / scale_factor
@@ -56,26 +63,27 @@
     got = lax.all_to_all(sent, "dep", 0, 0, tiled=True)
     summed = jnp.sum(got.astype(f32), axis=0) * (1.0 / up_gain)
     activated = jax.nn.gelu(summed + bias_up[None, :], approximate=True)
-    peak = jnp.full((256, 128), jnp.max(jnp.abs(activated)))
-    peak = lax.all_to_all(peak, ("row", "col", "dep"), 0, 0, tiled=True)
+    peak = jnp.full((8, 128), jnp.max(jnp.abs(activated)))
     q = jnp.clip(activated * scale_factor, -format_limit, format_limit).astype(bf16)
 
     h = 4 * n
     q1, q3 = from_y(q, 1), from_y(q, 3)
     p = lax.ppermute(q, "dep", x_lo_swap)
+    peak, q1, q3 = lax.optimization_barrier((peak_over(peak, ("row", 1), ("row", 2)), q1, q3))
     q2 = from_y(q1[:h], 1), from_y(q3[h:], 3)
     p1, p3 = from_y(p, 1), from_y(p, 3)
     p2 = from_y(p1[:h], 1), from_y(p3[h:], 3)
-    families = [
-        [jnp.concatenate([v0[s], v1[s], v2[i], v3[s]]) for i, s in enumerate((slice(0, h), slice(h, 2 * h)))]
-        for v0, v1, v2, v3 in ((q, q1, q2, q3), (p, p1, p2, p3))
-    ]
 
-    def away(rows):
-        return lax.ppermute((dot(rows[1], w_down) * factor).astype(f16), "col", core_swap)
+    def down(v0, v1, v2, v3, s):
+        return dot(jnp.concatenate([v0[s], v1[s], v2[s.start // h], v3[s]]), w_down) * factor
 
-    def near(rows, came):
-        total = (dot(rows[0], w_down) * factor + came.astype(f32)).reshape(8, 2, n, -1)
+    own_core, other_core = slice(0, h), slice(h, 2 * h)
+
+    def over_core(total):
+        return lax.ppermute(total.astype(f16), "col", core_swap)
+
+    def near(total, came):
+        total = (total + came.astype(f32)).reshape(8, 2, n, -1)
         return total[:, 0], total[:, 1].astype(f16)
 
     def turned(keep, came):
@@ -92,18 +100,25 @@
         mixed = jnp.sum(got.astype(f32), axis=0) * (1.0 / down_gain)
         return (mixed + bias_down[None, :]).astype(bf16)
 
-    q_rows, p_rows = families
-    q_came = away(q_rows)
-    q_keep, q_send = near(q_rows, q_came)
-    p_rows, peak = after((p_rows, peak), q_send)
-    q_got = over_row(turned(q_keep, over_x_hi(q_send)))
-    p_came = away(p_rows)
-    p_keep, p_send = near(p_rows, p_came)
-    p_got = over_row(after(turned(p_keep, over_x_hi(p_send)), q_got))
+    q_came = over_core(down(q, q1, q2, q3, other_core))
+    q_keep, q_send = near(down(q, q1, q2, q3, own_core), q_came)
+    p2 = after(p2, q_send)
+    p_came = over_core(down(p, p1, p2, p3, other_core))
+    p_total = down(p, p1, p2, p3, own_core)
+    q_sum = turned(q_keep, over_x_hi(q_send))
+    q_got = over_row(q_sum)
+    peak = peak_over(peak, ("row", 4), ("col", 1))
+    p_total, p_came, peak = after((p_total, p_came, peak), q_sum)
+    p_keep, p_send = near(p_total, p_came)
+    p_came, peak = lax.optimization_barrier((over_x_hi(p_send), peak))
+    peak = peak_over(peak, ("dep", 1), ("dep", 2))
+    p_sum, peak = after((turned(p_keep, p_came), peak), q_got)
+    p_got = over_row(p_sum)
+    peak = peak_over(peak, ("dep", 4), ("col", 2))
     q_out, p_out = finish(q_got), finish(p_got)
     first = lo == 0
     layer_output = jnp.concatenate([jnp.where(first, q_out, p_out), jnp.where(first, p_out, q_out)])
-    history_next = jnp.concatenate([jnp.max(peak).reshape(1), amax_history[:-1]])
+    history_next = jnp.concatenate([peak[0, :1], amax_history[:-1]])
     return (layer_output, history_next)
 
 

time: 193 us -> 182 us (0.943)
  matrix products: 19.5 us -> 14.5 us
  waiting for transfers between devices: 89.3 us -> 84.7 us
  other arithmetic: 10.8 us -> 8.1 us
    all_to_all x2, waiting for transfers between devices: 19.2 us -> 1.49 us  [over_row(): return lax.all_to_all(x, 'row', 0, 0, tiled=True)]
    ppermute x2 -> x10, waiting for transfers between devices: 0.01 us -> 15.4 us  [the longest x8 15.4 us: peak_over(): lax.ppermute(peak, axis, [(i, i ^ step) for i in range(size)])]
    ppermute x2 -> x10, starting transfers between devices: 0.19 us -> 11.3 us  [the longest x8 10.9 us: peak_over(): lax.ppermute(peak, axis, [(i, i ^ step) for i in range(size)])]
    all_to_all x1 -> x0, starting transfers between devices: 8.29 us -> none  [local(): peak = lax.all_to_all(peak, ('row', 'col', 'dep'), 0, 0, tiled=True)]
    dot_general x5, matrix products: 19.5 us -> 14.5 us  [dot(): return jnp.dot(a, b, preferred_element_type=f32)]
    ppermute x8, waiting for transfers between devices: 11.5 us -> 8.67 us  [from_y(): lax.ppermute(x, 'dep', [(4 * l + (i + k) % 4, 4 * l + i) for l in range(2...]
    ppermute x8, starting transfers between devices: 13.3 us -> 11.3 us  [from_y(): lax.ppermute(x, 'dep', [(4 * l + (i + k) % 4, 4 * l + i) for l in range(2...]
  transfers between devices with their start and end apart: 27 -> 34, of which waited for: 14 -> 23; matrix products, arithmetic and copies ran while one was open for 11% -> 8% of each run, Pallas kernels for 0% -> 0%
where the time goes in v3:
time: 182 us; the launch traced here: 179 us
  waiting for transfers between devices  84.7 us (47%)
  starting transfers between devices  66.8 us (37%)
  matrix products  14.5 us (8%)
  other arithmetic  8.1 us (4%)
  local copies, waits for them, and re-layouts  3.03 us (2%)
  between operations  2.38 us (1%)
    all_to_all x1, waiting for transfers between devices, local(): got = lax.all_to_all(sent, 'dep', 0, 0, tiled=True)  36.3 us
    ppermute x8, starting transfers between devices, from_z(): return lax.ppermute(x, 'row', [((i + k) % 8, i) for i in range(8)])  15.4 us
    ppermute x8, waiting for transfers between devices, peak_over(): lax.ppermute(peak, axis, [(i, i ^ step) for i in range(size)])  15.4 us
    dot_general x5, matrix products, dot(): return jnp.dot(a, b, preferred_element_type=f32)  14.5 us
    ppermute x8, waiting for transfers between devices, from_z(): return lax.ppermute(x, 'row', [((i + k) % 8, i) for i in range(8)])  13.6 us
    all_to_all x2, starting transfers between devices, over_row(): return lax.all_to_all(x, 'row', 0, 0, tiled=True)  12.4 us
    ppermute x8, starting transfers between devices, from_y(): lax.ppermute(x, 'dep', [(4 * l + (i + k) % 4, 4 * l + i) for l in range(2...  11.3 us
    ppermute x8, starting transfers between devices, peak_over(): lax.ppermute(peak, axis, [(i, i ^ step) for i in range(size)])  10.9 us
  transfers between devices with their start and end apart: 34, of which 23 were waited for; matrix products, arithmetic and copies ran while one was open for 8% of the time, Pallas kernels for 0%

profile of v3, /device:TPU:32, one launch (start us, length us, event | category | flops | bytes accessed | tf_op | source)
XLA Modules:
  0.0 179.5 jit_solution(2678802594032773914)
XLA Ops:
  0.6 3.1 %collective-permute-start = (bf16[32,1536]{1,0:T(8,128)(2,1)}, bf16[32,1536]{1,0:T(8,128)(2,1)S(1)}, u32[]{:S(2)}, u32[]{:S(2)}) collective-permute-start(bf16[32,1536]{1,0:T(8,128)(2,1)} %param.6), channel_id=1, source_target_pairs={{0,16},{16,0},{8,24},{24,8},{1,17},{17,1},{9,25},{25,9},{2,18},{18... | collective-permute-start | bytes 294920 | tf_op jit(solution)/shard_map/ppermute | solution.py:35
  9.0 4.6 %collective-permute-start.2 = (bf16[64,1536]{1,0:T(8,128)(2,1)S(1)}, bf16[64,1536]{1,0:T(8,128)(2,1)S(1)}, u32[]{:S(2)}, u32[]{:S(2)}) collective-permute-start(bf16[64,1536]{1,0:T(8,128)(2,1)S(1)} %pad_maximum_fusion), channel_id=1, source_target_pairs={{64,0},{96,32},{128,64},{160,96},{192,128},{224,160},{0,192},{32,2... | collective-permute-start | bytes 589832 | tf_op jit(solution)/shard_map/ppermute | solution.py:22
  14.6 6.0 %collective-permute-done.2 = bf16[64,1536]{1,0:T(8,128)(2,1)S(1)} collective-permute-done((bf16[64,1536]{1,0:T(8,128)(2,1)S(1)}, bf16[64,1536]{1,0:T(8,128)(2,1)S(1)}, u32[]{:S(2)}, u32[]{:S(2)}) %collective-permute-start.2) | collective-permute-done | bytes 196640 | tf_op jit(solution)/shard_map/ppermute | solution.py:22
  20.7 4.6 %collective-permute-start.4 = (bf16[32,1536]{1,0:T(8,128)(2,1)S(1)}, bf16[32,1536]{1,0:T(8,128)(2,1)S(1)}, u32[]{:S(2)}, u32[]{:S(2)}) collective-permute-start(bf16[32,1536]{1,0:T(8,128)(2,1)S(1)} %slice.104), channel_id=1, source_target_pairs={{64,0},{96,32},{128,64},{160,96},{192,128},{224,160},{0,192},{32,2... | collective-permute-start | bytes 294920 | tf_op jit(solution)/shard_map/ppermute | solution.py:22
  26.9 2.7 %collective-permute-start.3 = (bf16[64,1536]{1,0:T(8,128)(2,1)S(1)}, bf16[64,1536]{1,0:T(8,128)(2,1)S(1)}, u32[]{:S(2)}, u32[]{:S(2)}) collective-permute-start(bf16[64,1536]{1,0:T(8,128)(2,1)S(1)} %collective-permute-done.2), channel_id=1, source_target_pairs={{32,0},{64,32},{96,64},{128,96},{160,128},{192,160},{224,192},{0,2... | collective-permute-start | bytes 589832 | tf_op jit(solution)/shard_map/ppermute | solution.py:22
  30.1 3.6 %collective-permute-done.3 = bf16[64,1536]{1,0:T(8,128)(2,1)S(1)} collective-permute-done((bf16[64,1536]{1,0:T(8,128)(2,1)S(1)}, bf16[64,1536]{1,0:T(8,128)(2,1)S(1)}, u32[]{:S(2)}, u32[]{:S(2)}) %collective-permute-start.3) | collective-permute-done | bytes 196640 | tf_op jit(solution)/shard_map/ppermute | solution.py:22
  36.4 3.4 %collective-permute-done.9 = bf16[8,64,1536]{2,1,0:T(8,128)(2,1)S(1)} collective-permute-done((bf16[8,64,1536]{2,1,0:T(8,128)(2,1)S(1)}, bf16[8,64,1536]{2,1,0:T(8,128)(2,1)S(1)}, u32[]{:S(2)}, u32[]{:S(2)}) %collective-permute-start.9) | collective-permute-done | bytes 1572896 | tf_op jit(solution)/shard_map/ppermute | solution.py:41
  40.9 6.5 %multiply_convert_fusion = f16[1024,1536]{1,0:T(8,128)(2,1)} fusion(bf16[1024,1536]{1,0:T(8,128)(2,1)S(1)} %bitcast.57, bf16[1536,1536]{1,0:T(8,128)(2,1)S(1)} %bitcast.64), kind=kOutput, calls=%fused_computation.1 | convolution fusion | flops 4834983936 | bytes 11010048 | tf_op jit(solution)/shard_map/dot_general | solution.py:18
  47.3 6.0 %all-to-all-start = ((f16[8,128,1536]{2,1,0:T(8,128)(2,1)}), f16[8,128,1536]{2,1,0:T(8,128)(2,1)S(1)}, u32[]{:S(2)}, u32[]{:S(2)}) async-start(f16[8,128,1536]{2,1,0:T(8,128)(2,1)} %bitcast.56), calls=%async_computation | async-start | bytes 6291456 | tf_op jit(solution)/shard_map/all_to_all | solution.py:63
  54.7 36.3 %all-to-all-done = f16[8,128,1536]{2,1,0:T(8,128)(2,1)S(1)} async-done(((f16[8,128,1536]{2,1,0:T(8,128)(2,1)}), f16[8,128,1536]{2,1,0:T(8,128)(2,1)S(1)}, u32[]{:S(2)}, u32[]{:S(2)}) %all-to-all-start) | async-done | bytes 3145760 | tf_op jit(solution)/shard_map/all_to_all | solution.py:63
  93.0 2.8 %collective-permute-start.10 = (f32[8,128]{1,0:T(8,128)S(1)}, f32[8,128]{1,0:T(8,128)S(1)}, u32[]{:S(2)}, u32[]{:S(2)}) collective-permute-start(f32[8,128]{1,0:T(8,128)S(1)} %broadcast_in_dim.2), channel_id=1, source_target_pairs={{0,32},{32,0},{64,96},{96,64},{128,160},{160,128},{192,224},{224,1... | collective-permute-start | bytes 12296 | tf_op jit(solution)/shard_map/ppermute | solution.py:49
  100.9 2.9 %collective-permute-done.11 = f32[8,128]{1,0:T(8,128)S(1)} collective-permute-done((f32[8,128]{1,0:T(8,128)S(1)}, f32[8,128]{1,0:T(8,128)S(1)}, u32[]{:S(2)}, u32[]{:S(2)}) %collective-permute-start.11) | collective-permute-done | bytes 4128 | tf_op jit(solution)/shard_map/ppermute | solution.py:49
  104.5 2.5 %collective-permute-done.12 = bf16[128,1536]{1,0:T(8,128)(2,1)S(1)} collective-permute-done((bf16[128,1536]{1,0:T(8,128)(2,1)S(1)}, bf16[128,1536]{1,0:T(8,128)(2,1)S(1)}, u32[]{:S(2)}, u32[]{:S(2)}) %collective-permute-start.12) | collective-permute-done | bytes 393248 | tf_op jit(solution)/shard_map/ppermute | solution.py:26
  110.2 3.3 %collective-permute-start.14 = (bf16[64,1536]{1,0:T(8,128)(2,1)S(1)}, bf16[64,1536]{1,0:T(8,128)(2,1)S(1)}, u32[]{:S(2)}, u32[]{:S(2)}) collective-permute-start(bf16[64,1536]{1,0:T(8,128)(2,1)S(1)} %get-tuple-element.36), channel_id=1, source_target_pairs={{1,0},{2,1},{3,2},{0,3},{5,4},{6,5},{7,6},{4,7},{9,8},{10,9},{11,1... | collective-permute-start | bytes 589832 | tf_op jit(solution)/shard_map/ppermute | solution.py:26
  119.1 3.9 %fusion.1 = f16[256,1536]{1,0:T(8,128)(2,1)S(1)} fusion(bf16[1536,1536]{1,0:T(8,128)(2,1)} %param.9, bf16[64,1536]{1,0:T(8,128)(2,1)S(1)} %get-tuple-element.39, bf16[64,1536]{1,0:T(8,128)(2,1)S(1)} %collective-permute-done.15, bf16[64,1536]{1,0:T(8,128)(2,1)S(1)} %get-tuple-element.37, bf16[64,1536]{1,0:T(8,128)(2,1)S(1)} %get-tuple-element.35, f32[]{:T(128)S(6)} %div.18), kind=kOutput, calls=%fused_computation.8 | convolution fusion | flops 1211891712 | bytes 6291460 | tf_op jit(solution)/shard_map/dot_general | solution.py:18
  123.3 3.7 %collective-permute-start.20 = (bf16[64,1536]{1,0:T(8,128)(2,1)S(1)}, bf16[64,1536]{1,0:T(8,128)(2,1)S(1)}, u32[]{:S(2)}, u32[]{:S(2)}) collective-permute-start(bf16[64,1536]{1,0:T(8,128)(2,1)S(1)} %get-tuple-element.31), channel_id=1, source_target_pairs={{1,0},{2,1},{3,2},{0,3},{5,4},{6,5},{7,6},{4,7},{9,8},{10,9},{11,1... | collective-permute-start | bytes 589832 | tf_op jit(solution)/shard_map/ppermute | solution.py:26
  128.6 2.8 %collective-permute-start.17 = (f16[8,16,1536]{2,1,0:T(8,128)(2,1)S(1)}, f16[8,16,1536]{2,1,0:T(8,128)(2,1)S(1)}, u32[]{:S(2)}, u32[]{:S(2)}) collective-permute-start(f16[8,16,1536]{2,1,0:T(8,128)(2,1)S(1)} %fusion.44), channel_id=1, source_target_pairs={{0,16},{16,0},{8,24},{24,8},{1,17},{17,1},{9,25},{25,9},{2,18},{18... | collective-permute-start | bytes 1179656 | tf_op jit(solution)/shard_map/ppermute | solution.py:94
  131.5 2.5 %collective-permute-done.22 = bf16[64,1536]{1,0:T(8,128)(2,1)S(1)} collective-permute-done((bf16[64,1536]{1,0:T(8,128)(2,1)S(1)}, bf16[64,1536]{1,0:T(8,128)(2,1)S(1)}, u32[]{:S(2)}, u32[]{:S(2)}) %collective-permute-start.22) | collective-permute-done | bytes 196640 | tf_op jit(solution)/shard_map/ppermute | solution.py:26
  140.8 2.8 %collective-permute-start.26 = (f16[8,16,1536]{2,1,0:T(8,128)(2,1)S(1)}, f16[8,16,1536]{2,1,0:T(8,128)(2,1)S(1)}, u32[]{:S(2)}, u32[]{:S(2)}) collective-permute-start(f16[8,16,1536]{2,1,0:T(8,128)(2,1)S(1)} %fusion.45), channel_id=1, source_target_pairs={{0,16},{16,0},{8,24},{24,8},{1,17},{17,1},{9,25},{25,9},{2,18},{18... | collective-permute-start | bytes 1179656 | tf_op jit(solution)/shard_map/ppermute | solution.py:94
  143.7 6.9 %all-to-all-start.1 = ((f16[8,16,1536]{2,1,0:T(8,128)(2,1)}), f16[8,16,1536]{2,1,0:T(8,128)(2,1)S(1)}, u32[]{:S(2)}, u32[]{:S(2)}) async-start(f16[8,16,1536]{2,1,0:T(8,128)(2,1)} %fusion.43), calls=%async_computation.1 | async-start | bytes 786432 | tf_op jit(solution)/shard_map/all_to_all | solution.py:97
  156.2 4.0 %collective-permute-done.28 = f32[8,128]{1,0:T(8,128)S(1)} collective-permute-done((f32[8,128]{1,0:T(8,128)S(1)}, f32[8,128]{1,0:T(8,128)S(1)}, u32[]{:S(2)}, u32[]{:S(2)}) %collective-permute-start.28) | collective-permute-done | bytes 4128 | tf_op jit(solution)/shard_map/ppermute | solution.py:49
  161.7 5.5 %all-to-all-start.2 = ((f16[8,16,1536]{2,1,0:T(8,128)(2,1)}), f16[8,16,1536]{2,1,0:T(8,128)(2,1)S(1)}, u32[]{:S(2)}, u32[]{:S(2)}) async-start(f16[8,16,1536]{2,1,0:T(8,128)(2,1)} %fusion.42), calls=%async_computation.2 | async-start | bytes 786432 | tf_op jit(solution)/shard_map/all_to_all | solution.py:97
  167.2 3.0 %collective-permute-start.29 = (f32[8,128]{1,0:T(8,128)S(1)}, f32[8,128]{1,0:T(8,128)S(1)}, u32[]{:S(2)}, u32[]{:S(2)}) collective-permute-start(f32[8,128]{1,0:T(8,128)S(1)} %max.36), channel_id=1, source_target_pairs={{0,4},{1,5},{2,6},{3,7},{4,0},{5,1},{6,2},{7,3},{8,12},{9,13},{10,... | collective-permute-start | bytes 12296 | tf_op jit(solution)/shard_map/ppermute | solution.py:49
  171.8 2.7 %collective-permute-start.30 = (f32[8,128]{1,0:T(8,128)S(1)}, f32[8,128]{1,0:T(8,128)S(1)}, u32[]{:S(2)}, u32[]{:S(2)}) collective-permute-start(f32[8,128]{1,0:T(8,128)S(1)} %max.37), channel_id=1, source_target_pairs={{0,16},{8,24},{16,0},{24,8},{1,17},{9,25},{17,1},{25,9},{2,18},{10... | collective-permute-start | bytes 12296 | tf_op jit(solution)/shard_map/ppermute | solution.py:49
  (111 shorter events, 51.0 us)
Async XLA Ops:
  0.6 6.4 %collective-permute-start = (bf16[32,1536]{1,0:T(8,128)(2,1)}, bf16[32,1536]{1,0:T(8,128)(2,1)S(1)}, u32[]{:S(2)}, u32[]{:S(2)}) collective-permute-start(bf16[32,1536]{1,0:T(8,128)(2,1)} %param.6), channel_id=1, source_target_pairs={{0,16},{16,0},{8,24},{24,8},{1,17},{17,1},{9,25},{25,9},{2,18},{18... | collective-permute-start | bytes 294920 | tf_op jit(solution)/shard_map/ppermute | solution.py:35
  7.1 22.4 %collective-permute-start.1 = (bf16[64,1536]{1,0:T(8,128)(2,1)S(1)}, bf16[64,1536]{1,0:T(8,128)(2,1)S(1)}, u32[]{:S(2)}, u32[]{:S(2)}) collective-permute-start(bf16[64,1536]{1,0:T(8,128)(2,1)S(1)} %pad_maximum_fusion), channel_id=1, source_target_pairs={{32,0},{64,32},{96,64},{128,96},{160,128},{192,160},{224,192},{0,2... | collective-permute-start | bytes 589832 | tf_op jit(solution)/shard_map/ppermute | solution.py:22
  9.0 11.6 %collective-permute-start.2 = (bf16[64,1536]{1,0:T(8,128)(2,1)S(1)}, bf16[64,1536]{1,0:T(8,128)(2,1)S(1)}, u32[]{:S(2)}, u32[]{:S(2)}) collective-permute-start(bf16[64,1536]{1,0:T(8,128)(2,1)S(1)} %pad_maximum_fusion), channel_id=1, source_target_pairs={{64,0},{96,32},{128,64},{160,96},{192,128},{224,160},{0,192},{32,2... | collective-permute-start | bytes 589832 | tf_op jit(solution)/shard_map/ppermute | solution.py:22
  13.6 13.2 %collective-permute-start.5 = (bf16[64,1536]{1,0:T(8,128)(2,1)S(1)}, bf16[64,1536]{1,0:T(8,128)(2,1)S(1)}, u32[]{:S(2)}, u32[]{:S(2)}) collective-permute-start(bf16[64,1536]{1,0:T(8,128)(2,1)S(1)} %pad_maximum_fusion), channel_id=1, source_target_pairs={{192,0},{224,32},{0,64},{32,96},{64,128},{96,160},{128,192},{160,2... | collective-permute-start | bytes 589832 | tf_op jit(solution)/shard_map/ppermute | solution.py:22
  13.6 22.7 %collective-permute-start.8 = (bf16[64,1536]{1,0:T(8,128)(2,1)S(1)}, bf16[64,1536]{1,0:T(8,128)(2,1)S(1)}, u32[]{:S(2)}, u32[]{:S(2)}) collective-permute-start(bf16[64,1536]{1,0:T(8,128)(2,1)S(1)} %pad_maximum_fusion), channel_id=1, source_target_pairs={{224,0},{0,32},{32,64},{64,96},{96,128},{128,160},{160,192},{192,2... | collective-permute-start | bytes 589832 | tf_op jit(solution)/shard_map/ppermute | solution.py:22
  20.7 13.1 %collective-permute-start.4 = (bf16[32,1536]{1,0:T(8,128)(2,1)S(1)}, bf16[32,1536]{1,0:T(8,128)(2,1)S(1)}, u32[]{:S(2)}, u32[]{:S(2)}) collective-permute-start(bf16[32,1536]{1,0:T(8,128)(2,1)S(1)} %slice.104), channel_id=1, source_target_pairs={{64,0},{96,32},{128,64},{160,96},{192,128},{224,160},{0,192},{32,2... | collective-permute-start | bytes 294920 | tf_op jit(solution)/shard_map/ppermute | solution.py:22
  26.8 8.6 %collective-permute-start.6 = (bf16[32,1536]{1,0:T(8,128)(2,1)S(1)}, bf16[32,1536]{1,0:T(8,128)(2,1)S(1)}, u32[]{:S(2)}, u32[]{:S(2)}) collective-permute-start(bf16[32,1536]{1,0:T(8,128)(2,1)S(1)} %slice.105), channel_id=1, source_target_pairs={{192,0},{224,32},{0,64},{32,96},{64,128},{96,160},{128,192},{160,2... | collective-permute-start | bytes 294920 | tf_op jit(solution)/shard_map/ppermute | solution.py:22
  26.9 6.8 %collective-permute-start.3 = (bf16[64,1536]{1,0:T(8,128)(2,1)S(1)}, bf16[64,1536]{1,0:T(8,128)(2,1)S(1)}, u32[]{:S(2)}, u32[]{:S(2)}) collective-permute-start(bf16[64,1536]{1,0:T(8,128)(2,1)S(1)} %collective-permute-done.2), channel_id=1, source_target_pairs={{32,0},{64,32},{96,64},{128,96},{160,128},{192,160},{224,192},{0,2... | collective-permute-start | bytes 589832 | tf_op jit(solution)/shard_map/ppermute | solution.py:22
  29.5 6.7 %collective-permute-start.7 = (bf16[64,1536]{1,0:T(8,128)(2,1)S(1)}, bf16[64,1536]{1,0:T(8,128)(2,1)S(1)}, u32[]{:S(2)}, u32[]{:S(2)}) collective-permute-start(bf16[64,1536]{1,0:T(8,128)(2,1)S(1)} %collective-permute-done.5), channel_id=1, source_target_pairs={{224,0},{0,32},{32,64},{64,96},{96,128},{128,160},{160,192},{192,2... | collective-permute-start | bytes 589832 | tf_op jit(solution)/shard_map/ppermute | solution.py:22
  47.3 43.6 %all-to-all-start = ((f16[8,128,1536]{2,1,0:T(8,128)(2,1)}), f16[8,128,1536]{2,1,0:T(8,128)(2,1)S(1)}, u32[]{:S(2)}, u32[]{:S(2)}) async-start(f16[8,128,1536]{2,1,0:T(8,128)(2,1)} %bitcast.56), calls=%async_computation | async-start | bytes 6291456 | tf_op jit(solution)/shard_map/all_to_all | solution.py:63
  96.5 10.5 %collective-permute-start.12 = (bf16[128,1536]{1,0:T(8,128)(2,1)S(1)}, bf16[128,1536]{1,0:T(8,128)(2,1)S(1)}, u32[]{:S(2)}, u32[]{:S(2)}) collective-permute-start(bf16[128,1536]{1,0:T(8,128)(2,1)S(1)} %get-tuple-element.26), channel_id=1, source_target_pairs={{1,0},{2,1},{3,2},{0,3},{5,4},{6,5},{7,6},{4,7},{9,8},{10,9},{11,1... | collective-permute-start | bytes 1179656 | tf_op jit(solution)/shard_map/ppermute | solution.py:26
  98.5 10.7 %collective-permute-start.13 = (bf16[128,1536]{1,0:T(8,128)(2,1)S(1)}, bf16[128,1536]{1,0:T(8,128)(2,1)S(1)}, u32[]{:S(2)}, u32[]{:S(2)}) collective-permute-start(bf16[128,1536]{1,0:T(8,128)(2,1)S(1)} %get-tuple-element.26), channel_id=1, source_target_pairs={{3,0},{0,1},{1,2},{2,3},{7,4},{4,5},{5,6},{6,7},{11,8},{8,9},{9,10... | collective-permute-start | bytes 1179656 | tf_op jit(solution)/shard_map/ppermute | solution.py:26
  99.4 14.1 %collective-permute-start.18 = (bf16[128,1536]{1,0:T(8,128)(2,1)S(1)}, bf16[128,1536]{1,0:T(8,128)(2,1)S(1)}, u32[]{:S(2)}, u32[]{:S(2)}) collective-permute-start(bf16[128,1536]{1,0:T(8,128)(2,1)S(1)} %get-tuple-element.26), channel_id=1, source_target_pairs={{0,4},{1,5},{2,6},{3,7},{4,0},{5,1},{6,2},{7,3},{8,12},{9,13},{10,... | collective-permute-start | bytes 1179656 | tf_op jit(solution)/shard_map/ppermute | solution.py:71
  109.2 7.5 %collective-permute-start.24 = (f32[8,128]{1,0:T(8,128)S(1)}, f32[8,128]{1,0:T(8,128)S(1)}, u32[]{:S(2)}, u32[]{:S(2)}) collective-permute-start(f32[8,128]{1,0:T(8,128)S(1)} %fusion.65), channel_id=1, source_target_pairs={{0,128},{32,160},{64,192},{96,224},{128,0},{160,32},{192,64},{224,... | collective-permute-start | bytes 12296 | tf_op jit(solution)/shard_map/ppermute | solution.py:49
  110.0 9.0 %collective-permute-start.15 = (bf16[64,1536]{1,0:T(8,128)(2,1)S(1)}, bf16[64,1536]{1,0:T(8,128)(2,1)S(1)}, u32[]{:S(2)}, u32[]{:S(2)}) collective-permute-start(bf16[64,1536]{1,0:T(8,128)(2,1)S(1)} %get-tuple-element.39), channel_id=1, source_target_pairs={{3,0},{0,1},{1,2},{2,3},{7,4},{4,5},{5,6},{6,7},{11,8},{8,9},{9,10... | collective-permute-start | bytes 589832 | tf_op jit(solution)/shard_map/ppermute | solution.py:26
  110.2 17.0 %collective-permute-start.14 = (bf16[64,1536]{1,0:T(8,128)(2,1)S(1)}, bf16[64,1536]{1,0:T(8,128)(2,1)S(1)}, u32[]{:S(2)}, u32[]{:S(2)}) collective-permute-start(bf16[64,1536]{1,0:T(8,128)(2,1)S(1)} %get-tuple-element.36), channel_id=1, source_target_pairs={{1,0},{2,1},{3,2},{0,3},{5,4},{6,5},{7,6},{4,7},{9,8},{10,9},{11,1... | collective-permute-start | bytes 589832 | tf_op jit(solution)/shard_map/ppermute | solution.py:26
  113.5 9.8 %collective-permute-start.19 = (bf16[128,1536]{1,0:T(8,128)(2,1)S(1)}, bf16[128,1536]{1,0:T(8,128)(2,1)S(1)}, u32[]{:S(2)}, u32[]{:S(2)}) collective-permute-start(bf16[128,1536]{1,0:T(8,128)(2,1)S(1)} %collective-permute-done.18), channel_id=1, source_target_pairs={{1,0},{2,1},{3,2},{0,3},{5,4},{6,5},{7,6},{4,7},{9,8},{10,9},{11,1... | collective-permute-start | bytes 1179656 | tf_op jit(solution)/shard_map/ppermute | solution.py:26
  113.6 13.4 %collective-permute-start.21 = (bf16[128,1536]{1,0:T(8,128)(2,1)S(1)}, bf16[128,1536]{1,0:T(8,128)(2,1)S(1)}, u32[]{:S(2)}, u32[]{:S(2)}) collective-permute-start(bf16[128,1536]{1,0:T(8,128)(2,1)S(1)} %collective-permute-done.18), channel_id=1, source_target_pairs={{3,0},{0,1},{1,2},{2,3},{7,4},{4,5},{5,6},{6,7},{11,8},{8,9},{9,10... | collective-permute-start | bytes 1179656 | tf_op jit(solution)/shard_map/ppermute | solution.py:26
  123.3 8.1 %collective-permute-start.20 = (bf16[64,1536]{1,0:T(8,128)(2,1)S(1)}, bf16[64,1536]{1,0:T(8,128)(2,1)S(1)}, u32[]{:S(2)}, u32[]{:S(2)}) collective-permute-start(bf16[64,1536]{1,0:T(8,128)(2,1)S(1)} %get-tuple-element.31), channel_id=1, source_target_pairs={{1,0},{2,1},{3,2},{0,3},{5,4},{6,5},{7,6},{4,7},{9,8},{10,9},{11,1... | collective-permute-start | bytes 589832 | tf_op jit(solution)/shard_map/ppermute | solution.py:26
  127.0 7.0 %collective-permute-start.22 = (bf16[64,1536]{1,0:T(8,128)(2,1)S(1)}, bf16[64,1536]{1,0:T(8,128)(2,1)S(1)}, u32[]{:S(2)}, u32[]{:S(2)}) collective-permute-start(bf16[64,1536]{1,0:T(8,128)(2,1)S(1)} %get-tuple-element.32), channel_id=1, source_target_pairs={{3,0},{0,1},{1,2},{2,3},{7,4},{4,5},{5,6},{6,7},{11,8},{8,9},{9,10... | collective-permute-start | bytes 589832 | tf_op jit(solution)/shard_map/ppermute | solution.py:26
  128.6 10.9 %collective-permute-start.17 = (f16[8,16,1536]{2,1,0:T(8,128)(2,1)S(1)}, f16[8,16,1536]{2,1,0:T(8,128)(2,1)S(1)}, u32[]{:S(2)}, u32[]{:S(2)}) collective-permute-start(f16[8,16,1536]{2,1,0:T(8,128)(2,1)S(1)} %fusion.44), channel_id=1, source_target_pairs={{0,16},{16,0},{8,24},{24,8},{1,17},{17,1},{9,25},{25,9},{2,18},{18... | collective-permute-start | bytes 1179656 | tf_op jit(solution)/shard_map/ppermute | solution.py:94
  140.8 10.7 %collective-permute-start.26 = (f16[8,16,1536]{2,1,0:T(8,128)(2,1)S(1)}, f16[8,16,1536]{2,1,0:T(8,128)(2,1)S(1)}, u32[]{:S(2)}, u32[]{:S(2)}) collective-permute-start(f16[8,16,1536]{2,1,0:T(8,128)(2,1)S(1)} %fusion.45), channel_id=1, source_target_pairs={{0,16},{16,0},{8,24},{24,8},{1,17},{17,1},{9,25},{25,9},{2,18},{18... | collective-permute-start | bytes 1179656 | tf_op jit(solution)/shard_map/ppermute | solution.py:94
  143.7 18.1 %all-to-all-start.1 = ((f16[8,16,1536]{2,1,0:T(8,128)(2,1)}), f16[8,16,1536]{2,1,0:T(8,128)(2,1)S(1)}, u32[]{:S(2)}, u32[]{:S(2)}) async-start(f16[8,16,1536]{2,1,0:T(8,128)(2,1)} %fusion.43), calls=%async_computation.1 | async-start | bytes 786432 | tf_op jit(solution)/shard_map/all_to_all | solution.py:97
  161.7 17.0 %all-to-all-start.2 = ((f16[8,16,1536]{2,1,0:T(8,128)(2,1)}), f16[8,16,1536]{2,1,0:T(8,128)(2,1)S(1)}, u32[]{:S(2)}, u32[]{:S(2)}) async-start(f16[8,16,1536]{2,1,0:T(8,128)(2,1)} %fusion.42), calls=%async_computation.2 | async-start | bytes 786432 | tf_op jit(solution)/shard_map/all_to_all | solution.py:97
  (17 other events, 132.8 us)

commit v4 on v3

--- a/solution.py
+++ b/solution.py
@@ -59,9 +59,24 @@
     n, width = tokens.shape[0] // 2, tokens.shape[1]
 
     rows = gather_tokens(tokens)
-    sent = (dot(rows, w_up) * up_gain).astype(f16).reshape(8, 8 * n, -1)
-    got = lax.all_to_all(sent, "dep", 0, 0, tiled=True)
-    summed = jnp.sum(got.astype(f32), axis=0) * (1.0 / up_gain)
+    half, own_lo = w_up.shape[1] // 2, lo == 0
+
+    def up(w):
+        return (dot(rows, w) * up_gain).reshape(2, 4, 8 * n, -1)
+
+    def over_x_lo(x):
+        came = lax.ppermute(jnp.where(own_lo, x[1], x[0]).astype(f16), "dep", x_lo_swap)
+        return jnp.where(own_lo, x[0], x[1]) + came.astype(f32)
+
+    b_sent = up(w_up[:, half:]).astype(f16).transpose(1, 0, 2, 3)
+    b_got = lax.all_to_all(b_sent, "dep", 0, 0, tiled=True, axis_index_groups=[[0, 1, 2, 3], [4, 5, 6, 7]])
+    a_sum = over_x_lo(up(w_up[:, :half]))
+    a_sum = lax.dynamic_slice_in_dim(jnp.concatenate([a_sum, a_sum]), y, 4)
+    a_sent = a_sum.astype(f16)
+    a_got = [from_y(a_sent[j], 4 - j).astype(f32) for j in (1, 2, 3)]
+    b_sum = over_x_lo(jnp.sum(b_got.astype(f32), axis=0))
+    a_sum = a_sum[0] + a_got[0] + a_got[1] + a_got[2]
+    summed = jnp.concatenate([a_sum, b_sum], axis=1) * (1.0 / up_gain)
     activated = jax.nn.gelu(summed + bias_up[None, :], approximate=True)
     peak = jnp.full((8, 128), jnp.max(jnp.abs(activated)))
     q = jnp.clip(activated * scale_factor, -format_limit, format_limit).astype(bf16)
@@ -70,9 +85,8 @@
     q1, q3 = from_y(q, 1), from_y(q, 3)
     p = lax.ppermute(q, "dep", x_lo_swap)
     peak, q1, q3 = lax.optimization_barrier((peak_over(peak, ("row", 1), ("row", 2)), q1, q3))
-    q2 = from_y(q1[:h], 1), from_y(q3[h:], 3)
+    q2 = lax.optimization_barrier((from_y(q1[:h], 1), from_y(q3[h:], 3)))
     p1, p3 = from_y(p, 1), from_y(p, 3)
-    p2 = from_y(p1[:h], 1), from_y(p3[h:], 3)
 
     def down(v0, v1, v2, v3, s):
         return dot(jnp.concatenate([v0[s], v1[s], v2[s.start // h], v3[s]]), w_down) * factor
@@ -102,19 +116,20 @@
 
     q_came = over_core(down(q, q1, q2, q3, other_core))
     q_keep, q_send = near(down(q, q1, q2, q3, own_core), q_came)
-    p2 = after(p2, q_send)
+    p2_low, p2_high, peak = after((p1[:h], p3[h:], peak), q_send)
+    p2 = from_y(p2_low, 1), from_y(p2_high, 3)
     p_came = over_core(down(p, p1, p2, p3, other_core))
     p_total = down(p, p1, p2, p3, own_core)
     q_sum = turned(q_keep, over_x_hi(q_send))
     q_got = over_row(q_sum)
-    peak = peak_over(peak, ("row", 4), ("col", 1))
+    peak = peak_over(peak, ("row", 4))
     p_total, p_came, peak = after((p_total, p_came, peak), q_sum)
     p_keep, p_send = near(p_total, p_came)
     p_came, peak = lax.optimization_barrier((over_x_hi(p_send), peak))
     peak = peak_over(peak, ("dep", 1), ("dep", 2))
     p_sum, peak = after((turned(p_keep, p_came), peak), q_got)
     p_got = over_row(p_sum)
-    peak = peak_over(peak, ("dep", 4), ("col", 2))
+    peak = peak_over(peak, ("dep", 4), ("col", 1), ("col", 2))
     q_out, p_out = finish(q_got), finish(p_got)
     first = lo == 0
     layer_output = jnp.concatenate([jnp.where(first, q_out, p_out), jnp.where(first, p_out, q_out)])

time: 182 us -> 175 us (0.962); the launches traced: 179 us -> 174 us
  waiting for transfers between devices: 84.7 us -> 72.5 us
  other arithmetic: 8.1 us -> 12.1 us
  local copies, waits for them, and re-layouts: 3.03 us -> 4.93 us
    all_to_all x1, waiting for transfers between devices: 36.3 us -> 5.52 us  [local(): lax.all_to_all(b_sent, 'dep', 0, 0, tiled=True, axis_index_groups=[[0, 1,...]
    ppermute x0 -> x2, waiting for transfers between devices: none -> 8.39 us  [over_x_lo(): lax.ppermute(jnp.where(own_lo, x[1], x[0]).astype(f16), 'dep', x_lo_swap)]
    ppermute x8 -> x11, waiting for transfers between devices: 8.67 us -> 16.9 us  [from_y(): lax.ppermute(x, 'dep', [(4 * l + (i + k) % 4, 4 * l + i) for l in range(2...]
    ppermute x8 -> x11, starting transfers between devices: 11.3 us -> 15.5 us  [from_y(): lax.ppermute(x, 'dep', [(4 * l + (i + k) % 4, 4 * l + i) for l in range(2...]
    add x0 -> x3, other arithmetic: none -> 2.68 us  [the longest x2 1.45 us: over_x_lo(): return jnp.where(own_lo, x[0], x[1]) + came.astype(f32)]
    ppermute x8, waiting for transfers between devices: 13.6 us -> 16.1 us  [from_z(): return lax.ppermute(x, 'row', [((i + k) % 8, i) for i in range(8)])]
    ppermute x0 -> x2, starting transfers between devices: none -> 2.12 us  [over_x_lo(): lax.ppermute(jnp.where(own_lo, x[1], x[0]).astype(f16), 'dep', x_lo_swap)]
    dot_general x5 -> x6, matrix products: 14.5 us -> 15 us  [dot(): return jnp.dot(a, b, preferred_element_type=f32)]
  transfers between devices with their start and end apart: 34 -> 39, of which waited for: 23 -> 28; matrix products, arithmetic and copies ran while one was open for 8% -> 12% of each run, Pallas kernels for 0% -> 0%
where the time goes in v4:
time: 175 us; the launch traced here: 174 us
  waiting for transfers between devices  72.5 us (41%)
  starting transfers between devices  67.5 us (39%)
  matrix products  15 us (9%)
  other arithmetic  12.1 us (7%)
  local copies, waits for them, and re-layouts  4.93 us (3%)
  between operations  2.41 us (1%)
    ppermute x11, waiting for transfers between devices, from_y(): lax.ppermute(x, 'dep', [(4 * l + (i + k) % 4, 4 * l + i) for l in range(2...  16.9 us
    ppermute x8, waiting for transfers between devices, from_z(): return lax.ppermute(x, 'row', [((i + k) % 8, i) for i in range(8)])  16.1 us
    ppermute x11, starting transfers between devices, from_y(): lax.ppermute(x, 'dep', [(4 * l + (i + k) % 4, 4 * l + i) for l in range(2...  15.5 us
    dot_general x6, matrix products, dot(): return jnp.dot(a, b, preferred_element_type=f32)  15 us
    ppermute x8, waiting for transfers between devices, peak_over(): lax.ppermute(peak, axis, [(i, i ^ step) for i in range(size)])  13.9 us
    ppermute x8, starting transfers between devices, from_z(): return lax.ppermute(x, 'row', [((i + k) % 8, i) for i in range(8)])  13.8 us
    ppermute x8, starting transfers between devices, peak_over(): lax.ppermute(peak, axis, [(i, i ^ step) for i in range(size)])  10.9 us
    all_to_all x2, starting transfers between devices, over_row(): return lax.all_to_all(x, 'row', 0, 0, tiled=True)  10.9 us
  transfers between devices with their start and end apart: 39, of which 28 were waited for; matrix products, arithmetic and copies ran while one was open for 12% of the time, Pallas kernels for 0%

profile of v4, /device:TPU:32, one launch (start us, length us, event | category | flops | bytes accessed | tf_op | source)
XLA Modules:
  0.0 174.4 jit_solution(14135079946993759167)
XLA Ops:
  0.6 3.1 %collective-permute-start = (bf16[32,1536]{1,0:T(8,128)(2,1)}, bf16[32,1536]{1,0:T(8,128)(2,1)S(1)}, u32[]{:S(2)}, u32[]{:S(2)}) collective-permute-start(bf16[32,1536]{1,0:T(8,128)(2,1)} %param.6), channel_id=1, source_target_pairs={{0,16},{16,0},{8,24},{24,8},{1,17},{17,1},{9,25},{25,9},{2,18},{18... | collective-permute-start | bytes 294920 | tf_op jit(solution)/shard_map/ppermute | solution.py:35
  9.0 4.6 %collective-permute-start.2 = (bf16[64,1536]{1,0:T(8,128)(2,1)S(1)}, bf16[64,1536]{1,0:T(8,128)(2,1)S(1)}, u32[]{:S(2)}, u32[]{:S(2)}) collective-permute-start(bf16[64,1536]{1,0:T(8,128)(2,1)S(1)} %pad_maximum_fusion), channel_id=1, source_target_pairs={{64,0},{96,32},{128,64},{160,96},{192,128},{224,160},{0,192},{32,2... | collective-permute-start | bytes 589832 | tf_op jit(solution)/shard_map/ppermute | solution.py:22
  14.6 12.1 %collective-permute-done.5 = bf16[64,1536]{1,0:T(8,128)(2,1)S(1)} collective-permute-done((bf16[64,1536]{1,0:T(8,128)(2,1)S(1)}, bf16[64,1536]{1,0:T(8,128)(2,1)S(1)}, u32[]{:S(2)}, u32[]{:S(2)}) %collective-permute-start.5) | collective-permute-done | bytes 196640 | tf_op jit(solution)/shard_map/ppermute | solution.py:22
  26.9 4.2 %collective-permute-start.4 = (bf16[32,1536]{1,0:T(8,128)(2,1)S(1)}, bf16[32,1536]{1,0:T(8,128)(2,1)S(1)}, u32[]{:S(2)}, u32[]{:S(2)}) collective-permute-start(bf16[32,1536]{1,0:T(8,128)(2,1)S(1)} %slice.150), channel_id=1, source_target_pairs={{64,0},{96,32},{128,64},{160,96},{192,128},{224,160},{0,192},{32,2... | collective-permute-start | bytes 294920 | tf_op jit(solution)/shard_map/ppermute | solution.py:22
  33.1 3.6 %collective-permute-done.3 = bf16[64,1536]{1,0:T(8,128)(2,1)S(1)} collective-permute-done((bf16[64,1536]{1,0:T(8,128)(2,1)S(1)}, bf16[64,1536]{1,0:T(8,128)(2,1)S(1)}, u32[]{:S(2)}, u32[]{:S(2)}) %collective-permute-start.3) | collective-permute-done | bytes 196640 | tf_op jit(solution)/shard_map/ppermute | solution.py:22
  37.4 3.4 %collective-permute-done.9 = bf16[8,64,1536]{2,1,0:T(8,128)(2,1)S(1)} collective-permute-done((bf16[8,64,1536]{2,1,0:T(8,128)(2,1)S(1)}, bf16[8,64,1536]{2,1,0:T(8,128)(2,1)S(1)}, u32[]{:S(2)}, u32[]{:S(2)}) %collective-permute-start.9) | collective-permute-done | bytes 1572896 | tf_op jit(solution)/shard_map/ppermute | solution.py:41
  41.4 4.4 %fusion.6 = f32[1024,768]{1,0:T(8,128)S(1)} fusion(bf16[1024,1536]{1,0:T(8,128)(2,1)S(1)} %bitcast.80, bf16[1536,1536]{1,0:T(8,128)(2,1)} %param.7), kind=kOutput, calls=%fused_computation.15 | convolution fusion | flops 2416705536 | bytes 8650752 | tf_op jit(solution)/shard_map/dot_general | solution.py:18
  52.5 4.6 %all-to-all-start = ((f16[4,2,128,768]{3,2,1,0:T(8,128)(2,1)}), f16[4,2,128,768]{3,2,1,0:T(8,128)(2,1)S(1)}, u32[]{:S(2)}, u32[]{:S(2)}) async-start(f16[4,2,128,768]{3,2,1,0:T(8,128)(2,1)} %bitcast.75), calls=%async_computation | async-start | bytes 3145728 | tf_op jit(solution)/shard_map/all_to_all | solution.py:72
  58.4 8.4 %collective-permute-done.10 = f16[4,128,768]{2,1,0:T(8,128)(2,1)} collective-permute-done((f16[4,128,768]{2,1,0:T(8,128)(2,1)}, f16[4,128,768]{2,1,0:T(8,128)(2,1)}, u32[]{:S(2)}, u32[]{:S(2)}) %collective-permute-start.10) | collective-permute-done | bytes 786464 | tf_op jit(solution)/shard_map/ppermute | solution.py:68
  69.3 3.0 %collective-permute-start.13 = (f16[128,768]{1,0:T(8,128)(2,1)}, f16[128,768]{1,0:T(8,128)(2,1)}, u32[]{:S(2)}, u32[]{:S(2)}) collective-permute-start(f16[128,768]{1,0:T(8,128)(2,1)} %get-tuple-element.39), channel_id=1, source_target_pairs={{1,0},{2,1},{3,2},{0,3},{5,4},{6,5},{7,6},{4,7},{9,8},{10,9},{11,1... | collective-permute-start | bytes 589832 | tf_op jit(solution)/shard_map/ppermute | solution.py:26
  73.9 5.5 %all-to-all-done = f16[4,2,128,768]{3,2,1,0:T(8,128)(2,1)S(1)} async-done(((f16[4,2,128,768]{3,2,1,0:T(8,128)(2,1)}), f16[4,2,128,768]{3,2,1,0:T(8,128)(2,1)S(1)}, u32[]{:S(2)}, u32[]{:S(2)}) %all-to-all-start) | async-done | bytes 1572896 | tf_op jit(solution)/shard_map/all_to_all | solution.py:72
  83.7 2.7 %collective-permute-done.11 = f16[128,768]{1,0:T(8,128)(2,1)} collective-permute-done((f16[128,768]{1,0:T(8,128)(2,1)S(1)}, f16[128,768]{1,0:T(8,128)(2,1)}, u32[]{:S(2)}, u32[]{:S(2)}) %collective-permute-start.11) | collective-permute-done | bytes 196640 | tf_op jit(solution)/shard_map/ppermute | solution.py:26
  99.0 2.7 %collective-permute-done.17 = bf16[128,1536]{1,0:T(8,128)(2,1)S(1)} collective-permute-done((bf16[128,1536]{1,0:T(8,128)(2,1)S(1)}, bf16[128,1536]{1,0:T(8,128)(2,1)S(1)}, u32[]{:S(2)}, u32[]{:S(2)}) %collective-permute-start.17) | collective-permute-done | bytes 393248 | tf_op jit(solution)/shard_map/ppermute | solution.py:26
  106.2 3.0 %collective-permute-start.24 = (bf16[128,1536]{1,0:T(8,128)(2,1)S(1)}, bf16[128,1536]{1,0:T(8,128)(2,1)S(1)}, u32[]{:S(2)}, u32[]{:S(2)}) collective-permute-start(bf16[128,1536]{1,0:T(8,128)(2,1)S(1)} %collective-permute-done.23), channel_id=1, source_target_pairs={{1,0},{2,1},{3,2},{0,3},{5,4},{6,5},{7,6},{4,7},{9,8},{10,9},{11,1... | collective-permute-start | bytes 1179656 | tf_op jit(solution)/shard_map/ppermute | solution.py:26
  112.3 3.9 %fusion = f16[256,1536]{1,0:T(8,128)(2,1)S(1)} fusion(bf16[1536,1536]{1,0:T(8,128)(2,1)} %param.9, bf16[64,1536]{1,0:T(8,128)(2,1)S(1)} %get-tuple-element.50, bf16[64,1536]{1,0:T(8,128)(2,1)S(1)} %collective-permute-done.20, bf16[64,1536]{1,0:T(8,128)(2,1)S(1)} %get-tuple-element.51, bf16[64,1536]{1,0:T(8,128)(2,1)S(1)} %get-tuple-element.48, f32[]{:T(128)S(6)} %div.18), kind=kOutput, calls=%fused_computation.9 | convolution fusion | flops 1211891712 | bytes 6291460 | tf_op jit(solution)/shard_map/dot_general | solution.py:18
  122.9 2.8 %collective-permute-start.22 = (f16[8,16,1536]{2,1,0:T(8,128)(2,1)S(1)}, f16[8,16,1536]{2,1,0:T(8,128)(2,1)S(1)}, u32[]{:S(2)}, u32[]{:S(2)}) collective-permute-start(f16[8,16,1536]{2,1,0:T(8,128)(2,1)S(1)} %fusion.56), channel_id=1, source_target_pairs={{0,16},{16,0},{8,24},{24,8},{1,17},{17,1},{9,25},{25,9},{2,18},{18... | collective-permute-start | bytes 1179656 | tf_op jit(solution)/shard_map/ppermute | solution.py:108
  125.8 2.8 %collective-permute-start.26 = (bf16[64,1536]{1,0:T(8,128)(2,1)S(1)}, bf16[64,1536]{1,0:T(8,128)(2,1)S(1)}, u32[]{:S(2)}, u32[]{:S(2)}) collective-permute-start(bf16[64,1536]{1,0:T(8,128)(2,1)S(1)} %get-tuple-element.22), channel_id=1, source_target_pairs={{1,0},{2,1},{3,2},{0,3},{5,4},{6,5},{7,6},{4,7},{9,8},{10,9},{11,1... | collective-permute-start | bytes 589832 | tf_op jit(solution)/shard_map/ppermute | solution.py:26
  136.4 2.8 %collective-permute-start.30 = (f16[8,16,1536]{2,1,0:T(8,128)(2,1)S(1)}, f16[8,16,1536]{2,1,0:T(8,128)(2,1)S(1)}, u32[]{:S(2)}, u32[]{:S(2)}) collective-permute-start(f16[8,16,1536]{2,1,0:T(8,128)(2,1)S(1)} %fusion.57), channel_id=1, source_target_pairs={{0,16},{16,0},{8,24},{24,8},{1,17},{17,1},{9,25},{25,9},{2,18},{18... | collective-permute-start | bytes 1179656 | tf_op jit(solution)/shard_map/ppermute | solution.py:108
  139.2 5.5 %all-to-all-start.1 = ((f16[8,16,1536]{2,1,0:T(8,128)(2,1)}), f16[8,16,1536]{2,1,0:T(8,128)(2,1)S(1)}, u32[]{:S(2)}, u32[]{:S(2)}) async-start(f16[8,16,1536]{2,1,0:T(8,128)(2,1)} %fusion.55), calls=%async_computation.1 | async-start | bytes 786432 | tf_op jit(solution)/shard_map/all_to_all | solution.py:111
  144.7 3.0 %collective-permute-done.30 = f16[8,16,1536]{2,1,0:T(8,128)(2,1)S(1)} collective-permute-done((f16[8,16,1536]{2,1,0:T(8,128)(2,1)S(1)}, f16[8,16,1536]{2,1,0:T(8,128)(2,1)S(1)}, u32[]{:S(2)}, u32[]{:S(2)}) %collective-permute-start.30) | collective-permute-done | bytes 393248 | tf_op jit(solution)/shard_map/ppermute | solution.py:108
  148.4 3.0 %collective-permute-done.31 = f32[8,128]{1,0:T(8,128)S(1)} collective-permute-done((f32[8,128]{1,0:T(8,128)S(1)}, f32[8,128]{1,0:T(8,128)S(1)}, u32[]{:S(2)}, u32[]{:S(2)}) %collective-permute-start.31) | collective-permute-done | bytes 4128 | tf_op jit(solution)/shard_map/ppermute | solution.py:49
  156.5 5.4 %all-to-all-start.2 = ((f16[8,16,1536]{2,1,0:T(8,128)(2,1)}), f16[8,16,1536]{2,1,0:T(8,128)(2,1)S(1)}, u32[]{:S(2)}, u32[]{:S(2)}) async-start(f16[8,16,1536]{2,1,0:T(8,128)(2,1)} %fusion.54), calls=%async_computation.2 | async-start | bytes 786432 | tf_op jit(solution)/shard_map/all_to_all | solution.py:111
  162.5 3.1 %collective-permute-done.33 = f32[8,128]{1,0:T(8,128)S(1)} collective-permute-done((f32[8,128]{1,0:T(8,128)S(1)}, f32[8,128]{1,0:T(8,128)S(1)}, u32[]{:S(2)}, u32[]{:S(2)}) %collective-permute-start.33) | collective-permute-done | bytes 4128 | tf_op jit(solution)/shard_map/ppermute | solution.py:49
  166.7 2.7 %collective-permute-start.35 = (f32[8,128]{1,0:T(8,128)S(1)}, f32[8,128]{1,0:T(8,128)S(1)}, u32[]{:S(2)}, u32[]{:S(2)}) collective-permute-start(f32[8,128]{1,0:T(8,128)S(1)} %max.37), channel_id=1, source_target_pairs={{0,16},{8,24},{16,0},{24,8},{1,17},{9,25},{17,1},{25,9},{2,18},{10... | collective-permute-start | bytes 12296 | tf_op jit(solution)/shard_map/ppermute | solution.py:49
  (130 shorter events, 71.8 us)
Async XLA Ops:
  7.1 24.0 %collective-permute-start.1 = (bf16[64,1536]{1,0:T(8,128)(2,1)S(1)}, bf16[64,1536]{1,0:T(8,128)(2,1)S(1)}, u32[]{:S(2)}, u32[]{:S(2)}) collective-permute-start(bf16[64,1536]{1,0:T(8,128)(2,1)S(1)} %pad_maximum_fusion), channel_id=1, source_target_pairs={{32,0},{64,32},{96,64},{128,96},{160,128},{192,160},{224,192},{0,2... | collective-permute-start | bytes 589832 | tf_op jit(solution)/shard_map/ppermute | solution.py:22
  9.0 17.8 %collective-permute-start.2 = (bf16[64,1536]{1,0:T(8,128)(2,1)S(1)}, bf16[64,1536]{1,0:T(8,128)(2,1)S(1)}, u32[]{:S(2)}, u32[]{:S(2)}) collective-permute-start(bf16[64,1536]{1,0:T(8,128)(2,1)S(1)} %pad_maximum_fusion), channel_id=1, source_target_pairs={{64,0},{96,32},{128,64},{160,96},{192,128},{224,160},{0,192},{32,2... | collective-permute-start | bytes 589832 | tf_op jit(solution)/shard_map/ppermute | solution.py:22
  13.6 13.2 %collective-permute-start.5 = (bf16[64,1536]{1,0:T(8,128)(2,1)S(1)}, bf16[64,1536]{1,0:T(8,128)(2,1)S(1)}, u32[]{:S(2)}, u32[]{:S(2)}) collective-permute-start(bf16[64,1536]{1,0:T(8,128)(2,1)S(1)} %pad_maximum_fusion), channel_id=1, source_target_pairs={{192,0},{224,32},{0,64},{32,96},{64,128},{96,160},{128,192},{160,2... | collective-permute-start | bytes 589832 | tf_op jit(solution)/shard_map/ppermute | solution.py:22
  13.6 23.6 %collective-permute-start.8 = (bf16[64,1536]{1,0:T(8,128)(2,1)S(1)}, bf16[64,1536]{1,0:T(8,128)(2,1)S(1)}, u32[]{:S(2)}, u32[]{:S(2)}) collective-permute-start(bf16[64,1536]{1,0:T(8,128)(2,1)S(1)} %pad_maximum_fusion), channel_id=1, source_target_pairs={{224,0},{0,32},{32,64},{64,96},{96,128},{128,160},{160,192},{192,2... | collective-permute-start | bytes 589832 | tf_op jit(solution)/shard_map/ppermute | solution.py:22
  26.8 10.0 %collective-permute-start.6 = (bf16[32,1536]{1,0:T(8,128)(2,1)S(1)}, bf16[32,1536]{1,0:T(8,128)(2,1)S(1)}, u32[]{:S(2)}, u32[]{:S(2)}) collective-permute-start(bf16[32,1536]{1,0:T(8,128)(2,1)S(1)} %slice.151), channel_id=1, source_target_pairs={{192,0},{224,32},{0,64},{32,96},{64,128},{96,160},{128,192},{160,2... | collective-permute-start | bytes 294920 | tf_op jit(solution)/shard_map/ppermute | solution.py:22
  26.9 9.9 %collective-permute-start.4 = (bf16[32,1536]{1,0:T(8,128)(2,1)S(1)}, bf16[32,1536]{1,0:T(8,128)(2,1)S(1)}, u32[]{:S(2)}, u32[]{:S(2)}) collective-permute-start(bf16[32,1536]{1,0:T(8,128)(2,1)S(1)} %slice.150), channel_id=1, source_target_pairs={{64,0},{96,32},{128,64},{160,96},{192,128},{224,160},{0,192},{32,2... | collective-permute-start | bytes 294920 | tf_op jit(solution)/shard_map/ppermute | solution.py:22
  46.9 19.9 %collective-permute-start.10 = (f16[4,128,768]{2,1,0:T(8,128)(2,1)}, f16[4,128,768]{2,1,0:T(8,128)(2,1)}, u32[]{:S(2)}, u32[]{:S(2)}) collective-permute-start(f16[4,128,768]{2,1,0:T(8,128)(2,1)} %bitcast.13), channel_id=1, source_target_pairs={{0,4},{1,5},{2,6},{3,7},{4,0},{5,1},{6,2},{7,3},{8,12},{9,13},{10,... | collective-permute-start | bytes 2359304 | tf_op jit(solution)/shard_map/ppermute | solution.py:68
  52.5 26.9 %all-to-all-start = ((f16[4,2,128,768]{3,2,1,0:T(8,128)(2,1)}), f16[4,2,128,768]{3,2,1,0:T(8,128)(2,1)S(1)}, u32[]{:S(2)}, u32[]{:S(2)}) async-start(f16[4,2,128,768]{3,2,1,0:T(8,128)(2,1)} %bitcast.75), calls=%async_computation | async-start | bytes 3145728 | tf_op jit(solution)/shard_map/all_to_all | solution.py:72
  69.3 12.9 %collective-permute-start.13 = (f16[128,768]{1,0:T(8,128)(2,1)}, f16[128,768]{1,0:T(8,128)(2,1)}, u32[]{:S(2)}, u32[]{:S(2)}) collective-permute-start(f16[128,768]{1,0:T(8,128)(2,1)} %get-tuple-element.39), channel_id=1, source_target_pairs={{1,0},{2,1},{3,2},{0,3},{5,4},{6,5},{7,6},{4,7},{9,8},{10,9},{11,1... | collective-permute-start | bytes 589832 | tf_op jit(solution)/shard_map/ppermute | solution.py:26
  72.3 11.4 %collective-permute-start.12 = (f16[128,768]{1,0:T(8,128)(2,1)S(1)}, f16[128,768]{1,0:T(8,128)(2,1)}, u32[]{:S(2)}, u32[]{:S(2)}) collective-permute-start(f16[128,768]{1,0:T(8,128)(2,1)S(1)} %get-tuple-element.40), channel_id=1, source_target_pairs={{2,0},{3,1},{0,2},{1,3},{6,4},{7,5},{4,6},{5,7},{10,8},{11,9},{8,1... | collective-permute-start | bytes 589832 | tf_op jit(solution)/shard_map/ppermute | solution.py:26
  72.9 13.5 %collective-permute-start.11 = (f16[128,768]{1,0:T(8,128)(2,1)S(1)}, f16[128,768]{1,0:T(8,128)(2,1)}, u32[]{:S(2)}, u32[]{:S(2)}) collective-permute-start(f16[128,768]{1,0:T(8,128)(2,1)S(1)} %get-tuple-element.38), channel_id=1, source_target_pairs={{3,0},{0,1},{1,2},{2,3},{7,4},{4,5},{5,6},{6,7},{11,8},{8,9},{9,10... | collective-permute-start | bytes 589832 | tf_op jit(solution)/shard_map/ppermute | solution.py:26
  79.7 7.9 %collective-permute-start.14 = (f16[128,768]{1,0:T(8,128)(2,1)S(1)}, f16[128,768]{1,0:T(8,128)(2,1)S(1)}, u32[]{:S(2)}, u32[]{:S(2)}) collective-permute-start(f16[128,768]{1,0:T(8,128)(2,1)S(1)} %fusion.61), channel_id=1, source_target_pairs={{0,4},{1,5},{2,6},{3,7},{4,0},{5,1},{6,2},{7,3},{8,12},{9,13},{10,... | collective-permute-start | bytes 589832 | tf_op jit(solution)/shard_map/ppermute | solution.py:68
  90.9 10.8 %collective-permute-start.17 = (bf16[128,1536]{1,0:T(8,128)(2,1)S(1)}, bf16[128,1536]{1,0:T(8,128)(2,1)S(1)}, u32[]{:S(2)}, u32[]{:S(2)}) collective-permute-start(bf16[128,1536]{1,0:T(8,128)(2,1)S(1)} %get-tuple-element.36), channel_id=1, source_target_pairs={{1,0},{2,1},{3,2},{0,3},{5,4},{6,5},{7,6},{4,7},{9,8},{10,9},{11,1... | collective-permute-start | bytes 1179656 | tf_op jit(solution)/shard_map/ppermute | solution.py:26
  92.1 10.8 %collective-permute-start.18 = (bf16[128,1536]{1,0:T(8,128)(2,1)S(1)}, bf16[128,1536]{1,0:T(8,128)(2,1)S(1)}, u32[]{:S(2)}, u32[]{:S(2)}) collective-permute-start(bf16[128,1536]{1,0:T(8,128)(2,1)S(1)} %get-tuple-element.36), channel_id=1, source_target_pairs={{3,0},{0,1},{1,2},{2,3},{7,4},{4,5},{5,6},{6,7},{11,8},{8,9},{9,10... | collective-permute-start | bytes 1179656 | tf_op jit(solution)/shard_map/ppermute | solution.py:26
  95.9 10.0 %collective-permute-start.23 = (bf16[128,1536]{1,0:T(8,128)(2,1)S(1)}, bf16[128,1536]{1,0:T(8,128)(2,1)S(1)}, u32[]{:S(2)}, u32[]{:S(2)}) collective-permute-start(bf16[128,1536]{1,0:T(8,128)(2,1)S(1)} %get-tuple-element.36), channel_id=1, source_target_pairs={{0,4},{1,5},{2,6},{3,7},{4,0},{5,1},{6,2},{7,3},{8,12},{9,13},{10,... | collective-permute-start | bytes 1179656 | tf_op jit(solution)/shard_map/ppermute | solution.py:86
  103.3 9.0 %collective-permute-start.20 = (bf16[64,1536]{1,0:T(8,128)(2,1)S(1)}, bf16[64,1536]{1,0:T(8,128)(2,1)S(1)}, u32[]{:S(2)}, u32[]{:S(2)}) collective-permute-start(bf16[64,1536]{1,0:T(8,128)(2,1)S(1)} %get-tuple-element.50), channel_id=1, source_target_pairs={{3,0},{0,1},{1,2},{2,3},{7,4},{4,5},{5,6},{6,7},{11,8},{8,9},{9,10... | collective-permute-start | bytes 589832 | tf_op jit(solution)/shard_map/ppermute | solution.py:26
  105.9 12.3 %collective-permute-start.25 = (bf16[128,1536]{1,0:T(8,128)(2,1)S(1)}, bf16[128,1536]{1,0:T(8,128)(2,1)S(1)}, u32[]{:S(2)}, u32[]{:S(2)}) collective-permute-start(bf16[128,1536]{1,0:T(8,128)(2,1)S(1)} %collective-permute-done.23), channel_id=1, source_target_pairs={{3,0},{0,1},{1,2},{2,3},{7,4},{4,5},{5,6},{6,7},{11,8},{8,9},{9,10... | collective-permute-start | bytes 1179656 | tf_op jit(solution)/shard_map/ppermute | solution.py:26
  106.2 12.1 %collective-permute-start.24 = (bf16[128,1536]{1,0:T(8,128)(2,1)S(1)}, bf16[128,1536]{1,0:T(8,128)(2,1)S(1)}, u32[]{:S(2)}, u32[]{:S(2)}) collective-permute-start(bf16[128,1536]{1,0:T(8,128)(2,1)S(1)} %collective-permute-done.23), channel_id=1, source_target_pairs={{1,0},{2,1},{3,2},{0,3},{5,4},{6,5},{7,6},{4,7},{9,8},{10,9},{11,1... | collective-permute-start | bytes 1179656 | tf_op jit(solution)/shard_map/ppermute | solution.py:26
  120.0 8.7 %collective-permute-start.27 = (bf16[64,1536]{1,0:T(8,128)(2,1)S(1)}, bf16[64,1536]{1,0:T(8,128)(2,1)S(1)}, u32[]{:S(2)}, u32[]{:S(2)}) collective-permute-start(bf16[64,1536]{1,0:T(8,128)(2,1)S(1)} %get-tuple-element.23), channel_id=1, source_target_pairs={{3,0},{0,1},{1,2},{2,3},{7,4},{4,5},{5,6},{6,7},{11,8},{8,9},{9,10... | collective-permute-start | bytes 589832 | tf_op jit(solution)/shard_map/ppermute | solution.py:26
  120.6 8.0 %collective-permute-start.29 = (f32[8,128]{1,0:T(8,128)S(1)}, f32[8,128]{1,0:T(8,128)S(1)}, u32[]{:S(2)}, u32[]{:S(2)}) collective-permute-start(f32[8,128]{1,0:T(8,128)S(1)} %fusion.83), channel_id=1, source_target_pairs={{0,128},{32,160},{64,192},{96,224},{128,0},{160,32},{192,64},{224,... | collective-permute-start | bytes 12296 | tf_op jit(solution)/shard_map/ppermute | solution.py:49
  122.9 12.2 %collective-permute-start.22 = (f16[8,16,1536]{2,1,0:T(8,128)(2,1)S(1)}, f16[8,16,1536]{2,1,0:T(8,128)(2,1)S(1)}, u32[]{:S(2)}, u32[]{:S(2)}) collective-permute-start(f16[8,16,1536]{2,1,0:T(8,128)(2,1)S(1)} %fusion.56), channel_id=1, source_target_pairs={{0,16},{16,0},{8,24},{24,8},{1,17},{17,1},{9,25},{25,9},{2,18},{18... | collective-permute-start | bytes 1179656 | tf_op jit(solution)/shard_map/ppermute | solution.py:108
  136.4 11.3 %collective-permute-start.30 = (f16[8,16,1536]{2,1,0:T(8,128)(2,1)S(1)}, f16[8,16,1536]{2,1,0:T(8,128)(2,1)S(1)}, u32[]{:S(2)}, u32[]{:S(2)}) collective-permute-start(f16[8,16,1536]{2,1,0:T(8,128)(2,1)S(1)} %fusion.57), channel_id=1, source_target_pairs={{0,16},{16,0},{8,24},{24,8},{1,17},{17,1},{9,25},{25,9},{2,18},{18... | collective-permute-start | bytes 1179656 | tf_op jit(solution)/shard_map/ppermute | solution.py:108
  139.2 17.3 %all-to-all-start.1 = ((f16[8,16,1536]{2,1,0:T(8,128)(2,1)}), f16[8,16,1536]{2,1,0:T(8,128)(2,1)S(1)}, u32[]{:S(2)}, u32[]{:S(2)}) async-start(f16[8,16,1536]{2,1,0:T(8,128)(2,1)} %fusion.55), calls=%async_computation.1 | async-start | bytes 786432 | tf_op jit(solution)/shard_map/all_to_all | solution.py:111
  156.5 17.1 %all-to-all-start.2 = ((f16[8,16,1536]{2,1,0:T(8,128)(2,1)}), f16[8,16,1536]{2,1,0:T(8,128)(2,1)S(1)}, u32[]{:S(2)}, u32[]{:S(2)}) async-start(f16[8,16,1536]{2,1,0:T(8,128)(2,1)} %fusion.54), calls=%async_computation.2 | async-start | bytes 786432 | tf_op jit(solution)/shard_map/all_to_all | solution.py:111
  (22 other events, 136.0 us)

commit v5 on v4

--- a/solution.py
+++ b/solution.py
@@ -40,7 +40,7 @@
     mine = jnp.stack([own, z1, z2, z3, z4, z5, z6, z7])
     both = jnp.stack([mine, lax.ppermute(mine, "col", core_swap)])
     both = both.reshape(2, 4, 2, 2, 2 * n, width)
-    return both.transpose(3, 1, 0, 2, 4, 5).reshape(64 * n, width)
+    return both.transpose(1, 3, 0, 2, 4, 5).reshape(64 * n, width)
 
 
 def peak_over(peak, *steps):
@@ -62,13 +62,14 @@
     half, own_lo = w_up.shape[1] // 2, lo == 0
 
     def up(w):
-        return (dot(rows, w) * up_gain).reshape(2, 4, 8 * n, -1)
+        return (dot(rows, w) * up_gain).reshape(4, 2, 8 * n, -1)
 
     def over_x_lo(x):
-        came = lax.ppermute(jnp.where(own_lo, x[1], x[0]).astype(f16), "dep", x_lo_swap)
-        return jnp.where(own_lo, x[0], x[1]) + came.astype(f32)
+        x0, x1 = x[..., 0, :, :], x[..., 1, :, :]
+        came = lax.ppermute(jnp.where(own_lo, x1, x0).astype(f16), "dep", x_lo_swap)
+        return jnp.where(own_lo, x0, x1) + came.astype(f32)
 
-    b_sent = up(w_up[:, half:]).astype(f16).transpose(1, 0, 2, 3)
+    b_sent = up(w_up[:, half:]).astype(f16)
     b_got = lax.all_to_all(b_sent, "dep", 0, 0, tiled=True, axis_index_groups=[[0, 1, 2, 3], [4, 5, 6, 7]])
     a_sum = over_x_lo(up(w_up[:, :half]))
     a_sum = lax.dynamic_slice_in_dim(jnp.concatenate([a_sum, a_sum]), y, 4)

time: 175 us -> 174 us (level)
  local copies, waits for them, and re-layouts: 4.93 us -> 2.73 us
    ppermute x11, waiting for transfers between devices: 16.9 us -> 14.8 us  [from_y(): lax.ppermute(x, 'dep', [(4 * l + (i + k) % 4, 4 * l + i) for l in range(2...]
  transfers between devices with their start and end apart: 39 -> 39, of which waited for: 28 -> 29; matrix products, arithmetic and copies ran while one was open for 12% -> 12% of each run, Pallas kernels for 0% -> 0%
where the time goes in v5:
time: 174 us; the launch traced here: 173 us
  waiting for transfers between devices  71.4 us (41%)
  starting transfers between devices  68 us (39%)
  matrix products  16.1 us (9%)
  other arithmetic  12.5 us (7%)
  local copies, waits for them, and re-layouts  2.73 us (2%)
  between operations  2.43 us (1%)
    ppermute x8, waiting for transfers between devices, from_z(): return lax.ppermute(x, 'row', [((i + k) % 8, i) for i in range(8)])  16.1 us
    dot_general x6, matrix products, dot(): return jnp.dot(a, b, preferred_element_type=f32)  16.1 us
    ppermute x11, starting transfers between devices, from_y(): lax.ppermute(x, 'dep', [(4 * l + (i + k) % 4, 4 * l + i) for l in range(2...  15.4 us
    ppermute x11, waiting for transfers between devices, from_y(): lax.ppermute(x, 'dep', [(4 * l + (i + k) % 4, 4 * l + i) for l in range(2...  14.8 us
    ppermute x8, starting transfers between devices, from_z(): return lax.ppermute(x, 'row', [((i + k) % 8, i) for i in range(8)])  13.8 us
    ppermute x8, waiting for transfers between devices, peak_over(): lax.ppermute(peak, axis, [(i, i ^ step) for i in range(size)])  13.5 us
    ppermute x8, starting transfers between devices, peak_over(): lax.ppermute(peak, axis, [(i, i ^ step) for i in range(size)])  11.3 us
    all_to_all x2, starting transfers between devices, over_row(): return lax.all_to_all(x, 'row', 0, 0, tiled=True)  10.9 us
  transfers between devices with their start and end apart: 39, of which 29 were waited for; matrix products, arithmetic and copies ran while one was open for 12% of the time, Pallas kernels for 0%

profile of v5, /device:TPU:32, one launch (start us, length us, event | category | flops | bytes accessed | tf_op | source)
XLA Modules:
  0.0 173.2 jit_solution(10619777652679563156)
XLA Ops:
  0.6 3.1 %collective-permute-start = (bf16[32,1536]{1,0:T(8,128)(2,1)}, bf16[32,1536]{1,0:T(8,128)(2,1)S(1)}, u32[]{:S(2)}, u32[]{:S(2)}) collective-permute-start(bf16[32,1536]{1,0:T(8,128)(2,1)} %param.6), channel_id=1, source_target_pairs={{0,16},{16,0},{8,24},{24,8},{1,17},{17,1},{9,25},{25,9},{2,18},{18... | collective-permute-start | bytes 294920 | tf_op jit(solution)/shard_map/ppermute | solution.py:35
  9.0 4.6 %collective-permute-start.2 = (bf16[64,1536]{1,0:T(8,128)(2,1)S(1)}, bf16[64,1536]{1,0:T(8,128)(2,1)S(1)}, u32[]{:S(2)}, u32[]{:S(2)}) collective-permute-start(bf16[64,1536]{1,0:T(8,128)(2,1)S(1)} %pad_maximum_fusion), channel_id=1, source_target_pairs={{64,0},{96,32},{128,64},{160,96},{192,128},{224,160},{0,192},{32,2... | collective-permute-start | bytes 589832 | tf_op jit(solution)/shard_map/ppermute | solution.py:22
  14.6 12.1 %collective-permute-done.5 = bf16[64,1536]{1,0:T(8,128)(2,1)S(1)} collective-permute-done((bf16[64,1536]{1,0:T(8,128)(2,1)S(1)}, bf16[64,1536]{1,0:T(8,128)(2,1)S(1)}, u32[]{:S(2)}, u32[]{:S(2)}) %collective-permute-start.5) | collective-permute-done | bytes 196640 | tf_op jit(solution)/shard_map/ppermute | solution.py:22
  26.9 4.2 %collective-permute-start.4 = (bf16[32,1536]{1,0:T(8,128)(2,1)S(1)}, bf16[32,1536]{1,0:T(8,128)(2,1)S(1)}, u32[]{:S(2)}, u32[]{:S(2)}) collective-permute-start(bf16[32,1536]{1,0:T(8,128)(2,1)S(1)} %slice.144), channel_id=1, source_target_pairs={{64,0},{96,32},{128,64},{160,96},{192,128},{224,160},{0,192},{32,2... | collective-permute-start | bytes 294920 | tf_op jit(solution)/shard_map/ppermute | solution.py:22
  33.1 3.6 %collective-permute-done.3 = bf16[64,1536]{1,0:T(8,128)(2,1)S(1)} collective-permute-done((bf16[64,1536]{1,0:T(8,128)(2,1)S(1)}, bf16[64,1536]{1,0:T(8,128)(2,1)S(1)}, u32[]{:S(2)}, u32[]{:S(2)}) %collective-permute-start.3) | collective-permute-done | bytes 196640 | tf_op jit(solution)/shard_map/ppermute | solution.py:22
  37.4 3.4 %collective-permute-done.9 = bf16[8,64,1536]{2,1,0:T(8,128)(2,1)S(1)} collective-permute-done((bf16[8,64,1536]{2,1,0:T(8,128)(2,1)S(1)}, bf16[8,64,1536]{2,1,0:T(8,128)(2,1)S(1)}, u32[]{:S(2)}, u32[]{:S(2)}) %collective-permute-start.9) | collective-permute-done | bytes 1572896 | tf_op jit(solution)/shard_map/ppermute | solution.py:41
  41.4 4.4 %fusion.6 = f32[1024,768]{1,0:T(8,128)S(1)} fusion(bf16[1024,1536]{1,0:T(8,128)(2,1)S(1)} %bitcast.97, bf16[1536,1536]{1,0:T(8,128)(2,1)} %param.7), kind=kOutput, calls=%fused_computation.15 | convolution fusion | flops 2416705536 | bytes 8650752 | tf_op jit(solution)/shard_map/dot_general | solution.py:18
  48.4 3.7 %multiply_convert_fusion = f16[1024,768]{1,0:T(8,128)(2,1)} fusion(bf16[1024,1536]{1,0:T(8,128)(2,1)S(1)} %bitcast.98, bf16[1536,1536]{1,0:T(8,128)(2,1)S(1)} %bitcast.106), kind=kOutput, calls=%fused_computation.4 | convolution fusion | flops 2417491968 | bytes 7077888 | tf_op jit(solution)/shard_map/dot_general | solution.py:18
  52.1 4.6 %all-to-all-start = ((f16[4,2,128,768]{3,2,1,0:T(8,128)(2,1)}), f16[4,2,128,768]{3,2,1,0:T(8,128)(2,1)}, u32[]{:S(2)}, u32[]{:S(2)}) async-start(f16[4,2,128,768]{3,2,1,0:T(8,128)(2,1)} %bitcast.102), calls=%async_computation | async-start | bytes 3145728 | tf_op jit(solution)/shard_map/all_to_all | solution.py:73
  58.0 8.8 %collective-permute-done.10 = f16[4,128,768]{2,1,0:T(8,128)(2,1)} collective-permute-done((f16[4,128,768]{2,1,0:T(8,128)(2,1)}, f16[4,128,768]{2,1,0:T(8,128)(2,1)}, u32[]{:S(2)}, u32[]{:S(2)}) %collective-permute-start.10) | collective-permute-done | bytes 786464 | tf_op jit(solution)/shard_map/ppermute | solution.py:69
  68.7 3.1 %collective-permute-start.13 = (f16[128,768]{1,0:T(8,128)(2,1)S(1)}, f16[128,768]{1,0:T(8,128)(2,1)S(1)}, u32[]{:S(2)}, u32[]{:S(2)}) collective-permute-start(f16[128,768]{1,0:T(8,128)(2,1)S(1)} %get-tuple-element.37), channel_id=1, source_target_pairs={{1,0},{2,1},{3,2},{0,3},{5,4},{6,5},{7,6},{4,7},{9,8},{10,9},{11,1... | collective-permute-start | bytes 589832 | tf_op jit(solution)/shard_map/ppermute | solution.py:26
  73.4 5.6 %all-to-all-done = f16[4,2,128,768]{3,2,1,0:T(8,128)(2,1)} async-done(((f16[4,2,128,768]{3,2,1,0:T(8,128)(2,1)}), f16[4,2,128,768]{3,2,1,0:T(8,128)(2,1)}, u32[]{:S(2)}, u32[]{:S(2)}) %all-to-all-start) | async-done | bytes 1572896 | tf_op jit(solution)/shard_map/all_to_all | solution.py:73
  83.0 3.0 %collective-permute-done.11 = f16[128,768]{1,0:T(8,128)(2,1)S(1)} collective-permute-done((f16[128,768]{1,0:T(8,128)(2,1)S(1)}, f16[128,768]{1,0:T(8,128)(2,1)S(1)}, u32[]{:S(2)}, u32[]{:S(2)}) %collective-permute-start.11) | collective-permute-done | bytes 196640 | tf_op jit(solution)/shard_map/ppermute | solution.py:26
  104.7 3.0 %collective-permute-start.24 = (bf16[128,1536]{1,0:T(8,128)(2,1)S(1)}, bf16[128,1536]{1,0:T(8,128)(2,1)S(1)}, u32[]{:S(2)}, u32[]{:S(2)}) collective-permute-start(bf16[128,1536]{1,0:T(8,128)(2,1)S(1)} %collective-permute-done.23), channel_id=1, source_target_pairs={{1,0},{2,1},{3,2},{0,3},{5,4},{6,5},{7,6},{4,7},{9,8},{10,9},{11,1... | collective-permute-start | bytes 1179656 | tf_op jit(solution)/shard_map/ppermute | solution.py:26
  110.8 3.9 %fusion = f16[256,1536]{1,0:T(8,128)(2,1)S(1)} fusion(bf16[1536,1536]{1,0:T(8,128)(2,1)} %param.9, bf16[64,1536]{1,0:T(8,128)(2,1)S(1)} %get-tuple-element.48, bf16[64,1536]{1,0:T(8,128)(2,1)S(1)} %collective-permute-done.20, bf16[64,1536]{1,0:T(8,128)(2,1)S(1)} %get-tuple-element.49, bf16[64,1536]{1,0:T(8,128)(2,1)S(1)} %get-tuple-element.46, f32[]{:T(128)S(6)} %div.18), kind=kOutput, calls=%fused_computation.9 | convolution fusion | flops 1211891712 | bytes 6291460 | tf_op jit(solution)/shard_map/dot_general | solution.py:18
  121.7 2.8 %collective-permute-start.22 = (f16[8,16,1536]{2,1,0:T(8,128)(2,1)S(1)}, f16[8,16,1536]{2,1,0:T(8,128)(2,1)S(1)}, u32[]{:S(2)}, u32[]{:S(2)}) collective-permute-start(f16[8,16,1536]{2,1,0:T(8,128)(2,1)S(1)} %fusion.59), channel_id=1, source_target_pairs={{0,16},{16,0},{8,24},{24,8},{1,17},{17,1},{9,25},{25,9},{2,18},{18... | collective-permute-start | bytes 1179656 | tf_op jit(solution)/shard_map/ppermute | solution.py:109
  124.6 2.6 %collective-permute-start.26 = (bf16[64,1536]{1,0:T(8,128)(2,1)S(1)}, bf16[64,1536]{1,0:T(8,128)(2,1)S(1)}, u32[]{:S(2)}, u32[]{:S(2)}) collective-permute-start(bf16[64,1536]{1,0:T(8,128)(2,1)S(1)} %get-tuple-element.22), channel_id=1, source_target_pairs={{1,0},{2,1},{3,2},{0,3},{5,4},{6,5},{7,6},{4,7},{9,8},{10,9},{11,1... | collective-permute-start | bytes 589832 | tf_op jit(solution)/shard_map/ppermute | solution.py:26
  135.2 2.8 %collective-permute-start.30 = (f16[8,16,1536]{2,1,0:T(8,128)(2,1)S(1)}, f16[8,16,1536]{2,1,0:T(8,128)(2,1)S(1)}, u32[]{:S(2)}, u32[]{:S(2)}) collective-permute-start(f16[8,16,1536]{2,1,0:T(8,128)(2,1)S(1)} %fusion.60), channel_id=1, source_target_pairs={{0,16},{16,0},{8,24},{24,8},{1,17},{17,1},{9,25},{25,9},{2,18},{18... | collective-permute-start | bytes 1179656 | tf_op jit(solution)/shard_map/ppermute | solution.py:109
  138.0 5.5 %all-to-all-start.1 = ((f16[8,16,1536]{2,1,0:T(8,128)(2,1)}), f16[8,16,1536]{2,1,0:T(8,128)(2,1)S(1)}, u32[]{:S(2)}, u32[]{:S(2)}) async-start(f16[8,16,1536]{2,1,0:T(8,128)(2,1)} %fusion.58), calls=%async_computation.1 | async-start | bytes 786432 | tf_op jit(solution)/shard_map/all_to_all | solution.py:112
  143.5 3.0 %collective-permute-done.30 = f16[8,16,1536]{2,1,0:T(8,128)(2,1)S(1)} collective-permute-done((f16[8,16,1536]{2,1,0:T(8,128)(2,1)S(1)}, f16[8,16,1536]{2,1,0:T(8,128)(2,1)S(1)}, u32[]{:S(2)}, u32[]{:S(2)}) %collective-permute-start.30) | collective-permute-done | bytes 393248 | tf_op jit(solution)/shard_map/ppermute | solution.py:109
  147.1 3.0 %collective-permute-done.31 = f32[8,128]{1,0:T(8,128)S(1)} collective-permute-done((f32[8,128]{1,0:T(8,128)S(1)}, f32[8,128]{1,0:T(8,128)S(1)}, u32[]{:S(2)}, u32[]{:S(2)}) %collective-permute-start.31) | collective-permute-done | bytes 4128 | tf_op jit(solution)/shard_map/ppermute | solution.py:49
  155.3 5.4 %all-to-all-start.2 = ((f16[8,16,1536]{2,1,0:T(8,128)(2,1)}), f16[8,16,1536]{2,1,0:T(8,128)(2,1)S(1)}, u32[]{:S(2)}, u32[]{:S(2)}) async-start(f16[8,16,1536]{2,1,0:T(8,128)(2,1)} %fusion.57), calls=%async_computation.2 | async-start | bytes 786432 | tf_op jit(solution)/shard_map/all_to_all | solution.py:112
  161.2 3.1 %collective-permute-done.33 = f32[8,128]{1,0:T(8,128)S(1)} collective-permute-done((f32[8,128]{1,0:T(8,128)S(1)}, f32[8,128]{1,0:T(8,128)S(1)}, u32[]{:S(2)}, u32[]{:S(2)}) %collective-permute-start.33) | collective-permute-done | bytes 4128 | tf_op jit(solution)/shard_map/ppermute | solution.py:49
  165.5 2.7 %collective-permute-start.35 = (f32[8,128]{1,0:T(8,128)S(1)}, f32[8,128]{1,0:T(8,128)S(1)}, u32[]{:S(2)}, u32[]{:S(2)}) collective-permute-start(f32[8,128]{1,0:T(8,128)S(1)} %max.37), channel_id=1, source_target_pairs={{0,16},{8,24},{16,0},{24,8},{1,17},{9,25},{17,1},{25,9},{2,18},{10... | collective-permute-start | bytes 12296 | tf_op jit(solution)/shard_map/ppermute | solution.py:49
  (129 shorter events, 68.8 us)
Async XLA Ops:
  7.1 24.0 %collective-permute-start.1 = (bf16[64,1536]{1,0:T(8,128)(2,1)S(1)}, bf16[64,1536]{1,0:T(8,128)(2,1)S(1)}, u32[]{:S(2)}, u32[]{:S(2)}) collective-permute-start(bf16[64,1536]{1,0:T(8,128)(2,1)S(1)} %pad_maximum_fusion), channel_id=1, source_target_pairs={{32,0},{64,32},{96,64},{128,96},{160,128},{192,160},{224,192},{0,2... | collective-permute-start | bytes 589832 | tf_op jit(solution)/shard_map/ppermute | solution.py:22
  9.0 17.8 %collective-permute-start.2 = (bf16[64,1536]{1,0:T(8,128)(2,1)S(1)}, bf16[64,1536]{1,0:T(8,128)(2,1)S(1)}, u32[]{:S(2)}, u32[]{:S(2)}) collective-permute-start(bf16[64,1536]{1,0:T(8,128)(2,1)S(1)} %pad_maximum_fusion), channel_id=1, source_target_pairs={{64,0},{96,32},{128,64},{160,96},{192,128},{224,160},{0,192},{32,2... | collective-permute-start | bytes 589832 | tf_op jit(solution)/shard_map/ppermute | solution.py:22
  13.6 13.2 %collective-permute-start.5 = (bf16[64,1536]{1,0:T(8,128)(2,1)S(1)}, bf16[64,1536]{1,0:T(8,128)(2,1)S(1)}, u32[]{:S(2)}, u32[]{:S(2)}) collective-permute-start(bf16[64,1536]{1,0:T(8,128)(2,1)S(1)} %pad_maximum_fusion), channel_id=1, source_target_pairs={{192,0},{224,32},{0,64},{32,96},{64,128},{96,160},{128,192},{160,2... | collective-permute-start | bytes 589832 | tf_op jit(solution)/shard_map/ppermute | solution.py:22
  13.6 23.6 %collective-permute-start.8 = (bf16[64,1536]{1,0:T(8,128)(2,1)S(1)}, bf16[64,1536]{1,0:T(8,128)(2,1)S(1)}, u32[]{:S(2)}, u32[]{:S(2)}) collective-permute-start(bf16[64,1536]{1,0:T(8,128)(2,1)S(1)} %pad_maximum_fusion), channel_id=1, source_target_pairs={{224,0},{0,32},{32,64},{64,96},{96,128},{128,160},{160,192},{192,2... | collective-permute-start | bytes 589832 | tf_op jit(solution)/shard_map/ppermute | solution.py:22
  26.8 10.0 %collective-permute-start.6 = (bf16[32,1536]{1,0:T(8,128)(2,1)S(1)}, bf16[32,1536]{1,0:T(8,128)(2,1)S(1)}, u32[]{:S(2)}, u32[]{:S(2)}) collective-permute-start(bf16[32,1536]{1,0:T(8,128)(2,1)S(1)} %slice.145), channel_id=1, source_target_pairs={{192,0},{224,32},{0,64},{32,96},{64,128},{96,160},{128,192},{160,2... | collective-permute-start | bytes 294920 | tf_op jit(solution)/shard_map/ppermute | solution.py:22
  26.9 9.9 %collective-permute-start.4 = (bf16[32,1536]{1,0:T(8,128)(2,1)S(1)}, bf16[32,1536]{1,0:T(8,128)(2,1)S(1)}, u32[]{:S(2)}, u32[]{:S(2)}) collective-permute-start(bf16[32,1536]{1,0:T(8,128)(2,1)S(1)} %slice.144), channel_id=1, source_target_pairs={{64,0},{96,32},{128,64},{160,96},{192,128},{224,160},{0,192},{32,2... | collective-permute-start | bytes 294920 | tf_op jit(solution)/shard_map/ppermute | solution.py:22
  46.9 19.9 %collective-permute-start.10 = (f16[4,128,768]{2,1,0:T(8,128)(2,1)}, f16[4,128,768]{2,1,0:T(8,128)(2,1)}, u32[]{:S(2)}, u32[]{:S(2)}) collective-permute-start(f16[4,128,768]{2,1,0:T(8,128)(2,1)} %fusion.21), channel_id=1, source_target_pairs={{0,4},{1,5},{2,6},{3,7},{4,0},{5,1},{6,2},{7,3},{8,12},{9,13},{10,... | collective-permute-start | bytes 2359304 | tf_op jit(solution)/shard_map/ppermute | solution.py:69
  52.1 26.9 %all-to-all-start = ((f16[4,2,128,768]{3,2,1,0:T(8,128)(2,1)}), f16[4,2,128,768]{3,2,1,0:T(8,128)(2,1)}, u32[]{:S(2)}, u32[]{:S(2)}) async-start(f16[4,2,128,768]{3,2,1,0:T(8,128)(2,1)} %bitcast.102), calls=%async_computation | async-start | bytes 3145728 | tf_op jit(solution)/shard_map/all_to_all | solution.py:73
  68.7 12.8 %collective-permute-start.13 = (f16[128,768]{1,0:T(8,128)(2,1)S(1)}, f16[128,768]{1,0:T(8,128)(2,1)S(1)}, u32[]{:S(2)}, u32[]{:S(2)}) collective-permute-start(f16[128,768]{1,0:T(8,128)(2,1)S(1)} %get-tuple-element.37), channel_id=1, source_target_pairs={{1,0},{2,1},{3,2},{0,3},{5,4},{6,5},{7,6},{4,7},{9,8},{10,9},{11,1... | collective-permute-start | bytes 589832 | tf_op jit(solution)/shard_map/ppermute | solution.py:26
  71.8 11.3 %collective-permute-start.12 = (f16[128,768]{1,0:T(8,128)(2,1)S(1)}, f16[128,768]{1,0:T(8,128)(2,1)S(1)}, u32[]{:S(2)}, u32[]{:S(2)}) collective-permute-start(f16[128,768]{1,0:T(8,128)(2,1)S(1)} %get-tuple-element.38), channel_id=1, source_target_pairs={{2,0},{3,1},{0,2},{1,3},{6,4},{7,5},{4,6},{5,7},{10,8},{11,9},{8,1... | collective-permute-start | bytes 589832 | tf_op jit(solution)/shard_map/ppermute | solution.py:26
  72.4 13.6 %collective-permute-start.11 = (f16[128,768]{1,0:T(8,128)(2,1)S(1)}, f16[128,768]{1,0:T(8,128)(2,1)S(1)}, u32[]{:S(2)}, u32[]{:S(2)}) collective-permute-start(f16[128,768]{1,0:T(8,128)(2,1)S(1)} %get-tuple-element.36), channel_id=1, source_target_pairs={{3,0},{0,1},{1,2},{2,3},{7,4},{4,5},{5,6},{6,7},{11,8},{8,9},{9,10... | collective-permute-start | bytes 589832 | tf_op jit(solution)/shard_map/ppermute | solution.py:26
  89.8 10.4 %collective-permute-start.17 = (bf16[128,1536]{1,0:T(8,128)(2,1)S(1)}, bf16[128,1536]{1,0:T(8,128)(2,1)S(1)}, u32[]{:S(2)}, u32[]{:S(2)}) collective-permute-start(bf16[128,1536]{1,0:T(8,128)(2,1)S(1)} %get-tuple-element.34), channel_id=1, source_target_pairs={{1,0},{2,1},{3,2},{0,3},{5,4},{6,5},{7,6},{4,7},{9,8},{10,9},{11,1... | collective-permute-start | bytes 1179656 | tf_op jit(solution)/shard_map/ppermute | solution.py:26
  90.9 10.5 %collective-permute-start.18 = (bf16[128,1536]{1,0:T(8,128)(2,1)S(1)}, bf16[128,1536]{1,0:T(8,128)(2,1)S(1)}, u32[]{:S(2)}, u32[]{:S(2)}) collective-permute-start(bf16[128,1536]{1,0:T(8,128)(2,1)S(1)} %get-tuple-element.34), channel_id=1, source_target_pairs={{3,0},{0,1},{1,2},{2,3},{7,4},{4,5},{5,6},{6,7},{11,8},{8,9},{9,10... | collective-permute-start | bytes 1179656 | tf_op jit(solution)/shard_map/ppermute | solution.py:26
  94.8 9.6 %collective-permute-start.23 = (bf16[128,1536]{1,0:T(8,128)(2,1)S(1)}, bf16[128,1536]{1,0:T(8,128)(2,1)S(1)}, u32[]{:S(2)}, u32[]{:S(2)}) collective-permute-start(bf16[128,1536]{1,0:T(8,128)(2,1)S(1)} %get-tuple-element.34), channel_id=1, source_target_pairs={{0,4},{1,5},{2,6},{3,7},{4,0},{5,1},{6,2},{7,3},{8,12},{9,13},{10,... | collective-permute-start | bytes 1179656 | tf_op jit(solution)/shard_map/ppermute | solution.py:87
  101.4 7.8 %collective-permute-start.19 = (bf16[64,1536]{1,0:T(8,128)(2,1)S(1)}, bf16[64,1536]{1,0:T(8,128)(2,1)S(1)}, u32[]{:S(2)}, u32[]{:S(2)}) collective-permute-start(bf16[64,1536]{1,0:T(8,128)(2,1)S(1)} %get-tuple-element.50), channel_id=1, source_target_pairs={{1,0},{2,1},{3,2},{0,3},{5,4},{6,5},{7,6},{4,7},{9,8},{10,9},{11,1... | collective-permute-start | bytes 589832 | tf_op jit(solution)/shard_map/ppermute | solution.py:26
  101.8 8.9 %collective-permute-start.20 = (bf16[64,1536]{1,0:T(8,128)(2,1)S(1)}, bf16[64,1536]{1,0:T(8,128)(2,1)S(1)}, u32[]{:S(2)}, u32[]{:S(2)}) collective-permute-start(bf16[64,1536]{1,0:T(8,128)(2,1)S(1)} %get-tuple-element.48), channel_id=1, source_target_pairs={{3,0},{0,1},{1,2},{2,3},{7,4},{4,5},{5,6},{6,7},{11,8},{8,9},{9,10... | collective-permute-start | bytes 589832 | tf_op jit(solution)/shard_map/ppermute | solution.py:26
  104.5 11.9 %collective-permute-start.25 = (bf16[128,1536]{1,0:T(8,128)(2,1)S(1)}, bf16[128,1536]{1,0:T(8,128)(2,1)S(1)}, u32[]{:S(2)}, u32[]{:S(2)}) collective-permute-start(bf16[128,1536]{1,0:T(8,128)(2,1)S(1)} %collective-permute-done.23), channel_id=1, source_target_pairs={{3,0},{0,1},{1,2},{2,3},{7,4},{4,5},{5,6},{6,7},{11,8},{8,9},{9,10... | collective-permute-start | bytes 1179656 | tf_op jit(solution)/shard_map/ppermute | solution.py:26
  104.7 11.7 %collective-permute-start.24 = (bf16[128,1536]{1,0:T(8,128)(2,1)S(1)}, bf16[128,1536]{1,0:T(8,128)(2,1)S(1)}, u32[]{:S(2)}, u32[]{:S(2)}) collective-permute-start(bf16[128,1536]{1,0:T(8,128)(2,1)S(1)} %collective-permute-done.23), channel_id=1, source_target_pairs={{1,0},{2,1},{3,2},{0,3},{5,4},{6,5},{7,6},{4,7},{9,8},{10,9},{11,1... | collective-permute-start | bytes 1179656 | tf_op jit(solution)/shard_map/ppermute | solution.py:26
  118.7 8.5 %collective-permute-start.27 = (bf16[64,1536]{1,0:T(8,128)(2,1)S(1)}, bf16[64,1536]{1,0:T(8,128)(2,1)S(1)}, u32[]{:S(2)}, u32[]{:S(2)}) collective-permute-start(bf16[64,1536]{1,0:T(8,128)(2,1)S(1)} %get-tuple-element.23), channel_id=1, source_target_pairs={{3,0},{0,1},{1,2},{2,3},{7,4},{4,5},{5,6},{6,7},{11,8},{8,9},{9,10... | collective-permute-start | bytes 589832 | tf_op jit(solution)/shard_map/ppermute | solution.py:26
  119.4 7.8 %collective-permute-start.29 = (f32[8,128]{1,0:T(8,128)S(1)}, f32[8,128]{1,0:T(8,128)S(1)}, u32[]{:S(2)}, u32[]{:S(2)}) collective-permute-start(f32[8,128]{1,0:T(8,128)S(1)} %fusion.86), channel_id=1, source_target_pairs={{0,128},{32,160},{64,192},{96,224},{128,0},{160,32},{192,64},{224,... | collective-permute-start | bytes 12296 | tf_op jit(solution)/shard_map/ppermute | solution.py:49
  121.7 12.2 %collective-permute-start.22 = (f16[8,16,1536]{2,1,0:T(8,128)(2,1)S(1)}, f16[8,16,1536]{2,1,0:T(8,128)(2,1)S(1)}, u32[]{:S(2)}, u32[]{:S(2)}) collective-permute-start(f16[8,16,1536]{2,1,0:T(8,128)(2,1)S(1)} %fusion.59), channel_id=1, source_target_pairs={{0,16},{16,0},{8,24},{24,8},{1,17},{17,1},{9,25},{25,9},{2,18},{18... | collective-permute-start | bytes 1179656 | tf_op jit(solution)/shard_map/ppermute | solution.py:109
  135.2 11.3 %collective-permute-start.30 = (f16[8,16,1536]{2,1,0:T(8,128)(2,1)S(1)}, f16[8,16,1536]{2,1,0:T(8,128)(2,1)S(1)}, u32[]{:S(2)}, u32[]{:S(2)}) collective-permute-start(f16[8,16,1536]{2,1,0:T(8,128)(2,1)S(1)} %fusion.60), channel_id=1, source_target_pairs={{0,16},{16,0},{8,24},{24,8},{1,17},{17,1},{9,25},{25,9},{2,18},{18... | collective-permute-start | bytes 1179656 | tf_op jit(solution)/shard_map/ppermute | solution.py:109
  138.0 17.3 %all-to-all-start.1 = ((f16[8,16,1536]{2,1,0:T(8,128)(2,1)}), f16[8,16,1536]{2,1,0:T(8,128)(2,1)S(1)}, u32[]{:S(2)}, u32[]{:S(2)}) async-start(f16[8,16,1536]{2,1,0:T(8,128)(2,1)} %fusion.58), calls=%async_computation.1 | async-start | bytes 786432 | tf_op jit(solution)/shard_map/all_to_all | solution.py:112
  155.3 17.1 %all-to-all-start.2 = ((f16[8,16,1536]{2,1,0:T(8,128)(2,1)}), f16[8,16,1536]{2,1,0:T(8,128)(2,1)S(1)}, u32[]{:S(2)}, u32[]{:S(2)}) async-start(f16[8,16,1536]{2,1,0:T(8,128)(2,1)} %fusion.57), calls=%async_computation.2 | async-start | bytes 786432 | tf_op jit(solution)/shard_map/all_to_all | solution.py:112
  (22 other events, 132.8 us)

commit v6 on v5

--- a/solution.py
+++ b/solution.py
@@ -89,10 +89,8 @@
     q2 = lax.optimization_barrier((from_y(q1[:h], 1), from_y(q3[h:], 3)))
     p1, p3 = from_y(p, 1), from_y(p, 3)
 
-    def down(v0, v1, v2, v3, s):
-        return dot(jnp.concatenate([v0[s], v1[s], v2[s.start // h], v3[s]]), w_down) * factor
-
-    own_core, other_core = slice(0, h), slice(h, 2 * h)
+    def down(*rows):
+        return dot(jnp.concatenate(rows), w_down) * factor
 
     def over_core(total):
         return lax.ppermute(total.astype(f16), "col", core_swap)
@@ -115,12 +113,14 @@
         mixed = jnp.sum(got.astype(f32), axis=0) * (1.0 / down_gain)
         return (mixed + bias_down[None, :]).astype(bf16)
 
-    q_came = over_core(down(q, q1, q2, q3, other_core))
-    q_keep, q_send = near(down(q, q1, q2, q3, own_core), q_came)
+    q_own = dot(q, w_down) * factor
+    q_came = over_core(jnp.concatenate([q_own[h:], down(q1[h:], q2[1], q3[h:])]))
+    q_near = jnp.concatenate([q_own[:h], down(q1[:h], q2[0], q3[:h])])
+    q_keep, q_send = near(q_near, q_came)
     p2_low, p2_high, peak = after((p1[:h], p3[h:], peak), q_send)
     p2 = from_y(p2_low, 1), from_y(p2_high, 3)
-    p_came = over_core(down(p, p1, p2, p3, other_core))
-    p_total = down(p, p1, p2, p3, own_core)
+    p_came = over_core(down(p[h:], p1[h:], p2[1], p3[h:]))
+    p_total = down(p[:h], p1[:h], p2[0], p3[:h])
     q_sum = turned(q_keep, over_x_hi(q_send))
     q_got = over_row(q_sum)
     peak = peak_over(peak, ("row", 4))

time: 174 us -> 170 us (0.977)
  waiting for transfers between devices: 71.4 us -> 67 us
    ppermute x8, waiting for transfers between devices: 13.5 us -> 11.8 us  [peak_over(): lax.ppermute(peak, axis, [(i, i ^ step) for i in range(size)])]
    dot_general x6 -> x7, matrix products: 16.1 us -> 16.1 us  [dot(): return jnp.dot(a, b, preferred_element_type=f32)]
  transfers between devices with their start and end apart: 39 -> 39, of which waited for: 29 -> 24; matrix products, arithmetic and copies ran while one was open for 12% -> 13% of each run, Pallas kernels for 0% -> 0%
where the time goes in v6:
time: 170 us; the launch traced here: 169 us
  starting transfers between devices  68.1 us (40%)
  waiting for transfers between devices  67 us (39%)
  matrix products  16.1 us (9%)
  other arithmetic  13.1 us (8%)
  local copies, waits for them, and re-layouts  2.71 us (2%)
  between operations  2.49 us (1%)
    dot_general x7, matrix products, dot(): return jnp.dot(a, b, preferred_element_type=f32)  16.1 us
    ppermute x8, waiting for transfers between devices, from_z(): return lax.ppermute(x, 'row', [((i + k) % 8, i) for i in range(8)])  16.1 us
    ppermute x11, starting transfers between devices, from_y(): lax.ppermute(x, 'dep', [(4 * l + (i + k) % 4, 4 * l + i) for l in range(2...  15.5 us
    ppermute x11, waiting for transfers between devices, from_y(): lax.ppermute(x, 'dep', [(4 * l + (i + k) % 4, 4 * l + i) for l in range(2...  15 us
    ppermute x8, starting transfers between devices, from_z(): return lax.ppermute(x, 'row', [((i + k) % 8, i) for i in range(8)])  13.8 us
    ppermute x8, waiting for transfers between devices, peak_over(): lax.ppermute(peak, axis, [(i, i ^ step) for i in range(size)])  11.8 us
    ppermute x8, starting transfers between devices, peak_over(): lax.ppermute(peak, axis, [(i, i ^ step) for i in range(size)])  11.3 us
    all_to_all x2, starting transfers between devices, over_row(): return lax.all_to_all(x, 'row', 0, 0, tiled=True)  11 us
  transfers between devices with their start and end apart: 39, of which 24 were waited for; matrix products, arithmetic and copies ran while one was open for 13% of the time, Pallas kernels for 0%

profile of v6, /device:TPU:32, one launch (start us, length us, event | category | flops | bytes accessed | tf_op | source)
XLA Modules:
  0.0 169.5 jit_solution(10244662808412554471)
XLA Ops:
  0.6 3.1 %collective-permute-start = (bf16[32,1536]{1,0:T(8,128)(2,1)}, bf16[32,1536]{1,0:T(8,128)(2,1)S(1)}, u32[]{:S(2)}, u32[]{:S(2)}) collective-permute-start(bf16[32,1536]{1,0:T(8,128)(2,1)} %param.6), channel_id=1, source_target_pairs={{0,16},{16,0},{8,24},{24,8},{1,17},{17,1},{9,25},{25,9},{2,18},{18... | collective-permute-start | bytes 294920 | tf_op jit(solution)/shard_map/ppermute | solution.py:35
  4.6 2.5 %collective-permute-done = bf16[32,1536]{1,0:T(8,128)(2,1)S(1)} collective-permute-done((bf16[32,1536]{1,0:T(8,128)(2,1)}, bf16[32,1536]{1,0:T(8,128)(2,1)S(1)}, u32[]{:S(2)}, u32[]{:S(2)}) %collective-permute-start) | collective-permute-done | bytes 98336 | tf_op jit(solution)/shard_map/ppermute | solution.py:35
  9.0 4.6 %collective-permute-start.2 = (bf16[64,1536]{1,0:T(8,128)(2,1)S(1)}, bf16[64,1536]{1,0:T(8,128)(2,1)S(1)}, u32[]{:S(2)}, u32[]{:S(2)}) collective-permute-start(bf16[64,1536]{1,0:T(8,128)(2,1)S(1)} %pad_maximum_fusion.1), channel_id=1, source_target_pairs={{64,0},{96,32},{128,64},{160,96},{192,128},{224,160},{0,192},{32,2... | collective-permute-start | bytes 589832 | tf_op jit(solution)/shard_map/ppermute | solution.py:22
  14.6 12.1 %collective-permute-done.5 = bf16[64,1536]{1,0:T(8,128)(2,1)S(1)} collective-permute-done((bf16[64,1536]{1,0:T(8,128)(2,1)S(1)}, bf16[64,1536]{1,0:T(8,128)(2,1)S(1)}, u32[]{:S(2)}, u32[]{:S(2)}) %collective-permute-start.5) | collective-permute-done | bytes 196640 | tf_op jit(solution)/shard_map/ppermute | solution.py:22
  26.9 4.2 %collective-permute-start.4 = (bf16[32,1536]{1,0:T(8,128)(2,1)S(1)}, bf16[32,1536]{1,0:T(8,128)(2,1)S(1)}, u32[]{:S(2)}, u32[]{:S(2)}) collective-permute-start(bf16[32,1536]{1,0:T(8,128)(2,1)S(1)} %slice.145), channel_id=1, source_target_pairs={{64,0},{96,32},{128,64},{160,96},{192,128},{224,160},{0,192},{32,2... | collective-permute-start | bytes 294920 | tf_op jit(solution)/shard_map/ppermute | solution.py:22
  33.1 3.6 %collective-permute-done.3 = bf16[64,1536]{1,0:T(8,128)(2,1)S(1)} collective-permute-done((bf16[64,1536]{1,0:T(8,128)(2,1)S(1)}, bf16[64,1536]{1,0:T(8,128)(2,1)S(1)}, u32[]{:S(2)}, u32[]{:S(2)}) %collective-permute-start.3) | collective-permute-done | bytes 196640 | tf_op jit(solution)/shard_map/ppermute | solution.py:22
  37.4 3.4 %collective-permute-done.9 = bf16[8,64,1536]{2,1,0:T(8,128)(2,1)S(1)} collective-permute-done((bf16[8,64,1536]{2,1,0:T(8,128)(2,1)S(1)}, bf16[8,64,1536]{2,1,0:T(8,128)(2,1)S(1)}, u32[]{:S(2)}, u32[]{:S(2)}) %collective-permute-start.9) | collective-permute-done | bytes 1572896 | tf_op jit(solution)/shard_map/ppermute | solution.py:41
  41.4 4.4 %fusion.6 = f32[1024,768]{1,0:T(8,128)S(1)} fusion(bf16[1024,1536]{1,0:T(8,128)(2,1)S(1)} %bitcast.103, bf16[1536,1536]{1,0:T(8,128)(2,1)} %param.7), kind=kOutput, calls=%fused_computation.16 | convolution fusion | flops 2416705536 | bytes 8650752 | tf_op jit(solution)/shard_map/dot_general | solution.py:18
  48.4 3.7 %multiply_convert_fusion = f16[1024,768]{1,0:T(8,128)(2,1)} fusion(bf16[1024,1536]{1,0:T(8,128)(2,1)S(1)} %bitcast.104, bf16[1536,1536]{1,0:T(8,128)(2,1)S(1)} %bitcast.110), kind=kOutput, calls=%fused_computation.4 | convolution fusion | flops 2417491968 | bytes 7077888 | tf_op jit(solution)/shard_map/dot_general | solution.py:18
  52.1 4.6 %all-to-all-start = ((f16[4,2,128,768]{3,2,1,0:T(8,128)(2,1)}), f16[4,2,128,768]{3,2,1,0:T(8,128)(2,1)}, u32[]{:S(2)}, u32[]{:S(2)}) async-start(f16[4,2,128,768]{3,2,1,0:T(8,128)(2,1)} %bitcast.106), calls=%async_computation | async-start | bytes 3145728 | tf_op jit(solution)/shard_map/all_to_all | solution.py:73
  58.0 8.8 %collective-permute-done.10 = f16[4,128,768]{2,1,0:T(8,128)(2,1)} collective-permute-done((f16[4,128,768]{2,1,0:T(8,128)(2,1)}, f16[4,128,768]{2,1,0:T(8,128)(2,1)}, u32[]{:S(2)}, u32[]{:S(2)}) %collective-permute-start.10) | collective-permute-done | bytes 786464 | tf_op jit(solution)/shard_map/ppermute | solution.py:69
  68.7 3.1 %collective-permute-start.13 = (f16[128,768]{1,0:T(8,128)(2,1)S(1)}, f16[128,768]{1,0:T(8,128)(2,1)S(1)}, u32[]{:S(2)}, u32[]{:S(2)}) collective-permute-start(f16[128,768]{1,0:T(8,128)(2,1)S(1)} %get-tuple-element.39), channel_id=1, source_target_pairs={{1,0},{2,1},{3,2},{0,3},{5,4},{6,5},{7,6},{4,7},{9,8},{10,9},{11,1... | collective-permute-start | bytes 589832 | tf_op jit(solution)/shard_map/ppermute | solution.py:26
  73.4 5.6 %all-to-all-done = f16[4,2,128,768]{3,2,1,0:T(8,128)(2,1)} async-done(((f16[4,2,128,768]{3,2,1,0:T(8,128)(2,1)}), f16[4,2,128,768]{3,2,1,0:T(8,128)(2,1)}, u32[]{:S(2)}, u32[]{:S(2)}) %all-to-all-start) | async-done | bytes 1572896 | tf_op jit(solution)/shard_map/all_to_all | solution.py:73
  83.0 3.0 %collective-permute-done.11 = f16[128,768]{1,0:T(8,128)(2,1)S(1)} collective-permute-done((f16[128,768]{1,0:T(8,128)(2,1)S(1)}, f16[128,768]{1,0:T(8,128)(2,1)S(1)}, u32[]{:S(2)}, u32[]{:S(2)}) %collective-permute-start.11) | collective-permute-done | bytes 196640 | tf_op jit(solution)/shard_map/ppermute | solution.py:26
  95.6 3.1 %convolution_multiply_fusion.4 = f32[128,1536]{1,0:T(8,128)S(1)} fusion(bf16[128,1536]{1,0:T(8,128)(2,1)S(1)} %get-tuple-element.34, bf16[1536,1536]{1,0:T(8,128)(2,1)} %param.9, f32[]{:T(128)S(6)} %div.18), kind=kOutput, calls=%fused_computation.11 | convolution fusion | flops 604176384 | bytes 5898244 | tf_op jit(solution)/shard_map/dot_general | solution.py:18
  105.0 2.8 %collective-permute-start.24 = (bf16[128,1536]{1,0:T(8,128)(2,1)S(1)}, bf16[128,1536]{1,0:T(8,128)(2,1)S(1)}, u32[]{:S(2)}, u32[]{:S(2)}) collective-permute-start(bf16[128,1536]{1,0:T(8,128)(2,1)S(1)} %collective-permute-done.23), channel_id=1, source_target_pairs={{1,0},{2,1},{3,2},{0,3},{5,4},{6,5},{7,6},{4,7},{9,8},{10,9},{11,1... | collective-permute-start | bytes 1179656 | tf_op jit(solution)/shard_map/ppermute | solution.py:26
  119.5 2.8 %collective-permute-start.22 = (f16[8,16,1536]{2,1,0:T(8,128)(2,1)S(1)}, f16[8,16,1536]{2,1,0:T(8,128)(2,1)S(1)}, u32[]{:S(2)}, u32[]{:S(2)}) collective-permute-start(f16[8,16,1536]{2,1,0:T(8,128)(2,1)S(1)} %fusion.53), channel_id=1, source_target_pairs={{0,16},{16,0},{8,24},{24,8},{1,17},{17,1},{9,25},{25,9},{2,18},{18... | collective-permute-start | bytes 1179656 | tf_op jit(solution)/shard_map/ppermute | solution.py:107
  122.3 2.8 %collective-permute-start.26 = (bf16[64,1536]{1,0:T(8,128)(2,1)S(1)}, bf16[64,1536]{1,0:T(8,128)(2,1)S(1)}, u32[]{:S(2)}, u32[]{:S(2)}) collective-permute-start(bf16[64,1536]{1,0:T(8,128)(2,1)S(1)} %get-tuple-element.22), channel_id=1, source_target_pairs={{1,0},{2,1},{3,2},{0,3},{5,4},{6,5},{7,6},{4,7},{9,8},{10,9},{11,1... | collective-permute-start | bytes 589832 | tf_op jit(solution)/shard_map/ppermute | solution.py:26
  132.2 2.8 %collective-permute-start.30 = (f16[8,16,1536]{2,1,0:T(8,128)(2,1)S(1)}, f16[8,16,1536]{2,1,0:T(8,128)(2,1)S(1)}, u32[]{:S(2)}, u32[]{:S(2)}) collective-permute-start(f16[8,16,1536]{2,1,0:T(8,128)(2,1)S(1)} %fusion.54), channel_id=1, source_target_pairs={{0,16},{16,0},{8,24},{24,8},{1,17},{17,1},{9,25},{25,9},{2,18},{18... | collective-permute-start | bytes 1179656 | tf_op jit(solution)/shard_map/ppermute | solution.py:107
  135.0 5.5 %all-to-all-start.1 = ((f16[8,16,1536]{2,1,0:T(8,128)(2,1)}), f16[8,16,1536]{2,1,0:T(8,128)(2,1)S(1)}, u32[]{:S(2)}, u32[]{:S(2)}) async-start(f16[8,16,1536]{2,1,0:T(8,128)(2,1)} %fusion.52), calls=%async_computation.1 | async-start | bytes 786432 | tf_op jit(solution)/shard_map/all_to_all | solution.py:110
  143.3 3.1 %collective-permute-done.31 = f32[8,128]{1,0:T(8,128)S(1)} collective-permute-done((f32[8,128]{1,0:T(8,128)S(1)}, f32[8,128]{1,0:T(8,128)S(1)}, u32[]{:S(2)}, u32[]{:S(2)}) %collective-permute-start.31) | collective-permute-done | bytes 4128 | tf_op jit(solution)/shard_map/ppermute | solution.py:49
  151.5 5.5 %all-to-all-start.2 = ((f16[8,16,1536]{2,1,0:T(8,128)(2,1)}), f16[8,16,1536]{2,1,0:T(8,128)(2,1)S(1)}, u32[]{:S(2)}, u32[]{:S(2)}) async-start(f16[8,16,1536]{2,1,0:T(8,128)(2,1)} %fusion.51), calls=%async_computation.2 | async-start | bytes 786432 | tf_op jit(solution)/shard_map/all_to_all | solution.py:110
  157.7 2.9 %collective-permute-done.33 = f32[8,128]{1,0:T(8,128)S(1)} collective-permute-done((f32[8,128]{1,0:T(8,128)S(1)}, f32[8,128]{1,0:T(8,128)S(1)}, u32[]{:S(2)}, u32[]{:S(2)}) %collective-permute-start.33) | collective-permute-done | bytes 4128 | tf_op jit(solution)/shard_map/ppermute | solution.py:49
  161.8 2.7 %collective-permute-start.35 = (f32[8,128]{1,0:T(8,128)S(1)}, f32[8,128]{1,0:T(8,128)S(1)}, u32[]{:S(2)}, u32[]{:S(2)}) collective-permute-start(f32[8,128]{1,0:T(8,128)S(1)} %max.37), channel_id=1, source_target_pairs={{0,16},{8,24},{16,0},{24,8},{1,17},{9,25},{17,1},{25,9},{2,18},{10... | collective-permute-start | bytes 12296 | tf_op jit(solution)/shard_map/ppermute | solution.py:49
  (132 shorter events, 66.3 us)
Async XLA Ops:
  7.1 24.0 %collective-permute-start.1 = (bf16[64,1536]{1,0:T(8,128)(2,1)S(1)}, bf16[64,1536]{1,0:T(8,128)(2,1)S(1)}, u32[]{:S(2)}, u32[]{:S(2)}) collective-permute-start(bf16[64,1536]{1,0:T(8,128)(2,1)S(1)} %pad_maximum_fusion.1), channel_id=1, source_target_pairs={{32,0},{64,32},{96,64},{128,96},{160,128},{192,160},{224,192},{0,2... | collective-permute-start | bytes 589832 | tf_op jit(solution)/shard_map/ppermute | solution.py:22
  9.0 17.8 %collective-permute-start.2 = (bf16[64,1536]{1,0:T(8,128)(2,1)S(1)}, bf16[64,1536]{1,0:T(8,128)(2,1)S(1)}, u32[]{:S(2)}, u32[]{:S(2)}) collective-permute-start(bf16[64,1536]{1,0:T(8,128)(2,1)S(1)} %pad_maximum_fusion.1), channel_id=1, source_target_pairs={{64,0},{96,32},{128,64},{160,96},{192,128},{224,160},{0,192},{32,2... | collective-permute-start | bytes 589832 | tf_op jit(solution)/shard_map/ppermute | solution.py:22
  13.6 13.2 %collective-permute-start.5 = (bf16[64,1536]{1,0:T(8,128)(2,1)S(1)}, bf16[64,1536]{1,0:T(8,128)(2,1)S(1)}, u32[]{:S(2)}, u32[]{:S(2)}) collective-permute-start(bf16[64,1536]{1,0:T(8,128)(2,1)S(1)} %pad_maximum_fusion.1), channel_id=1, source_target_pairs={{192,0},{224,32},{0,64},{32,96},{64,128},{96,160},{128,192},{160,2... | collective-permute-start | bytes 589832 | tf_op jit(solution)/shard_map/ppermute | solution.py:22
  13.6 23.6 %collective-permute-start.8 = (bf16[64,1536]{1,0:T(8,128)(2,1)S(1)}, bf16[64,1536]{1,0:T(8,128)(2,1)S(1)}, u32[]{:S(2)}, u32[]{:S(2)}) collective-permute-start(bf16[64,1536]{1,0:T(8,128)(2,1)S(1)} %pad_maximum_fusion.1), channel_id=1, source_target_pairs={{224,0},{0,32},{32,64},{64,96},{96,128},{128,160},{160,192},{192,2... | collective-permute-start | bytes 589832 | tf_op jit(solution)/shard_map/ppermute | solution.py:22
  26.8 10.0 %collective-permute-start.6 = (bf16[32,1536]{1,0:T(8,128)(2,1)S(1)}, bf16[32,1536]{1,0:T(8,128)(2,1)S(1)}, u32[]{:S(2)}, u32[]{:S(2)}) collective-permute-start(bf16[32,1536]{1,0:T(8,128)(2,1)S(1)} %slice.146), channel_id=1, source_target_pairs={{192,0},{224,32},{0,64},{32,96},{64,128},{96,160},{128,192},{160,2... | collective-permute-start | bytes 294920 | tf_op jit(solution)/shard_map/ppermute | solution.py:22
  26.9 9.9 %collective-permute-start.4 = (bf16[32,1536]{1,0:T(8,128)(2,1)S(1)}, bf16[32,1536]{1,0:T(8,128)(2,1)S(1)}, u32[]{:S(2)}, u32[]{:S(2)}) collective-permute-start(bf16[32,1536]{1,0:T(8,128)(2,1)S(1)} %slice.145), channel_id=1, source_target_pairs={{64,0},{96,32},{128,64},{160,96},{192,128},{224,160},{0,192},{32,2... | collective-permute-start | bytes 294920 | tf_op jit(solution)/shard_map/ppermute | solution.py:22
  46.9 19.9 %collective-permute-start.10 = (f16[4,128,768]{2,1,0:T(8,128)(2,1)}, f16[4,128,768]{2,1,0:T(8,128)(2,1)}, u32[]{:S(2)}, u32[]{:S(2)}) collective-permute-start(f16[4,128,768]{2,1,0:T(8,128)(2,1)} %fusion.21), channel_id=1, source_target_pairs={{0,4},{1,5},{2,6},{3,7},{4,0},{5,1},{6,2},{7,3},{8,12},{9,13},{10,... | collective-permute-start | bytes 2359304 | tf_op jit(solution)/shard_map/ppermute | solution.py:69
  52.1 26.9 %all-to-all-start = ((f16[4,2,128,768]{3,2,1,0:T(8,128)(2,1)}), f16[4,2,128,768]{3,2,1,0:T(8,128)(2,1)}, u32[]{:S(2)}, u32[]{:S(2)}) async-start(f16[4,2,128,768]{3,2,1,0:T(8,128)(2,1)} %bitcast.106), calls=%async_computation | async-start | bytes 3145728 | tf_op jit(solution)/shard_map/all_to_all | solution.py:73
  68.7 12.9 %collective-permute-start.13 = (f16[128,768]{1,0:T(8,128)(2,1)S(1)}, f16[128,768]{1,0:T(8,128)(2,1)S(1)}, u32[]{:S(2)}, u32[]{:S(2)}) collective-permute-start(f16[128,768]{1,0:T(8,128)(2,1)S(1)} %get-tuple-element.39), channel_id=1, source_target_pairs={{1,0},{2,1},{3,2},{0,3},{5,4},{6,5},{7,6},{4,7},{9,8},{10,9},{11,1... | collective-permute-start | bytes 589832 | tf_op jit(solution)/shard_map/ppermute | solution.py:26
  71.8 11.3 %collective-permute-start.12 = (f16[128,768]{1,0:T(8,128)(2,1)S(1)}, f16[128,768]{1,0:T(8,128)(2,1)S(1)}, u32[]{:S(2)}, u32[]{:S(2)}) collective-permute-start(f16[128,768]{1,0:T(8,128)(2,1)S(1)} %get-tuple-element.40), channel_id=1, source_target_pairs={{2,0},{3,1},{0,2},{1,3},{6,4},{7,5},{4,6},{5,7},{10,8},{11,9},{8,1... | collective-permute-start | bytes 589832 | tf_op jit(solution)/shard_map/ppermute | solution.py:26
  72.4 13.7 %collective-permute-start.11 = (f16[128,768]{1,0:T(8,128)(2,1)S(1)}, f16[128,768]{1,0:T(8,128)(2,1)S(1)}, u32[]{:S(2)}, u32[]{:S(2)}) collective-permute-start(f16[128,768]{1,0:T(8,128)(2,1)S(1)} %get-tuple-element.38), channel_id=1, source_target_pairs={{3,0},{0,1},{1,2},{2,3},{7,4},{4,5},{5,6},{6,7},{11,8},{8,9},{9,10... | collective-permute-start | bytes 589832 | tf_op jit(solution)/shard_map/ppermute | solution.py:26
  90.4 10.5 %collective-permute-start.17 = (bf16[128,1536]{1,0:T(8,128)(2,1)S(1)}, bf16[128,1536]{1,0:T(8,128)(2,1)S(1)}, u32[]{:S(2)}, u32[]{:S(2)}) collective-permute-start(bf16[128,1536]{1,0:T(8,128)(2,1)S(1)} %get-tuple-element.34), channel_id=1, source_target_pairs={{1,0},{2,1},{3,2},{0,3},{5,4},{6,5},{7,6},{4,7},{9,8},{10,9},{11,1... | collective-permute-start | bytes 1179656 | tf_op jit(solution)/shard_map/ppermute | solution.py:26
  91.6 10.6 %collective-permute-start.18 = (bf16[128,1536]{1,0:T(8,128)(2,1)S(1)}, bf16[128,1536]{1,0:T(8,128)(2,1)S(1)}, u32[]{:S(2)}, u32[]{:S(2)}) collective-permute-start(bf16[128,1536]{1,0:T(8,128)(2,1)S(1)} %get-tuple-element.34), channel_id=1, source_target_pairs={{3,0},{0,1},{1,2},{2,3},{7,4},{4,5},{5,6},{6,7},{11,8},{8,9},{9,10... | collective-permute-start | bytes 1179656 | tf_op jit(solution)/shard_map/ppermute | solution.py:26
  92.5 11.9 %collective-permute-start.23 = (bf16[128,1536]{1,0:T(8,128)(2,1)S(1)}, bf16[128,1536]{1,0:T(8,128)(2,1)S(1)}, u32[]{:S(2)}, u32[]{:S(2)}) collective-permute-start(bf16[128,1536]{1,0:T(8,128)(2,1)S(1)} %get-tuple-element.34), channel_id=1, source_target_pairs={{0,4},{1,5},{2,6},{3,7},{4,0},{5,1},{6,2},{7,3},{8,12},{9,13},{10,... | collective-permute-start | bytes 1179656 | tf_op jit(solution)/shard_map/ppermute | solution.py:87
  102.3 7.9 %collective-permute-start.19 = (bf16[64,1536]{1,0:T(8,128)(2,1)S(1)}, bf16[64,1536]{1,0:T(8,128)(2,1)S(1)}, u32[]{:S(2)}, u32[]{:S(2)}) collective-permute-start(bf16[64,1536]{1,0:T(8,128)(2,1)S(1)} %get-tuple-element.48), channel_id=1, source_target_pairs={{1,0},{2,1},{3,2},{0,3},{5,4},{6,5},{7,6},{4,7},{9,8},{10,9},{11,1... | collective-permute-start | bytes 589832 | tf_op jit(solution)/shard_map/ppermute | solution.py:26
  102.5 9.0 %collective-permute-start.20 = (bf16[64,1536]{1,0:T(8,128)(2,1)S(1)}, bf16[64,1536]{1,0:T(8,128)(2,1)S(1)}, u32[]{:S(2)}, u32[]{:S(2)}) collective-permute-start(bf16[64,1536]{1,0:T(8,128)(2,1)S(1)} %get-tuple-element.49), channel_id=1, source_target_pairs={{3,0},{0,1},{1,2},{2,3},{7,4},{4,5},{5,6},{6,7},{11,8},{8,9},{9,10... | collective-permute-start | bytes 589832 | tf_op jit(solution)/shard_map/ppermute | solution.py:26
  104.4 11.9 %collective-permute-start.25 = (bf16[128,1536]{1,0:T(8,128)(2,1)S(1)}, bf16[128,1536]{1,0:T(8,128)(2,1)S(1)}, u32[]{:S(2)}, u32[]{:S(2)}) collective-permute-start(bf16[128,1536]{1,0:T(8,128)(2,1)S(1)} %collective-permute-done.23), channel_id=1, source_target_pairs={{3,0},{0,1},{1,2},{2,3},{7,4},{4,5},{5,6},{6,7},{11,8},{8,9},{9,10... | collective-permute-start | bytes 1179656 | tf_op jit(solution)/shard_map/ppermute | solution.py:26
  105.0 11.4 %collective-permute-start.24 = (bf16[128,1536]{1,0:T(8,128)(2,1)S(1)}, bf16[128,1536]{1,0:T(8,128)(2,1)S(1)}, u32[]{:S(2)}, u32[]{:S(2)}) collective-permute-start(bf16[128,1536]{1,0:T(8,128)(2,1)S(1)} %collective-permute-done.23), channel_id=1, source_target_pairs={{1,0},{2,1},{3,2},{0,3},{5,4},{6,5},{7,6},{4,7},{9,8},{10,9},{11,1... | collective-permute-start | bytes 1179656 | tf_op jit(solution)/shard_map/ppermute | solution.py:26
  116.7 8.5 %collective-permute-start.27 = (bf16[64,1536]{1,0:T(8,128)(2,1)S(1)}, bf16[64,1536]{1,0:T(8,128)(2,1)S(1)}, u32[]{:S(2)}, u32[]{:S(2)}) collective-permute-start(bf16[64,1536]{1,0:T(8,128)(2,1)S(1)} %get-tuple-element.23), channel_id=1, source_target_pairs={{3,0},{0,1},{1,2},{2,3},{7,4},{4,5},{5,6},{6,7},{11,8},{8,9},{9,10... | collective-permute-start | bytes 589832 | tf_op jit(solution)/shard_map/ppermute | solution.py:26
  117.2 8.0 %collective-permute-start.29 = (f32[8,128]{1,0:T(8,128)S(1)}, f32[8,128]{1,0:T(8,128)S(1)}, u32[]{:S(2)}, u32[]{:S(2)}) collective-permute-start(f32[8,128]{1,0:T(8,128)S(1)} %fusion.81), channel_id=1, source_target_pairs={{0,128},{32,160},{64,192},{96,224},{128,0},{160,32},{192,64},{224,... | collective-permute-start | bytes 12296 | tf_op jit(solution)/shard_map/ppermute | solution.py:49
  119.5 11.4 %collective-permute-start.22 = (f16[8,16,1536]{2,1,0:T(8,128)(2,1)S(1)}, f16[8,16,1536]{2,1,0:T(8,128)(2,1)S(1)}, u32[]{:S(2)}, u32[]{:S(2)}) collective-permute-start(f16[8,16,1536]{2,1,0:T(8,128)(2,1)S(1)} %fusion.53), channel_id=1, source_target_pairs={{0,16},{16,0},{8,24},{24,8},{1,17},{17,1},{9,25},{25,9},{2,18},{18... | collective-permute-start | bytes 1179656 | tf_op jit(solution)/shard_map/ppermute | solution.py:107
  132.2 10.5 %collective-permute-start.30 = (f16[8,16,1536]{2,1,0:T(8,128)(2,1)S(1)}, f16[8,16,1536]{2,1,0:T(8,128)(2,1)S(1)}, u32[]{:S(2)}, u32[]{:S(2)}) collective-permute-start(f16[8,16,1536]{2,1,0:T(8,128)(2,1)S(1)} %fusion.54), channel_id=1, source_target_pairs={{0,16},{16,0},{8,24},{24,8},{1,17},{17,1},{9,25},{25,9},{2,18},{18... | collective-permute-start | bytes 1179656 | tf_op jit(solution)/shard_map/ppermute | solution.py:107
  135.0 16.5 %all-to-all-start.1 = ((f16[8,16,1536]{2,1,0:T(8,128)(2,1)}), f16[8,16,1536]{2,1,0:T(8,128)(2,1)S(1)}, u32[]{:S(2)}, u32[]{:S(2)}) async-start(f16[8,16,1536]{2,1,0:T(8,128)(2,1)} %fusion.52), calls=%async_computation.1 | async-start | bytes 786432 | tf_op jit(solution)/shard_map/all_to_all | solution.py:110
  151.5 17.2 %all-to-all-start.2 = ((f16[8,16,1536]{2,1,0:T(8,128)(2,1)}), f16[8,16,1536]{2,1,0:T(8,128)(2,1)S(1)}, u32[]{:S(2)}, u32[]{:S(2)}) async-start(f16[8,16,1536]{2,1,0:T(8,128)(2,1)} %fusion.51), calls=%async_computation.2 | async-start | bytes 786432 | tf_op jit(solution)/shard_map/all_to_all | solution.py:110
  (22 other events, 157.3 us)

commit v7 on v6

--- a/solution.py
+++ b/solution.py
@@ -38,9 +38,10 @@
     z3, z5 = from_z(z2, 1), from_z(z6, 7)
     z4 = jnp.concatenate([from_z(z2[: 2 * n], 2), from_z(z6[2 * n :], 6)])
     mine = jnp.stack([own, z1, z2, z3, z4, z5, z6, z7])
-    both = jnp.stack([mine, lax.ppermute(mine, "col", core_swap)])
-    both = both.reshape(2, 4, 2, 2, 2 * n, width)
-    return both.transpose(1, 3, 0, 2, 4, 5).reshape(64 * n, width)
+    def ordered(x):
+        return x.reshape(4, 2, 2, 2 * n, width).transpose(0, 2, 1, 3, 4).reshape(32 * n, width)
+
+    return ordered(mine), ordered(lax.ppermute(mine, "col", core_swap))
 
 
 def peak_over(peak, *steps):
@@ -58,20 +59,21 @@
     turn = (24 - z - 2 * y) % 8
     n, width = tokens.shape[0] // 2, tokens.shape[1]
 
-    rows = gather_tokens(tokens)
+    mine, other = gather_tokens(tokens)
     half, own_lo = w_up.shape[1] // 2, lo == 0
 
-    def up(w):
-        return (dot(rows, w) * up_gain).reshape(4, 2, 8 * n, -1)
+    def up(rows, w):
+        return (dot(rows, w) * up_gain).reshape(4, 2, rows.shape[0] // 8, -1)
 
     def over_x_lo(x):
         x0, x1 = x[..., 0, :, :], x[..., 1, :, :]
         came = lax.ppermute(jnp.where(own_lo, x1, x0).astype(f16), "dep", x_lo_swap)
         return jnp.where(own_lo, x0, x1) + came.astype(f32)
 
-    b_sent = up(w_up[:, half:]).astype(f16)
+    rows = jnp.concatenate([v.reshape(8, 4 * n, width) for v in (mine, other)], axis=1).reshape(64 * n, width)
+    b_sent = up(rows, w_up[:, half:]).astype(f16)
     b_got = lax.all_to_all(b_sent, "dep", 0, 0, tiled=True, axis_index_groups=[[0, 1, 2, 3], [4, 5, 6, 7]])
-    a_sum = over_x_lo(up(w_up[:, :half]))
+    a_sum = over_x_lo(jnp.concatenate([up(mine, w_up[:, :half]), up(other, w_up[:, :half])], axis=2))
     a_sum = lax.dynamic_slice_in_dim(jnp.concatenate([a_sum, a_sum]), y, 4)
     a_sent = a_sum.astype(f16)
     a_got = [from_y(a_sent[j], 4 - j).astype(f32) for j in (1, 2, 3)]

time: 170 us -> 170 us (level)
  local copies, waits for them, and re-layouts: 2.71 us -> 4.74 us
  waiting for transfers between devices: 67 us -> 65.2 us
    ppermute x1, waiting for transfers between devices: 3.38 us -> 0.17 us  [gather_tokens(): return (ordered(mine), ordered(lax.ppermute(mine, 'col', core_swap)))]
    ppermute x11, waiting for transfers between devices: 15 us -> 17.8 us  [from_y(): lax.ppermute(x, 'dep', [(4 * l + (i + k) % 4, 4 * l + i) for l in range(2...]
    dot_general x7 -> x8, matrix products: 16.1 us -> 16.4 us  [dot(): return jnp.dot(a, b, preferred_element_type=f32)]
  transfers between devices with their start and end apart: 39 -> 39, of which waited for: 24 -> 23; matrix products, arithmetic and copies ran while one was open for 13% -> 16% of each run, Pallas kernels for 0% -> 0%
where the time goes in v7:
time: 170 us; the launch traced here: 169 us
  starting transfers between devices  67 us (39%)
  waiting for transfers between devices  65.2 us (38%)
  matrix products  16.4 us (10%)
  other arithmetic  13.3 us (8%)
  local copies, waits for them, and re-layouts  4.74 us (3%)
  between operations  2.51 us (1%)
    ppermute x11, waiting for transfers between devices, from_y(): lax.ppermute(x, 'dep', [(4 * l + (i + k) % 4, 4 * l + i) for l in range(2...  17.8 us
    dot_general x8, matrix products, dot(): return jnp.dot(a, b, preferred_element_type=f32)  16.4 us
    ppermute x8, waiting for transfers between devices, from_z(): return lax.ppermute(x, 'row', [((i + k) % 8, i) for i in range(8)])  16.1 us
    ppermute x11, starting transfers between devices, from_y(): lax.ppermute(x, 'dep', [(4 * l + (i + k) % 4, 4 * l + i) for l in range(2...  15.4 us
    ppermute x8, starting transfers between devices, from_z(): return lax.ppermute(x, 'row', [((i + k) % 8, i) for i in range(8)])  13.8 us
    ppermute x8, waiting for transfers between devices, peak_over(): lax.ppermute(peak, axis, [(i, i ^ step) for i in range(size)])  12.2 us
    all_to_all x2, starting transfers between devices, over_row(): return lax.all_to_all(x, 'row', 0, 0, tiled=True)  11 us
    ppermute x8, starting transfers between devices, peak_over(): lax.ppermute(peak, axis, [(i, i ^ step) for i in range(size)])  10.8 us
  transfers between devices with their start and end apart: 39, of which 23 were waited for; matrix products, arithmetic and copies ran while one was open for 16% of the time, Pallas kernels for 0%

profile of v7, /device:TPU:32, one launch (start us, length us, event | category | flops | bytes accessed | tf_op | source)
XLA Modules:
  0.0 169.2 jit_solution(17575376751042982713)
XLA Ops:
  0.6 3.1 %collective-permute-start = (bf16[32,1536]{1,0:T(8,128)(2,1)}, bf16[32,1536]{1,0:T(8,128)(2,1)S(1)}, u32[]{:S(2)}, u32[]{:S(2)}) collective-permute-start(bf16[32,1536]{1,0:T(8,128)(2,1)} %param.6), channel_id=1, source_target_pairs={{0,16},{16,0},{8,24},{24,8},{1,17},{17,1},{9,25},{25,9},{2,18},{18... | collective-permute-start | bytes 294920 | tf_op jit(solution)/shard_map/ppermute | solution.py:35
  4.6 2.5 %collective-permute-done = bf16[32,1536]{1,0:T(8,128)(2,1)S(1)} collective-permute-done((bf16[32,1536]{1,0:T(8,128)(2,1)}, bf16[32,1536]{1,0:T(8,128)(2,1)S(1)}, u32[]{:S(2)}, u32[]{:S(2)}) %collective-permute-start) | collective-permute-done | bytes 98336 | tf_op jit(solution)/shard_map/ppermute | solution.py:35
  9.0 4.6 %collective-permute-start.2 = (bf16[64,1536]{1,0:T(8,128)(2,1)S(1)}, bf16[64,1536]{1,0:T(8,128)(2,1)S(1)}, u32[]{:S(2)}, u32[]{:S(2)}) collective-permute-start(bf16[64,1536]{1,0:T(8,128)(2,1)S(1)} %pad_maximum_fusion.3), channel_id=1, source_target_pairs={{64,0},{96,32},{128,64},{160,96},{192,128},{224,160},{0,192},{32,2... | collective-permute-start | bytes 589832 | tf_op jit(solution)/shard_map/ppermute | solution.py:22
  14.6 12.1 %collective-permute-done.5 = bf16[64,1536]{1,0:T(8,128)(2,1)S(1)} collective-permute-done((bf16[64,1536]{1,0:T(8,128)(2,1)S(1)}, bf16[64,1536]{1,0:T(8,128)(2,1)S(1)}, u32[]{:S(2)}, u32[]{:S(2)}) %collective-permute-start.5) | collective-permute-done | bytes 196640 | tf_op jit(solution)/shard_map/ppermute | solution.py:22
  26.9 4.2 %collective-permute-start.4 = (bf16[32,1536]{1,0:T(8,128)(2,1)S(1)}, bf16[32,1536]{1,0:T(8,128)(2,1)S(1)}, u32[]{:S(2)}, u32[]{:S(2)}) collective-permute-start(bf16[32,1536]{1,0:T(8,128)(2,1)S(1)} %slice.146), channel_id=1, source_target_pairs={{64,0},{96,32},{128,64},{160,96},{192,128},{224,160},{0,192},{32,2... | collective-permute-start | bytes 294920 | tf_op jit(solution)/shard_map/ppermute | solution.py:22
  33.1 3.6 %collective-permute-done.3 = bf16[64,1536]{1,0:T(8,128)(2,1)S(1)} collective-permute-done((bf16[64,1536]{1,0:T(8,128)(2,1)S(1)}, bf16[64,1536]{1,0:T(8,128)(2,1)S(1)}, u32[]{:S(2)}, u32[]{:S(2)}) %collective-permute-start.3) | collective-permute-done | bytes 196640 | tf_op jit(solution)/shard_map/ppermute | solution.py:22
  37.5 3.2 %fusion.14 = f32[512,768]{1,0:T(8,128)S(1)} fusion(bf16[512,1536]{1,0:T(8,128)(2,1)S(1)} %bitcast.107, bf16[1536,1536]{1,0:T(8,128)(2,1)} %param.7), kind=kOutput, calls=%fused_computation.29 | convolution fusion | flops 1208352768 | bytes 5505024 | tf_op jit(solution)/shard_map/dot_general | solution.py:18
  46.9 3.7 %multiply_convert_fusion = f16[1024,768]{1,0:T(8,128)(2,1)} fusion(bf16[1024,1536]{1,0:T(8,128)(2,1)S(1)} %bitcast.117, bf16[1536,1536]{1,0:T(8,128)(2,1)S(1)} %bitcast.122), kind=kOutput, calls=%fused_computation.6 | convolution fusion | flops 2417491968 | bytes 7077888 | tf_op jit(solution)/shard_map/dot_general | solution.py:18
  50.6 4.6 %all-to-all-start = ((f16[4,2,128,768]{3,2,1,0:T(8,128)(2,1)}), f16[4,2,128,768]{3,2,1,0:T(8,128)(2,1)S(1)}, u32[]{:S(2)}, u32[]{:S(2)}) async-start(f16[4,2,128,768]{3,2,1,0:T(8,128)(2,1)} %bitcast.119), calls=%async_computation | async-start | bytes 3145728 | tf_op jit(solution)/shard_map/all_to_all | solution.py:75
  56.5 8.8 %collective-permute-done.10 = f16[4,128,768]{2,1,0:T(8,128)(2,1)} collective-permute-done((f16[4,128,768]{2,1,0:T(8,128)(2,1)}, f16[4,128,768]{2,1,0:T(8,128)(2,1)}, u32[]{:S(2)}, u32[]{:S(2)}) %collective-permute-start.10) | collective-permute-done | bytes 786464 | tf_op jit(solution)/shard_map/ppermute | solution.py:70
  68.3 3.0 %collective-permute-start.13 = (f16[128,768]{1,0:T(8,128)(2,1)}, f16[128,768]{1,0:T(8,128)(2,1)}, u32[]{:S(2)}, u32[]{:S(2)}) collective-permute-start(f16[128,768]{1,0:T(8,128)(2,1)} %get-tuple-element.39), channel_id=1, source_target_pairs={{1,0},{2,1},{3,2},{0,3},{5,4},{6,5},{7,6},{4,7},{9,8},{10,9},{11,1... | collective-permute-start | bytes 589832 | tf_op jit(solution)/shard_map/ppermute | solution.py:26
  72.9 4.5 %all-to-all-done = f16[4,2,128,768]{3,2,1,0:T(8,128)(2,1)S(1)} async-done(((f16[4,2,128,768]{3,2,1,0:T(8,128)(2,1)}), f16[4,2,128,768]{3,2,1,0:T(8,128)(2,1)S(1)}, u32[]{:S(2)}, u32[]{:S(2)}) %all-to-all-start) | async-done | bytes 1572896 | tf_op jit(solution)/shard_map/all_to_all | solution.py:75
  81.7 2.9 %collective-permute-done.11 = f16[128,768]{1,0:T(8,128)(2,1)} collective-permute-done((f16[128,768]{1,0:T(8,128)(2,1)S(1)}, f16[128,768]{1,0:T(8,128)(2,1)}, u32[]{:S(2)}, u32[]{:S(2)}) %collective-permute-start.11) | collective-permute-done | bytes 196640 | tf_op jit(solution)/shard_map/ppermute | solution.py:26
  94.9 3.2 %convolution_multiply_fusion.4 = f32[128,1536]{1,0:T(8,128)S(1)} fusion(bf16[128,1536]{1,0:T(8,128)(2,1)S(1)} %get-tuple-element.34, bf16[1536,1536]{1,0:T(8,128)(2,1)} %param.9, f32[]{:T(128)S(6)} %div.18), kind=kOutput, calls=%fused_computation.13 | convolution fusion | flops 604176384 | bytes 5898244 | tf_op jit(solution)/shard_map/dot_general | solution.py:18
  104.6 2.8 %collective-permute-start.24 = (bf16[128,1536]{1,0:T(8,128)(2,1)S(1)}, bf16[128,1536]{1,0:T(8,128)(2,1)S(1)}, u32[]{:S(2)}, u32[]{:S(2)}) collective-permute-start(bf16[128,1536]{1,0:T(8,128)(2,1)S(1)} %collective-permute-done.23), channel_id=1, source_target_pairs={{1,0},{2,1},{3,2},{0,3},{5,4},{6,5},{7,6},{4,7},{9,8},{10,9},{11,1... | collective-permute-start | bytes 1179656 | tf_op jit(solution)/shard_map/ppermute | solution.py:26
  119.5 2.8 %collective-permute-start.22 = (f16[8,16,1536]{2,1,0:T(8,128)(2,1)S(1)}, f16[8,16,1536]{2,1,0:T(8,128)(2,1)S(1)}, u32[]{:S(2)}, u32[]{:S(2)}) collective-permute-start(f16[8,16,1536]{2,1,0:T(8,128)(2,1)S(1)} %fusion.59), channel_id=1, source_target_pairs={{0,16},{16,0},{8,24},{24,8},{1,17},{17,1},{9,25},{25,9},{2,18},{18... | collective-permute-start | bytes 1179656 | tf_op jit(solution)/shard_map/ppermute | solution.py:109
  122.3 2.8 %collective-permute-start.26 = (bf16[64,1536]{1,0:T(8,128)(2,1)S(1)}, bf16[64,1536]{1,0:T(8,128)(2,1)S(1)}, u32[]{:S(2)}, u32[]{:S(2)}) collective-permute-start(bf16[64,1536]{1,0:T(8,128)(2,1)S(1)} %get-tuple-element.22), channel_id=1, source_target_pairs={{1,0},{2,1},{3,2},{0,3},{5,4},{6,5},{7,6},{4,7},{9,8},{10,9},{11,1... | collective-permute-start | bytes 589832 | tf_op jit(solution)/shard_map/ppermute | solution.py:26
  131.9 2.8 %collective-permute-start.30 = (f16[8,16,1536]{2,1,0:T(8,128)(2,1)S(1)}, f16[8,16,1536]{2,1,0:T(8,128)(2,1)S(1)}, u32[]{:S(2)}, u32[]{:S(2)}) collective-permute-start(f16[8,16,1536]{2,1,0:T(8,128)(2,1)S(1)} %fusion.60), channel_id=1, source_target_pairs={{0,16},{16,0},{8,24},{24,8},{1,17},{17,1},{9,25},{25,9},{2,18},{18... | collective-permute-start | bytes 1179656 | tf_op jit(solution)/shard_map/ppermute | solution.py:109
  134.7 5.5 %all-to-all-start.1 = ((f16[8,16,1536]{2,1,0:T(8,128)(2,1)}), f16[8,16,1536]{2,1,0:T(8,128)(2,1)S(1)}, u32[]{:S(2)}, u32[]{:S(2)}) async-start(f16[8,16,1536]{2,1,0:T(8,128)(2,1)} %fusion.58), calls=%async_computation.1 | async-start | bytes 786432 | tf_op jit(solution)/shard_map/all_to_all | solution.py:112
  143.4 2.7 %collective-permute-done.31 = f32[8,128]{1,0:T(8,128)S(1)} collective-permute-done((f32[8,128]{1,0:T(8,128)S(1)}, f32[8,128]{1,0:T(8,128)S(1)}, u32[]{:S(2)}, u32[]{:S(2)}) %collective-permute-start.31) | collective-permute-done | bytes 4128 | tf_op jit(solution)/shard_map/ppermute | solution.py:50
  151.2 5.5 %all-to-all-start.2 = ((f16[8,16,1536]{2,1,0:T(8,128)(2,1)}), f16[8,16,1536]{2,1,0:T(8,128)(2,1)S(1)}, u32[]{:S(2)}, u32[]{:S(2)}) async-start(f16[8,16,1536]{2,1,0:T(8,128)(2,1)} %fusion.57), calls=%async_computation.2 | async-start | bytes 786432 | tf_op jit(solution)/shard_map/all_to_all | solution.py:112
  156.9 3.4 %collective-permute-done.33 = f32[8,128]{1,0:T(8,128)S(1)} collective-permute-done((f32[8,128]{1,0:T(8,128)S(1)}, f32[8,128]{1,0:T(8,128)S(1)}, u32[]{:S(2)}, u32[]{:S(2)}) %collective-permute-start.33) | collective-permute-done | bytes 4128 | tf_op jit(solution)/shard_map/ppermute | solution.py:50
  161.5 2.4 %collective-permute-start.35 = (f32[8,128]{1,0:T(8,128)S(1)}, f32[8,128]{1,0:T(8,128)S(1)}, u32[]{:S(2)}, u32[]{:S(2)}) collective-permute-start(f32[8,128]{1,0:T(8,128)S(1)} %max.37), channel_id=1, source_target_pairs={{0,16},{8,24},{16,0},{24,8},{1,17},{9,25},{17,1},{25,9},{2,18},{10... | collective-permute-start | bytes 12296 | tf_op jit(solution)/shard_map/ppermute | solution.py:50
  163.9 2.6 %collective-permute-done.35 = f32[8,128]{1,0:T(8,128)S(1)} collective-permute-done((f32[8,128]{1,0:T(8,128)S(1)}, f32[8,128]{1,0:T(8,128)S(1)}, u32[]{:S(2)}, u32[]{:S(2)}) %collective-permute-start.35) | collective-permute-done | bytes 4128 | tf_op jit(solution)/shard_map/ppermute | solution.py:50
  (136 shorter events, 69.3 us)
Async XLA Ops:
  7.1 24.0 %collective-permute-start.1 = (bf16[64,1536]{1,0:T(8,128)(2,1)S(1)}, bf16[64,1536]{1,0:T(8,128)(2,1)S(1)}, u32[]{:S(2)}, u32[]{:S(2)}) collective-permute-start(bf16[64,1536]{1,0:T(8,128)(2,1)S(1)} %pad_maximum_fusion.3), channel_id=1, source_target_pairs={{32,0},{64,32},{96,64},{128,96},{160,128},{192,160},{224,192},{0,2... | collective-permute-start | bytes 589832 | tf_op jit(solution)/shard_map/ppermute | solution.py:22
  9.0 17.8 %collective-permute-start.2 = (bf16[64,1536]{1,0:T(8,128)(2,1)S(1)}, bf16[64,1536]{1,0:T(8,128)(2,1)S(1)}, u32[]{:S(2)}, u32[]{:S(2)}) collective-permute-start(bf16[64,1536]{1,0:T(8,128)(2,1)S(1)} %pad_maximum_fusion.3), channel_id=1, source_target_pairs={{64,0},{96,32},{128,64},{160,96},{192,128},{224,160},{0,192},{32,2... | collective-permute-start | bytes 589832 | tf_op jit(solution)/shard_map/ppermute | solution.py:22
  13.6 13.2 %collective-permute-start.5 = (bf16[64,1536]{1,0:T(8,128)(2,1)S(1)}, bf16[64,1536]{1,0:T(8,128)(2,1)S(1)}, u32[]{:S(2)}, u32[]{:S(2)}) collective-permute-start(bf16[64,1536]{1,0:T(8,128)(2,1)S(1)} %pad_maximum_fusion.3), channel_id=1, source_target_pairs={{192,0},{224,32},{0,64},{32,96},{64,128},{96,160},{128,192},{160,2... | collective-permute-start | bytes 589832 | tf_op jit(solution)/shard_map/ppermute | solution.py:22
  13.6 23.6 %collective-permute-start.8 = (bf16[64,1536]{1,0:T(8,128)(2,1)S(1)}, bf16[64,1536]{1,0:T(8,128)(2,1)S(1)}, u32[]{:S(2)}, u32[]{:S(2)}) collective-permute-start(bf16[64,1536]{1,0:T(8,128)(2,1)S(1)} %pad_maximum_fusion.3), channel_id=1, source_target_pairs={{224,0},{0,32},{32,64},{64,96},{96,128},{128,160},{160,192},{192,2... | collective-permute-start | bytes 589832 | tf_op jit(solution)/shard_map/ppermute | solution.py:22
  26.8 10.0 %collective-permute-start.6 = (bf16[32,1536]{1,0:T(8,128)(2,1)S(1)}, bf16[32,1536]{1,0:T(8,128)(2,1)S(1)}, u32[]{:S(2)}, u32[]{:S(2)}) collective-permute-start(bf16[32,1536]{1,0:T(8,128)(2,1)S(1)} %slice.147), channel_id=1, source_target_pairs={{192,0},{224,32},{0,64},{32,96},{64,128},{96,160},{128,192},{160,2... | collective-permute-start | bytes 294920 | tf_op jit(solution)/shard_map/ppermute | solution.py:22
  26.9 9.9 %collective-permute-start.4 = (bf16[32,1536]{1,0:T(8,128)(2,1)S(1)}, bf16[32,1536]{1,0:T(8,128)(2,1)S(1)}, u32[]{:S(2)}, u32[]{:S(2)}) collective-permute-start(bf16[32,1536]{1,0:T(8,128)(2,1)S(1)} %slice.146), channel_id=1, source_target_pairs={{64,0},{96,32},{128,64},{160,96},{192,128},{224,160},{0,192},{32,2... | collective-permute-start | bytes 294920 | tf_op jit(solution)/shard_map/ppermute | solution.py:22
  45.2 20.1 %collective-permute-start.10 = (f16[4,128,768]{2,1,0:T(8,128)(2,1)}, f16[4,128,768]{2,1,0:T(8,128)(2,1)}, u32[]{:S(2)}, u32[]{:S(2)}) collective-permute-start(f16[4,128,768]{2,1,0:T(8,128)(2,1)} %fusion.27), channel_id=1, source_target_pairs={{0,4},{1,5},{2,6},{3,7},{4,0},{5,1},{6,2},{7,3},{8,12},{9,13},{10,... | collective-permute-start | bytes 2359304 | tf_op jit(solution)/shard_map/ppermute | solution.py:70
  50.6 26.8 %all-to-all-start = ((f16[4,2,128,768]{3,2,1,0:T(8,128)(2,1)}), f16[4,2,128,768]{3,2,1,0:T(8,128)(2,1)S(1)}, u32[]{:S(2)}, u32[]{:S(2)}) async-start(f16[4,2,128,768]{3,2,1,0:T(8,128)(2,1)} %bitcast.119), calls=%async_computation | async-start | bytes 3145728 | tf_op jit(solution)/shard_map/all_to_all | solution.py:75
  68.3 11.9 %collective-permute-start.13 = (f16[128,768]{1,0:T(8,128)(2,1)}, f16[128,768]{1,0:T(8,128)(2,1)}, u32[]{:S(2)}, u32[]{:S(2)}) collective-permute-start(f16[128,768]{1,0:T(8,128)(2,1)} %get-tuple-element.39), channel_id=1, source_target_pairs={{1,0},{2,1},{3,2},{0,3},{5,4},{6,5},{7,6},{4,7},{9,8},{10,9},{11,1... | collective-permute-start | bytes 589832 | tf_op jit(solution)/shard_map/ppermute | solution.py:26
  71.3 10.4 %collective-permute-start.12 = (f16[128,768]{1,0:T(8,128)(2,1)S(1)}, f16[128,768]{1,0:T(8,128)(2,1)}, u32[]{:S(2)}, u32[]{:S(2)}) collective-permute-start(f16[128,768]{1,0:T(8,128)(2,1)S(1)} %get-tuple-element.40), channel_id=1, source_target_pairs={{2,0},{3,1},{0,2},{1,3},{6,4},{7,5},{4,6},{5,7},{10,8},{11,9},{8,1... | collective-permute-start | bytes 589832 | tf_op jit(solution)/shard_map/ppermute | solution.py:26
  71.9 12.7 %collective-permute-start.11 = (f16[128,768]{1,0:T(8,128)(2,1)S(1)}, f16[128,768]{1,0:T(8,128)(2,1)}, u32[]{:S(2)}, u32[]{:S(2)}) collective-permute-start(f16[128,768]{1,0:T(8,128)(2,1)S(1)} %get-tuple-element.38), channel_id=1, source_target_pairs={{3,0},{0,1},{1,2},{2,3},{7,4},{4,5},{5,6},{6,7},{11,8},{8,9},{9,10... | collective-permute-start | bytes 589832 | tf_op jit(solution)/shard_map/ppermute | solution.py:26
  77.7 8.1 %collective-permute-start.14 = (f16[128,768]{1,0:T(8,128)(2,1)S(1)}, f16[128,768]{1,0:T(8,128)(2,1)S(1)}, u32[]{:S(2)}, u32[]{:S(2)}) collective-permute-start(f16[128,768]{1,0:T(8,128)(2,1)S(1)} %fusion.64), channel_id=1, source_target_pairs={{0,4},{1,5},{2,6},{3,7},{4,0},{5,1},{6,2},{7,3},{8,12},{9,13},{10,... | collective-permute-start | bytes 589832 | tf_op jit(solution)/shard_map/ppermute | solution.py:70
  89.7 10.8 %collective-permute-start.17 = (bf16[128,1536]{1,0:T(8,128)(2,1)S(1)}, bf16[128,1536]{1,0:T(8,128)(2,1)S(1)}, u32[]{:S(2)}, u32[]{:S(2)}) collective-permute-start(bf16[128,1536]{1,0:T(8,128)(2,1)S(1)} %get-tuple-element.34), channel_id=1, source_target_pairs={{1,0},{2,1},{3,2},{0,3},{5,4},{6,5},{7,6},{4,7},{9,8},{10,9},{11,1... | collective-permute-start | bytes 1179656 | tf_op jit(solution)/shard_map/ppermute | solution.py:26
  91.0 10.9 %collective-permute-start.18 = (bf16[128,1536]{1,0:T(8,128)(2,1)S(1)}, bf16[128,1536]{1,0:T(8,128)(2,1)S(1)}, u32[]{:S(2)}, u32[]{:S(2)}) collective-permute-start(bf16[128,1536]{1,0:T(8,128)(2,1)S(1)} %get-tuple-element.34), channel_id=1, source_target_pairs={{3,0},{0,1},{1,2},{2,3},{7,4},{4,5},{5,6},{6,7},{11,8},{8,9},{9,10... | collective-permute-start | bytes 1179656 | tf_op jit(solution)/shard_map/ppermute | solution.py:26
  91.9 12.3 %collective-permute-start.23 = (bf16[128,1536]{1,0:T(8,128)(2,1)S(1)}, bf16[128,1536]{1,0:T(8,128)(2,1)S(1)}, u32[]{:S(2)}, u32[]{:S(2)}) collective-permute-start(bf16[128,1536]{1,0:T(8,128)(2,1)S(1)} %get-tuple-element.34), channel_id=1, source_target_pairs={{0,4},{1,5},{2,6},{3,7},{4,0},{5,1},{6,2},{7,3},{8,12},{9,13},{10,... | collective-permute-start | bytes 1179656 | tf_op jit(solution)/shard_map/ppermute | solution.py:89
  102.2 9.0 %collective-permute-start.20 = (bf16[64,1536]{1,0:T(8,128)(2,1)S(1)}, bf16[64,1536]{1,0:T(8,128)(2,1)S(1)}, u32[]{:S(2)}, u32[]{:S(2)}) collective-permute-start(bf16[64,1536]{1,0:T(8,128)(2,1)S(1)} %get-tuple-element.49), channel_id=1, source_target_pairs={{3,0},{0,1},{1,2},{2,3},{7,4},{4,5},{5,6},{6,7},{11,8},{8,9},{9,10... | collective-permute-start | bytes 589832 | tf_op jit(solution)/shard_map/ppermute | solution.py:26
  104.1 12.2 %collective-permute-start.25 = (bf16[128,1536]{1,0:T(8,128)(2,1)S(1)}, bf16[128,1536]{1,0:T(8,128)(2,1)S(1)}, u32[]{:S(2)}, u32[]{:S(2)}) collective-permute-start(bf16[128,1536]{1,0:T(8,128)(2,1)S(1)} %collective-permute-done.23), channel_id=1, source_target_pairs={{3,0},{0,1},{1,2},{2,3},{7,4},{4,5},{5,6},{6,7},{11,8},{8,9},{9,10... | collective-permute-start | bytes 1179656 | tf_op jit(solution)/shard_map/ppermute | solution.py:26
  104.6 11.7 %collective-permute-start.24 = (bf16[128,1536]{1,0:T(8,128)(2,1)S(1)}, bf16[128,1536]{1,0:T(8,128)(2,1)S(1)}, u32[]{:S(2)}, u32[]{:S(2)}) collective-permute-start(bf16[128,1536]{1,0:T(8,128)(2,1)S(1)} %collective-permute-done.23), channel_id=1, source_target_pairs={{1,0},{2,1},{3,2},{0,3},{5,4},{6,5},{7,6},{4,7},{9,8},{10,9},{11,1... | collective-permute-start | bytes 1179656 | tf_op jit(solution)/shard_map/ppermute | solution.py:26
  116.7 8.5 %collective-permute-start.27 = (bf16[64,1536]{1,0:T(8,128)(2,1)S(1)}, bf16[64,1536]{1,0:T(8,128)(2,1)S(1)}, u32[]{:S(2)}, u32[]{:S(2)}) collective-permute-start(bf16[64,1536]{1,0:T(8,128)(2,1)S(1)} %get-tuple-element.23), channel_id=1, source_target_pairs={{3,0},{0,1},{1,2},{2,3},{7,4},{4,5},{5,6},{6,7},{11,8},{8,9},{9,10... | collective-permute-start | bytes 589832 | tf_op jit(solution)/shard_map/ppermute | solution.py:26
  117.2 8.0 %collective-permute-start.29 = (f32[8,128]{1,0:T(8,128)S(1)}, f32[8,128]{1,0:T(8,128)S(1)}, u32[]{:S(2)}, u32[]{:S(2)}) collective-permute-start(f32[8,128]{1,0:T(8,128)S(1)} %fusion.88), channel_id=1, source_target_pairs={{0,128},{32,160},{64,192},{96,224},{128,0},{160,32},{192,64},{224,... | collective-permute-start | bytes 12296 | tf_op jit(solution)/shard_map/ppermute | solution.py:50
  119.5 11.1 %collective-permute-start.22 = (f16[8,16,1536]{2,1,0:T(8,128)(2,1)S(1)}, f16[8,16,1536]{2,1,0:T(8,128)(2,1)S(1)}, u32[]{:S(2)}, u32[]{:S(2)}) collective-permute-start(f16[8,16,1536]{2,1,0:T(8,128)(2,1)S(1)} %fusion.59), channel_id=1, source_target_pairs={{0,16},{16,0},{8,24},{24,8},{1,17},{17,1},{9,25},{25,9},{2,18},{18... | collective-permute-start | bytes 1179656 | tf_op jit(solution)/shard_map/ppermute | solution.py:109
  131.9 10.5 %collective-permute-start.30 = (f16[8,16,1536]{2,1,0:T(8,128)(2,1)S(1)}, f16[8,16,1536]{2,1,0:T(8,128)(2,1)S(1)}, u32[]{:S(2)}, u32[]{:S(2)}) collective-permute-start(f16[8,16,1536]{2,1,0:T(8,128)(2,1)S(1)} %fusion.60), channel_id=1, source_target_pairs={{0,16},{16,0},{8,24},{24,8},{1,17},{17,1},{9,25},{25,9},{2,18},{18... | collective-permute-start | bytes 1179656 | tf_op jit(solution)/shard_map/ppermute | solution.py:109
  134.7 16.4 %all-to-all-start.1 = ((f16[8,16,1536]{2,1,0:T(8,128)(2,1)}), f16[8,16,1536]{2,1,0:T(8,128)(2,1)S(1)}, u32[]{:S(2)}, u32[]{:S(2)}) async-start(f16[8,16,1536]{2,1,0:T(8,128)(2,1)} %fusion.58), calls=%async_computation.1 | async-start | bytes 786432 | tf_op jit(solution)/shard_map/all_to_all | solution.py:112
  151.2 17.2 %all-to-all-start.2 = ((f16[8,16,1536]{2,1,0:T(8,128)(2,1)}), f16[8,16,1536]{2,1,0:T(8,128)(2,1)S(1)}, u32[]{:S(2)}, u32[]{:S(2)}) async-start(f16[8,16,1536]{2,1,0:T(8,128)(2,1)} %fusion.57), calls=%async_computation.2 | async-start | bytes 786432 | tf_op jit(solution)/shard_map/all_to_all | solution.py:112
  (23 other events, 159.0 us)
